TPU v7x, 512 devices: a whole 4x4x16 slice. The times are simulated.
512 devices in a mesh: dp: 32 (over x, y, core), fsdp: 16 (over z).
Axes of the slice: x: 4, y: 4, z: 16, core: 2. Of those that a mesh axis runs over, the one named last changes fastest.
Arguments:
- patches: bfloat16 [32, 16, 3, 80, 1280], P('dp', 'fsdp'), may hold values from -16 to 16
- counts: int32 [32, 16, 3], P('dp', 'fsdp'), may hold values from 0 to 80, as said below
- norm_gain: float32 [1280], replicated, may hold values from 0.25 to 1.75
- norm_bias: float32 [1280], replicated, may hold values from -1.75 to 1.75
- input_weight: bfloat16 [1280, 1920], P('fsdp'), may hold values from -5 to 5
- latent_query: bfloat16 [64, 640], replicated, may hold values from -16 to 16
- cotangent: bfloat16 [32, 16, 3, 64, 640], P('dp', 'fsdp'), may hold values from -0.0390625 to 0.0390625
Outputs:
- latents: float32 [32, 16, 3, 64, 640], P('dp', 'fsdp')
- grad_value: float32 [1280, 640], P('fsdp')
Inputs may be any that keep to these rules, and one draw needn't show every extreme that they name: `counts`: A device holds its images in its first slots, each with 64 to 80 patches, and count 0 in the slots after them; it holds 1 to 3 images, and the devices of one fsdp index hold 2 times the dp axis's size images in all. Some device holds exactly 3 images and some image has exactly 80 patches.
All inputs are finite; a program needn't handle non-finite values.
Results may differ from a plain program's by a relative error of at most 0.012.
The roundings to bfloat16 on the way count: a program that leaves them out, or rounds other values in their place, can miss the bound.
Values may be sent and summed in bfloat16 or wider, within the bound.
No kernel may reach another device: no remote copies, remote signals or barrier semaphores. Data moves between devices by JAX's collectives and lax.ppermute only.
A program may use at most 64 MiB of HBM per device.

v0:
```python
import math

import jax
import jax.numpy as jnp
from jax import lax
from jax.sharding import PartitionSpec as P

HEADS = 8
IMAGES = 2


EPSILON = 1e-06
MASKED = -1e30


def layer_norm(rows, gain, bias):
    values = rows.astype(jnp.float32)
    centre = values - jnp.mean(values, axis=-1, keepdims=True)
    spread = jnp.mean(centre * centre, axis=-1, keepdims=True)
    return (centre * lax.rsqrt(spread + EPSILON) * gain + bias).astype(jnp.bfloat16)


def project(normed, input_weight):
    return jnp.dot(
        normed,
        lax.all_gather(input_weight, "fsdp", axis=0, tiled=True),
        preferred_element_type=jnp.float32,
    )


def forward_window(projected, segment, groups, kinds, latent_query):
    width = projected.shape[1] // 3
    head_size = width // HEADS
    span = projected.shape[0] // groups
    scale = 1.0 / math.sqrt(head_size)
    parts = projected.astype(jnp.bfloat16).reshape(groups, span, 3, HEADS, head_size)
    queries = parts[:, :, 0]
    keys = parts[:, :, 1]
    values = parts[:, :, 2]
    labels = segment.reshape(groups, span)
    valid = labels < kinds
    allowed = ((labels[:, :, None] == labels[:, None, :]) & valid[:, :, None])[:, None]
    scores = (
        jnp.einsum("gqhd,gchd->ghqc", queries, keys, preferred_element_type=jnp.float32) * scale
    )
    scores = jnp.where(allowed, scores, MASKED)
    raised = jnp.where(allowed, jnp.exp(scores - jnp.max(scores, axis=-1, keepdims=True)), 0.0)
    weights = (raised / jnp.maximum(jnp.sum(raised, axis=-1, keepdims=True), 1.0)).astype(
        jnp.bfloat16
    )
    mixed = jnp.einsum(
        "ghqc,gchd->gqhd", weights, values, preferred_element_type=jnp.float32
    ).astype(jnp.bfloat16)
    member = labels[:, None, :] == jnp.arange(kinds, dtype=jnp.int32)[None, :, None]
    latent_wide = latent_query.reshape(latent_query.shape[0], HEADS, head_size)
    latent_scores = (
        jnp.einsum("lhd,grhd->ghlr", latent_wide, mixed, preferred_element_type=jnp.float32) * scale
    )
    inside = member[:, None, None]
    masked = jnp.where(inside, latent_scores[:, :, :, None, :], MASKED)
    raised_latent = jnp.where(
        inside, jnp.exp(masked - jnp.max(masked, axis=-1, keepdims=True)), 0.0
    )
    shares = raised_latent / jnp.maximum(jnp.sum(raised_latent, axis=-1, keepdims=True), 1.0)
    shares_low = shares.astype(jnp.bfloat16)
    latents = jnp.einsum("ghlkr,grhd->gklhd", shares_low, mixed, preferred_element_type=jnp.float32)
    return (
        latents.reshape(groups * kinds, latent_query.shape[0], width),
        (weights, mixed, shares, shares_low),
    )


def backward_window(saved, grads, groups, kinds, latent_query):
    weights, mixed, shares, shares_low = saved
    width = latent_query.shape[1]
    head_size = width // HEADS
    count_latent = latent_query.shape[0]
    scale = 1.0 / math.sqrt(head_size)
    grad_blocks = grads.reshape(groups, kinds, count_latent, HEADS, head_size)
    share_grads = jnp.einsum(
        "gklhd,grhd->ghlkr", grad_blocks, mixed, preferred_element_type=jnp.float32
    )
    centre = jnp.sum(shares * share_grads, axis=-1, keepdims=True)
    score_grads = shares * (share_grads - centre) * scale
    from_values = jnp.einsum(
        "ghlkr,gklhd->grhd", shares_low, grad_blocks, preferred_element_type=jnp.float32
    )
    query_wide = latent_query.reshape(count_latent, HEADS, head_size).astype(jnp.float32)
    from_keys = jnp.einsum(
        "ghlkr,lhd->grhd", score_grads, query_wide, precision=lax.Precision.HIGHEST
    )
    mixed_grad = (from_values + from_keys).astype(jnp.bfloat16)
    value_grad = jnp.einsum(
        "ghqc,gqhd->gchd", weights, mixed_grad, preferred_element_type=jnp.float32
    ).astype(jnp.bfloat16)
    return value_grad.reshape(groups * value_grad.shape[1], width)


def on_device(patches, counts, norm_gain, norm_bias, input_weight, latent_query, cotangent):
    slots = patches.shape[2]
    capacity = patches.shape[3]
    width_in = patches.shape[4]
    images = patches.reshape(slots, capacity, width_in)
    sizes_own = counts.reshape(slots)
    grads_own = cotangent.reshape(slots, cotangent.shape[3], cotangent.shape[4])
    nothing = jnp.zeros((), jnp.bfloat16)
    zero_float = jnp.zeros((), jnp.float32)
    devices = lax.axis_size("dp")
    own_index = lax.axis_index("dp")
    device_ids = jnp.arange(devices, dtype=jnp.int32)
    all_counts = lax.all_gather(sizes_own, "dp", axis=0, tiled=True).reshape(devices, slots)
    owned = jnp.sum((all_counts > 0).astype(jnp.int32), axis=1)
    first = jnp.cumsum(owned) - owned
    first_own = jnp.sum(jnp.where(device_ids == own_index, first, 0))
    owned_own = jnp.sum(jnp.where(device_ids == own_index, owned, 0))
    out_slot = jnp.mod(device_ids - first_own, devices)
    sending = (out_slot < owned_own)[:, None, None]
    out_pick = jnp.minimum(out_slot, slots - 1)
    send_rows = jnp.where(sending, jnp.take(images, out_pick, axis=0), nothing)
    send_grads = jnp.where(sending, jnp.take(grads_own, out_pick, axis=0), nothing)
    came_rows, came_grads = (
        lax.all_to_all(send_rows, "dp", split_axis=0, concat_axis=0, tiled=True),
        lax.all_to_all(send_grads, "dp", split_axis=0, concat_axis=0, tiled=True),
    )
    in_slot = jnp.mod(own_index - first, devices)
    receiving = in_slot < owned
    in_pick = jnp.minimum(in_slot, slots - 1)
    in_count = jnp.where(
        receiving, jnp.take_along_axis(all_counts, in_pick[:, None], axis=1)[:, 0], 0
    )
    taken = receiving.astype(jnp.int32)
    rank = jnp.cumsum(taken) - taken
    start = jnp.cumsum(in_count) - in_count
    packed_rows = 128 * ((IMAGES * capacity + 127) // 128)
    row_ids = jnp.arange(packed_rows, dtype=jnp.int32)
    inside = (row_ids[:, None] >= start[None, :]) & (row_ids[:, None] < (start + in_count)[None, :])
    filled = jnp.any(inside, axis=1)
    source = jnp.sum(jnp.where(inside, device_ids[None, :], 0), axis=1)
    offset = row_ids - jnp.sum(jnp.where(inside, start[None, :], 0), axis=1)
    labels = jnp.where(filled, jnp.sum(jnp.where(inside, rank[None, :], 0), axis=1), IMAGES)
    flat_rows = came_rows.reshape(devices * capacity, width_in)
    pointer = jnp.where(filled, source * capacity + offset, 0)
    rows = jnp.where(filled[:, None], jnp.take(flat_rows, pointer, axis=0), nothing)
    normed = layer_norm(rows, norm_gain, norm_bias)
    projected = project(normed, input_weight)
    latents, saved = forward_window(projected, labels, 1, IMAGES, latent_query)
    back_pick = jnp.minimum(rank, IMAGES - 1)
    send_back = jnp.where(
        receiving[:, None, None], jnp.take(latents, back_pick, axis=0), zero_float
    )
    returned = lax.all_to_all(send_back, "dp", split_axis=0, concat_axis=0, tiled=True)
    slot_ids = jnp.arange(slots, dtype=jnp.int32)
    target = jnp.mod(first_own + slot_ids, devices)
    latents_own = jnp.where(
        (slot_ids < owned_own)[:, None, None], jnp.take(returned, target, axis=0), zero_float
    )
    image_ids = jnp.arange(IMAGES, dtype=jnp.int32)
    chosen = receiving[None, :] & (rank[None, :] == image_ids[:, None])
    owner_of = jnp.sum(jnp.where(chosen, device_ids[None, :], 0), axis=1)
    grads_here = jnp.take(came_grads, owner_of, axis=0)
    value_grad = backward_window(saved, grads_here, 1, IMAGES, latent_query)
    shard = lax.psum_scatter(
        jnp.einsum("rd,rv->dv", normed, value_grad, preferred_element_type=jnp.float32),
        "fsdp",
        scatter_dimension=0,
        tiled=True,
    )
    grad_value = lax.psum(shard, "dp")
    return (latents_own.reshape(cotangent.shape), grad_value)


def solution(mesh):
    placed = (
        P("dp", "fsdp", None, None, None),
        P("dp", "fsdp", None),
        P(),
        P(),
        P("fsdp", None),
        P(),
        P("dp", "fsdp", None, None, None),
    )
    return jax.shard_map(
        on_device,
        mesh=mesh,
        in_specs=placed,
        out_specs=(P("dp", "fsdp", None, None, None), P("fsdp", None)),
        check_vma=False,
    )
```

profile of v0, /device:TPU:1, one launch (start us, length us, event | category | flops | bytes accessed | tf_op | source)
XLA Modules:
  0.0 423.9 jit_solution(6074949543958144225)
XLA Ops:
  7.2 1.3 dynamic-slice
  9.2 0.8 bitcast_dynamic-update-slice_fusion
  9.9 14.4 %all-reduce = s32[96]{0:T(128)S(1)} all-reduce(s32[96]{0:T(128)S(1)} %bitcast_dynamic-update-slice_fusion), channel_id=2, replica_groups=mesh['dp'=32,'fsdp'=16] {'dp'}, use_global_device_ids=true, to_apply=%add | all-reduce | flops 96 | bytes 768
  25.6 0.7 fusion.31
  26.3 1.3 compare_and_fusion.2
  27.7 2.0 gather_fusion.4
  29.6 2.0 select_select_fusion.2
  31.6 10.9 %all-to-all-start.2 = ((bf16[32,64,640]{2,1,0:T(8,128)(2,1)}), bf16[32,64,640]{2,1,0:T(8,128)(2,1)S(1)}, u32[]{:S(2)}, u32[]{:S(2)}) async-start(bf16[32,64,640]{2,1,0:T(8,128)(2,1)} %select_select_fusion.2), calls=%async_computation.2 | async-start | bytes 5242880 | tf_op jit(solution)/shard_map/all_to_all | solution.py:123
  43.3 3.7 gather_fusion
  46.9 6.3 %select_select_fusion = bf16[32,80,1280]{2,1,0:T(8,128)(2,1)} fusion(bf16[32,80,1280]{2,1,0:T(8,128)(2,1)} %gather_fusion, pred[32]{0:T(512)(128)(4,1)S(1)} %get-tuple-element.25, pred[32]{0:T(512)(128)(4,1)S(1)} %get-tuple-element.26), kind=kLoop, calls=%fused_computation.8 | loop fusion | flops 6553600 | bytes 13107264 | tf_op jit(solution)/shard_map/jit(_where)/select_n | solution.py:119
  53.3 23.1 %all-to-all-done.2 = bf16[32,64,640]{2,1,0:T(8,128)(2,1)S(1)} async-done(((bf16[32,64,640]{2,1,0:T(8,128)(2,1)}), bf16[32,64,640]{2,1,0:T(8,128)(2,1)S(1)}, u32[]{:S(2)}, u32[]{:S(2)}) %all-to-all-start.2) | async-done | bytes 2621472 | tf_op jit(solution)/shard_map/all_to_all | solution.py:123
  76.4 5.5 %all-to-all-start = ((bf16[32,80,1280]{2,1,0:T(8,128)(2,1)}), bf16[32,80,1280]{2,1,0:T(8,128)(2,1)}, u32[]{:S(2)}, u32[]{:S(2)}) async-start(bf16[32,80,1280]{2,1,0:T(8,128)(2,1)} %select_select_fusion), calls=%async_computation | async-start | bytes 13107200 | tf_op jit(solution)/shard_map/all_to_all | solution.py:122
  87.9 0.7 copy_select_fusion
  88.6 74.7 %all-to-all-done = bf16[32,80,1280]{2,1,0:T(8,128)(2,1)} async-done(((bf16[32,80,1280]{2,1,0:T(8,128)(2,1)}), bf16[32,80,1280]{2,1,0:T(8,128)(2,1)}, u32[]{:S(2)}, u32[]{:S(2)}) %all-to-all-start) | async-done | bytes 6553632 | tf_op jit(solution)/shard_map/all_to_all | solution.py:122
  163.4 5.5 %gather_fusion.1 = bf16[256,1280]{1,0:T(8,128)(2,1)S(1)} fusion(bf16[2560,1280]{1,0:T(8,128)(2,1)} %bitcast.7, s32[1024]{0:T(1024)S(1)} %pad_clamp_fusion.3), kind=kCustom, calls=%fused_computation.1 | custom fusion | bytes 1311744 | tf_op jit(solution)/shard_map/jit(_take)/gather | solution.py:143
  169.7 5.0 %convolution_convert_fusion = bf16[256,1920]{1,0:T(8,128)(2,1)} fusion(bf16[1280,1920]{1,0:T(8,128)(2,1)} %all-gather.3.cloned.1.call-done, bf16[256,1280]{1,0:T(8,128)(2,1)S(1)} %get-tuple-element.14, f32[1280]{0:T(1024)S(1)} %copy-done.5, f32[1280]{0:T(1024)S(1)} %copy-done.6, f32[256]{0:T(256)S(1)} %add_rsqrt_fusion, f32[256]{0:T(256)S(1)} %broadcast_multiply_fusion), kind=kOutput, calls=%fused_computation.11 | convolution fusion | flops 1260748800 | bytes 6565888 | tf_op jit(solution)/shard_map/dot_general | solution.py:24
  174.7 1.6 copy.42
  176.3 2.4 fusion.66
  178.7 1.8 divide_convert_fusion
  180.4 1.3 convolution_convert_fusion.2
  184.0 1.3 convolution_bitcast_fusion
  185.3 2.1 convolution_convert_fusion.1
  187.5 2.7 fusion.60
  191.7 3.2 gather_fusion.2
  195.0 6.0 %select_select_fusion.1 = f32[32,64,640]{2,1,0:T(8,128)} fusion(f32[32,64,640]{2,1,0:T(8,128)} %gather_fusion.2, pred[32]{0:T(512)(128)(4,1)S(1)} %copy-done.13, pred[32]{0:T(512)(128)(4,1)S(1)} %copy-done.10), kind=kLoop, calls=%fused_computation.9 | loop fusion | flops 2621440 | bytes 10485824 | tf_op jit(solution)/shard_map/jit(_where)/select_n | solution.py:148
  200.9 13.9 %all-to-all-start.1 = ((f32[32,64,640]{2,1,0:T(8,128)}), f32[32,64,640]{2,1,0:T(8,128)}, u32[]{:S(2)}, u32[]{:S(2)}) async-start(f32[32,64,640]{2,1,0:T(8,128)} %select_select_fusion.1), calls=%async_computation.1 | async-start | bytes 10485760 | tf_op jit(solution)/shard_map/all_to_all | solution.py:151
  215.5 1.3 compare_and_fusion.5
  216.8 62.6 %all-to-all-done.1 = f32[32,64,640]{2,1,0:T(8,128)} async-done(((f32[32,64,640]{2,1,0:T(8,128)}), f32[32,64,640]{2,1,0:T(8,128)}, u32[]{:S(2)}, u32[]{:S(2)}) %all-to-all-start.1) | async-done | bytes 5242912 | tf_op jit(solution)/shard_map/all_to_all | solution.py:151
  279.4 3.1 gather_fusion.3
  282.5 0.9 fusion.19
  283.4 132.3 %all-reduce.3.cloned.1.call-done = f32[80,640]{1,0:T(8,128)} async-done(((f32[80,640]{1,0:T(8,128)}), f32[80,640]{1,0:T(8,128)}) %all-reduce.3.cloned.1.call-update) | async-done | bytes 204816 | tf_op jit(solution)/shard_map/psum | solution.py:168
  415.7 1.6 copy.62
  (93 shorter events, 13.1 us)
Async XLA Ops:
  7.2 36.1 %copy-start = (bf16[1,1,3,80,1280]{4,3,2,1,0:T(8,128)(2,1)S(1)}, bf16[1,1,3,80,1280]{4,3,2,1,0:T(8,128)(2,1)}, u32[]{:S(2)}) copy-start(bf16[1,1,3,80,1280]{4,3,2,1,0:T(8,128)(2,1)} %param.7) | copy-start | bytes 1843204
  31.6 44.8 %all-to-all-start.2 = ((bf16[32,64,640]{2,1,0:T(8,128)(2,1)}), bf16[32,64,640]{2,1,0:T(8,128)(2,1)S(1)}, u32[]{:S(2)}, u32[]{:S(2)}) async-start(bf16[32,64,640]{2,1,0:T(8,128)(2,1)} %select_select_fusion.2), calls=%async_computation.2 | async-start | bytes 5242880 | tf_op jit(solution)/shard_map/all_to_all | solution.py:123
  42.5 127.1 %all-gather.3.cloned.1.call-start = ((), (), s32[]{:S(2)}) async-start(), calls=%async_computation.4 | async-start | bytes 5222400 | tf_op jit(solution)/shard_map/all_gather | solution.py:26
  53.3 30.7 %copy-start.3 = (bf16[64,640]{1,0:T(8,128)(2,1)S(1)}, bf16[64,640]{1,0:T(8,128)(2,1)}, u32[]{:S(2)}) copy-start(bf16[64,640]{1,0:T(8,128)(2,1)} %param.12) | copy-start | bytes 245764
  76.4 86.9 %all-to-all-start = ((bf16[32,80,1280]{2,1,0:T(8,128)(2,1)}), bf16[32,80,1280]{2,1,0:T(8,128)(2,1)}, u32[]{:S(2)}, u32[]{:S(2)}) async-start(bf16[32,80,1280]{2,1,0:T(8,128)(2,1)} %select_select_fusion), calls=%async_computation | async-start | bytes 13107200 | tf_op jit(solution)/shard_map/all_to_all | solution.py:122
  81.9 200.6 %reduce-scatter.2.cloned.1.call-start = ((), (), s32[]{:S(2)}) async-start(), calls=%async_computation.5 | async-start | bytes 3481600 | tf_op jit(solution)/shard_map/reduce_scatter | solution.py:162
  84.8 2.8 copy-start.9
  84.9 2.7 copy-start.7
  88.6 93.1 %copy-start.2 = (bf16[2,64,8,80]{3,1,0,2:T(8,128)(2,1)}, bf16[2,64,8,80]{3,1,0,2:T(8,128)(2,1)S(1)}, u32[]{:S(2)}) copy-start(bf16[2,64,8,80]{3,1,0,2:T(8,128)(2,1)S(1)} %copy_select_fusion) | copy-start | bytes 491524
  163.4 5.5 %copy-start.8 = (pred[256]{0:T(512)(128)(4,1)S(1)}, pred[256]{0:T(512)(128)(4,1)}, u32[]{:S(2)}) copy-start(pred[256]{0:T(512)(128)(4,1)} %copy-done.7) | copy-start | bytes 772
  163.4 5.5 %copy-start.11 = (pred[256]{0:T(512)(128)(4,1)S(1)}, pred[256]{0:T(512)(128)(4,1)}, u32[]{:S(2)}) copy-start(pred[256]{0:T(512)(128)(4,1)} %get-tuple-element.22) | copy-start | bytes 772
  163.4 6.3 %copy-start.5 = (f32[1280]{0:T(1024)S(1)}, f32[1280]{0:T(1024)}, u32[]{:S(2)}) copy-start(f32[1280]{0:T(1024)} %param.10) | copy-start | bytes 15364
  163.4 6.3 %copy-start.6 = (f32[1280]{0:T(1024)S(1)}, f32[1280]{0:T(1024)}, u32[]{:S(2)}) copy-start(f32[1280]{0:T(1024)} %param.9) | copy-start | bytes 15364
  169.6 6.7 %copy-start.4 = (pred[256,256]{0,1:T(8,128)(4,1)S(1)}, pred[256,256]{0,1:T(8,128)(4,1)}, u32[]{:S(2)}) copy-start(pred[256,256]{0,1:T(8,128)(4,1)} %compare_and_fusion) | copy-start | bytes 196612
  176.3 2.4 copy-start.1
  190.1 0.6 copy-start.12
  191.7 3.3 copy-start.10
  191.7 3.2 copy-start.13
  200.9 78.5 %all-to-all-start.1 = ((f32[32,64,640]{2,1,0:T(8,128)}), f32[32,64,640]{2,1,0:T(8,128)}, u32[]{:S(2)}, u32[]{:S(2)}) async-start(f32[32,64,640]{2,1,0:T(8,128)} %select_select_fusion.1), calls=%async_computation.1 | async-start | bytes 10485760 | tf_op jit(solution)/shard_map/all_to_all | solution.py:151
  214.8 200.9 %all-reduce.3.cloned.1.call-start = ((), (), s32[]{:S(2)}) async-start(), calls=%async_computation.6 | async-start | bytes 409600 | tf_op jit(solution)/shard_map/psum | solution.py:168
Sparse Core Ops, SparseCore 0:
  45.4 74.1 all-gather.2
  190.3 75.5 reduce-scatter.1
  282.7 133.0 all-reduce.2
where the time goes:
time: 425 us; the launch traced here: 424 us
  waiting for transfers between devices  294 us (69%)
  starting transfers between devices  30.3 us (7%)
  other arithmetic  29 us (7%)
  local copies, waits for them, and re-layouts  26 us (6%)
  matrix products  15.7 us (4%)
  between operations  14.8 us (3%)
  blocking collectives  14.4 us (3%)
    psum x1, waiting for transfers between devices, on_device(): grad_value = lax.psum(shard, 'dp')  132 us
    all_to_all x1, waiting for transfers between devices, on_device(): lax.all_to_all(send_rows, 'dp', split_axis=0, concat_axis=0, tiled=True)  74.7 us
    all_to_all x1, waiting for transfers between devices, on_device(): lax.all_to_all(send_back, 'dp', split_axis=0, concat_axis=0, tiled=True)  62.6 us
    all_to_all x1, waiting for transfers between devices, on_device(): lax.all_to_all(send_grads, 'dp', split_axis=0, concat_axis=0, tiled=True)  23.1 us
    unnamed x1, blocking collectives  14.4 us
    all_to_all x1, starting transfers between devices, on_device(): lax.all_to_all(send_back, 'dp', split_axis=0, concat_axis=0, tiled=True)  13.9 us
    all_to_all x1, starting transfers between devices, on_device(): lax.all_to_all(send_grads, 'dp', split_axis=0, concat_axis=0, tiled=True)  10.9 us
  transfers between devices with their start and end apart: 6, of which 4 were waited for; matrix products, arithmetic and copies ran while one was open for 9% of the time, Pallas kernels for 0%

commit v1 on v0

v1 whole, which is shorter than its diff:
```python
import math

import jax
import jax.numpy as jnp
from jax import lax
from jax.sharding import Mesh
from jax.sharding import PartitionSpec as P

HEADS = 2
EPSILON = 1e-06
MASKED = -1e30
DP = ("xp", "xi", "y", "c")
PLANE = ("xp", "y")
SWAP = [(0, 1), (1, 0)]


def layer_norm(rows, gain, bias):
    values = rows.astype(jnp.float32)
    centre = values - jnp.mean(values, axis=-1, keepdims=True)
    spread = jnp.mean(centre * centre, axis=-1, keepdims=True)
    return (centre * lax.rsqrt(spread + EPSILON) * gain + bias).astype(jnp.bfloat16)


def forward_window(projected, sizes, latent_query):
    groups = sizes.shape[0]
    width = projected.shape[1] // 3
    head_size = width // HEADS
    span = projected.shape[0] // groups
    scale = 1.0 / math.sqrt(head_size)
    parts = projected.astype(jnp.bfloat16).reshape(groups, span, 3, HEADS, head_size)
    queries, keys, values = parts[:, :, 0], parts[:, :, 1], parts[:, :, 2]
    valid = jnp.arange(span, dtype=jnp.int32)[None, :] < sizes[:, None]
    allowed = (valid[:, :, None] & valid[:, None, :])[:, None]
    scores = (
        jnp.einsum("gqhd,gchd->ghqc", queries, keys, preferred_element_type=jnp.float32) * scale
    )
    scores = jnp.where(allowed, scores, MASKED)
    raised = jnp.where(allowed, jnp.exp(scores - jnp.max(scores, axis=-1, keepdims=True)), 0.0)
    weights = (raised / jnp.maximum(jnp.sum(raised, axis=-1, keepdims=True), 1.0)).astype(
        jnp.bfloat16
    )
    mixed = jnp.einsum(
        "ghqc,gchd->gqhd", weights, values, preferred_element_type=jnp.float32
    ).astype(jnp.bfloat16)
    latent_wide = latent_query.reshape(latent_query.shape[0], HEADS, head_size)
    latent_scores = (
        jnp.einsum("lhd,grhd->ghlr", latent_wide, mixed, preferred_element_type=jnp.float32) * scale
    )
    inside = valid[:, None, None, :]
    masked = jnp.where(inside, latent_scores, MASKED)
    raised_latent = jnp.where(
        inside, jnp.exp(masked - jnp.max(masked, axis=-1, keepdims=True)), 0.0
    )
    shares = raised_latent / jnp.maximum(jnp.sum(raised_latent, axis=-1, keepdims=True), 1.0)
    shares_low = shares.astype(jnp.bfloat16)
    latents = jnp.einsum("ghlr,grhd->glhd", shares_low, mixed, preferred_element_type=jnp.float32)
    return (
        latents.reshape(groups, latent_query.shape[0], width),
        (weights, mixed, shares, shares_low),
    )


def backward_window(saved, grads, latent_query):
    weights, mixed, shares, shares_low = saved
    width = latent_query.shape[1]
    head_size = width // HEADS
    groups = grads.shape[0]
    count_latent = latent_query.shape[0]
    scale = 1.0 / math.sqrt(head_size)
    grad_blocks = grads.reshape(groups, count_latent, HEADS, head_size)
    share_grads = jnp.einsum(
        "glhd,grhd->ghlr", grad_blocks, mixed, preferred_element_type=jnp.float32
    )
    centre = jnp.sum(shares * share_grads, axis=-1, keepdims=True)
    score_grads = shares * (share_grads - centre) * scale
    from_values = jnp.einsum(
        "ghlr,glhd->grhd", shares_low, grad_blocks, preferred_element_type=jnp.float32
    )
    query_wide = latent_query.reshape(count_latent, HEADS, head_size).astype(jnp.float32)
    from_keys = jnp.einsum(
        "ghlr,lhd->grhd", score_grads, query_wide, precision=lax.Precision.HIGHEST
    )
    mixed_grad = (from_values + from_keys).astype(jnp.bfloat16)
    value_grad = jnp.einsum(
        "ghqc,gqhd->gchd", weights, mixed_grad, preferred_element_type=jnp.float32
    ).astype(jnp.bfloat16)
    return value_grad.reshape(groups * value_grad.shape[1], width)


def copies(piece, count):
    return jnp.broadcast_to(piece[None], (count,) + piece.shape)


def exchange(array, axes):
    return lax.all_to_all(array, axes, 0, 0, tiled=True)


def own_half(array, index, axis):
    low, high = jnp.split(array, 2, axis=axis)
    return jnp.where(index == 0, low, high), jnp.where(index == 0, high, low)


def on_device(patches, counts, norm_gain, norm_bias, input_weight, latent_query, cotangent):
    slots, capacity, width_in = patches.shape[2:]
    latent_count, width = cotangent.shape[3:]
    depth = input_weight.shape[0]
    ring = lax.axis_size("z")
    sharers = lax.axis_size(PLANE)
    xp, xi, y, c = (lax.axis_index(a) for a in DP)
    pair = 2 * xi + c
    quarter = width // 4

    images = patches.reshape(slots * capacity, width_in)
    grads = cotangent.reshape(slots * latent_count, width)
    sizes = jnp.zeros((16, width), jnp.bfloat16) + jnp.pad(
        counts.reshape(slots).astype(jnp.bfloat16), (0, 16 - slots)
    )[:, None]
    ride = jnp.concatenate([grads, sizes], axis=0)

    keep, give = own_half(ride, xi, 1)
    images_x = lax.ppermute(images, "xi", SWAP)
    ride_x = lax.ppermute(give, "xi", SWAP)

    piece = quarter // 4
    rows = lax.dynamic_slice_in_dim(input_weight, xp * (depth // 2), depth // 2, 0)
    target = jnp.arange(3 * piece, dtype=jnp.int32)
    source = width * (target // piece) + quarter * pair + piece * y + target % piece
    pick = (jnp.arange(3 * width, dtype=jnp.int32)[:, None] == source[None, :]).astype(jnp.bfloat16)
    own = jnp.dot(rows, pick, preferred_element_type=jnp.float32).astype(jnp.bfloat16)
    along = exchange(copies(own, ring), "z")

    images_two = jnp.stack([images, images_x])
    mine, theirs = own_half(jnp.stack([keep, ride_x]), c, 2)
    images_c = lax.ppermute(images_two, "c", SWAP)
    ride_c = lax.ppermute(theirs, "c", SWAP)

    whole = exchange(copies(along, sharers), PLANE)
    weight = (
        whole.reshape(2, 4, ring, depth // 2, 3, piece)
        .transpose(2, 0, 3, 4, 1, 5)
        .reshape(ring * depth, 3 * quarter)
    )

    rides = jnp.concatenate([mine, ride_c])
    sizes_all = rides[:, slots * latent_count :][:, :slots, 0].astype(jnp.int32).reshape(4 * slots)
    grads_all = rides[:, : slots * latent_count].reshape(4 * slots, latent_count, quarter)
    normed = layer_norm(jnp.concatenate([images_two, images_c]), norm_gain, norm_bias)
    normed = normed.reshape(4 * slots * capacity, width_in)
    projected = jnp.dot(normed, weight, preferred_element_type=jnp.float32)
    query = lax.dynamic_slice_in_dim(latent_query, pair * quarter, quarter, 1)
    latents, saved = forward_window(projected, sizes_all, query)
    value_grad = backward_window(saved, grads_all, query)
    partial = jnp.einsum("rd,rv->dv", normed, value_grad, preferred_element_type=jnp.float32)

    part = depth // sharers
    partial = partial.astype(jnp.bfloat16).reshape(ring, sharers, part, quarter)
    came = exchange(partial.transpose(1, 0, 2, 3), PLANE)
    summed = jnp.sum(came.astype(jnp.float32), axis=0)
    summed = jnp.sum(exchange(summed, "z"), axis=0)
    done = exchange(copies(summed, 4 * sharers), DP)
    grad_value = (
        done.reshape(2, 2, 4, 2, part, quarter).transpose(0, 2, 4, 1, 3, 5).reshape(depth, width)
    )

    latents = latents.reshape(2, 2, slots, latent_count, quarter)
    other_c = lax.ppermute(latents[1], "c", SWAP)
    by_c = jnp.where(c == 0, jnp.stack([latents[0], other_c]), jnp.stack([other_c, latents[0]]))
    other_x = lax.ppermute(by_c[:, 1], "xi", SWAP)
    own_x = by_c[:, 0]
    by_x = jnp.where(xi == 0, jnp.stack([own_x, other_x]), jnp.stack([other_x, own_x]))
    latents_own = by_x.transpose(2, 3, 0, 1, 4).reshape(cotangent.shape)
    return latents_own, grad_value


def solution(mesh):
    fine = Mesh(mesh.devices.reshape(2, 2, 4, 2, 16), DP + ("z",))
    placed = (
        P(DP, "z", None, None, None),
        P(DP, "z", None),
        P(),
        P(),
        P("z", None),
        P(),
        P(DP, "z", None, None, None),
    )
    return jax.shard_map(
        on_device,
        mesh=fine,
        in_specs=placed,
        out_specs=(P(DP, "z", None, None, None), P("z", None)),
        check_vma=False,
    )
```

time: 425 us -> 202 us (0.48)
  waiting for transfers between devices: 294 us -> 41 us
  starting transfers between devices: 30.3 us -> 65.5 us
  local copies, waits for them, and re-layouts: 26 us -> 59.4 us
  blocking collectives: 14.4 us -> 0 us
  between operations: 14.8 us -> 1.11 us
  matrix products: 15.7 us -> 9.91 us
  other arithmetic: 29 us -> 23.4 us
    psum x1 -> x0, waiting for transfers between devices: 132 us -> none  [on_device(): grad_value = lax.psum(shard, 'dp')]
    all_to_all x3 -> x5, waiting for transfers between devices: 160 us -> 30.3 us  [exchange(): return lax.all_to_all(array, axes, 0, 0, tiled=True)]
    reshape x2 -> x7, local copies, waits for them, and re-layouts: 0.29 us -> 24.3 us  [the longest x1 12.4 us: on_device(): weight = whole.reshape(2, 4, ring, depth // 2, 3, piece).transpose(2, 0,...]
    ppermute x0 -> x6, starting transfers between devices: none -> 20.6 us  [the longest x1 7.32 us: on_device(): ride_c = lax.ppermute(theirs, 'c', SWAP)]
    gather x10 -> x0, local copies, waits for them, and re-layouts: 19.1 us -> none  [the longest x1 5.51 us: on_device(): jnp.take(flat_rows, pointer, axis=0)]
    transpose x1 -> x4, local copies, waits for them, and re-layouts: 0.32 us -> 18.2 us  [the longest x1 16.1 us: on_device(): weight = whole.reshape(2, 4, ring, depth // 2, 3, piece).transpose(2, 0,...]
    all_to_all x3 -> x5, starting transfers between devices: 30.2 us -> 44.9 us  [exchange(): return lax.all_to_all(array, axes, 0, 0, tiled=True)]
    select_n x11 -> x2, other arithmetic: 18 us -> 3.32 us  [the longest x1 2.1 us: own_half(): return (jnp.where(index == 0, low, high), jnp.where(index == 0, high, low))]
  transfers between devices with their start and end apart: 6 -> 11, of which waited for: 4 -> 6; matrix products, arithmetic and copies ran while one was open for 9% -> 30% of each run, Pallas kernels for 0% -> 0%
where the time goes in v1:
time: 202 us; the launch traced here: 200 us
  starting transfers between devices  65.5 us (32%)
  local copies, waits for them, and re-layouts  59.4 us (29%)
  waiting for transfers between devices  41 us (20%)
  other arithmetic  23.4 us (12%)
  matrix products  9.91 us (5%)
    all_to_all x5, starting transfers between devices, exchange(): return lax.all_to_all(array, axes, 0, 0, tiled=True)  44.9 us
    all_to_all x5, waiting for transfers between devices, exchange(): return lax.all_to_all(array, axes, 0, 0, tiled=True)  30.3 us
    transpose x1, local copies, waits for them, and re-layouts, on_device(): weight = whole.reshape(2, 4, ring, depth // 2, 3, piece).transpose(2, 0,...  16.1 us
    reshape x1, local copies, waits for them, and re-layouts, on_device(): weight = whole.reshape(2, 4, ring, depth // 2, 3, piece).transpose(2, 0,...  12.4 us
    ppermute x1, waiting for transfers between devices, on_device(): ride_x = lax.ppermute(give, 'xi', SWAP)  10.2 us
    ppermute x1, starting transfers between devices, on_device(): ride_c = lax.ppermute(theirs, 'c', SWAP)  7.32 us
    reshape x1, local copies, waits for them, and re-layouts, on_device(): whole.reshape(2, 4, ring, depth // 2, 3, piece).transpose(2, 0, 3, 4, 1, 5)  5.27 us
    sub x1, other arithmetic, backward_window(): score_grads = shares * (share_grads - centre) * scale  4.92 us
  transfers between devices with their start and end apart: 11, of which 6 were waited for; matrix products, arithmetic and copies ran while one was open for 30% of the time, Pallas kernels for 0%

profile of v1, /device:TPU:1, one launch (start us, length us, event | category | flops | bytes accessed | tf_op | source)
XLA Modules:
  0.0 200.3 jit_solution(8155651364634202619)
XLA Ops:
  0.7 4.1 %collective-permute-start = (bf16[240,1280]{1,0:T(8,128)(2,1)}, bf16[240,1280]{1,0:T(8,128)(2,1)S(1)}, u32[]{:S(2)}, u32[]{:S(2)}) collective-permute-start(bf16[240,1280]{1,0:T(8,128)(2,1)} %bitcast.80), channel_id=1, source_target_pairs={{0,128},{128,0},{1,129},{129,1},{2,130},{130,2},{3,131},{131,3},{4... | collective-permute-start | bytes 1843208 | tf_op jit(solution)/shard_map/ppermute | solution.py:121
  5.8 14.9 %all-to-all-start = ((bf16[16,40,120]{2,1,0:T(8,128)(2,1)}), bf16[16,40,120]{2,1,0:T(8,128)(2,1)S(1)}, u32[]{:S(2)}, u32[]{:S(2)}) async-start(bf16[16,40,120]{2,1,0:T(8,128)(2,1)} %broadcast_in_dim.44), calls=%async_computation | async-start | bytes 327680 | tf_op jit(solution)/shard_map/all_to_all | solution.py:95
  21.5 2.2 %pad_maximum_fusion.1 = bf16[2,240,1280]{2,1,0:T(8,128)(2,1)} fusion(bf16[1,240,1280]{2,1,0:T(8,128)(2,1)S(1)} %bitcast.85, bf16[1,240,1280]{2,1,0:T(8,128)(2,1)} %bitcast.81), kind=kLoop, calls=%fused_computation.36 | loop fusion | flops 614400 | bytes 2457600 | tf_op jit(solution)/shard_map/stack | solution.py:132
  23.7 3.1 %collective-permute-start.1 = (bf16[2,240,1280]{2,1,0:T(8,128)(2,1)}, bf16[2,240,1280]{2,1,0:T(8,128)(2,1)S(1)}, u32[]{:S(2)}, u32[]{:S(2)}) collective-permute-start(bf16[2,240,1280]{2,1,0:T(8,128)(2,1)} %pad_maximum_fusion.1), channel_id=1, source_target_pairs={{0,16},{16,0},{1,17},{17,1},{2,18},{18,2},{3,19},{19,3},{4,20},{20... | collective-permute-start | bytes 3686408 | tf_op jit(solution)/shard_map/ppermute | solution.py:134
  27.7 5.2 %all-to-all-done = bf16[16,40,120]{2,1,0:T(8,128)(2,1)S(1)} async-done(((bf16[16,40,120]{2,1,0:T(8,128)(2,1)}), bf16[16,40,120]{2,1,0:T(8,128)(2,1)S(1)}, u32[]{:S(2)}, u32[]{:S(2)}) %all-to-all-start) | async-done | bytes 153632 | tf_op jit(solution)/shard_map/all_to_all | solution.py:95
  34.1 6.4 %all-to-all-start.1 = ((bf16[8,16,40,120]{3,2,1,0:T(8,128)(2,1)}), bf16[8,16,40,120]{3,2,1,0:T(8,128)(2,1)S(1)}, u32[]{:S(2)}, u32[]{:S(2)}) async-start(bf16[8,16,40,120]{3,2,1,0:T(8,128)(2,1)} %broadcast_in_dim.74), calls=%async_computation.1 | async-start | bytes 2621440 | tf_op jit(solution)/shard_map/all_to_all | solution.py:95
  40.5 1.8 select_bitcast_fusion
  42.3 1.9 collective-permute-start.2
  44.2 10.2 %collective-permute-done.2 = bf16[208,320]{1,0:T(8,128)(2,1)} collective-permute-done((bf16[208,320]{1,0:T(8,128)(2,1)}, bf16[208,320]{1,0:T(8,128)(2,1)}, u32[]{:S(2)}, u32[]{:S(2)}) %collective-permute-start.2) | collective-permute-done | bytes 133152 | tf_op jit(solution)/shard_map/ppermute | solution.py:122
  54.5 2.1 %broadcast_select_fusion.1 = (bf16[2,208,160]{2,1,0:T(8,128)(2,1)}, bf16[2,208,160]{2,1,0:T(8,128)(2,1)}) fusion(pred[]{:T(512)S(6)} %eq.13, bf16[1,208,320]{2,1,0:T(8,128)(2,1)} %bitcast.9, bf16[1,208,320]{2,1,0:T(8,128)(2,1)} %get-tuple-element.11), kind=kLoop, calls=%fused_computation.71 | loop fusion | flops 931840 | bytes 532481 | tf_op jit(solution)/shard_map/jit(_where)/select_n | solution.py:100
  56.6 7.3 %collective-permute-start.3 = (bf16[2,208,160]{2,1,0:T(8,128)(2,1)}, bf16[2,208,160]{2,1,0:T(8,128)(2,1)}, u32[]{:S(2)}, u32[]{:S(2)}) collective-permute-start(bf16[2,208,160]{2,1,0:T(8,128)(2,1)} %get-tuple-element.10), channel_id=1, source_target_pairs={{0,16},{16,0},{1,17},{17,1},{2,18},{18,2},{3,19},{19,3},{4,20},{20... | collective-permute-start | bytes 399368 | tf_op jit(solution)/shard_map/ppermute | solution.py:135
  66.2 1.8 pad_maximum_fusion.2
  68.1 2.0 reshape_reshape.4
  71.0 5.3 %reshape.325 = bf16[2,4,16,40,3,40]{5,4,3,2,1,0:T(4,128)(2,1)} reshape(bf16[8,16,40,120]{3,2,1,0:T(8,128)(2,1)S(1)} %all-to-all-done.1) | data formatting | bytes 2457600 | tf_op jit(solution)/shard_map/reshape | solution.py:139
  76.3 16.1 %copy.120 = bf16[16,2,40,3,4,40]{2,1,0,5,4,3:T(2,128)(2,1)} copy(bf16[16,2,40,3,4,40]{5,3,2,0,4,1:T(4,128)(2,1)} %bitcast.77) | data formatting | bytes 2457600 | tf_op jit(solution)/shard_map/transpose | solution.py:140
  92.4 12.4 %reshape.326 = bf16[1280,480]{0,1:T(8,128)(2,1)} reshape(bf16[16,2,40,3,4,40]{2,1,0,5,4,3:T(2,128)(2,1)} %copy.120) | data formatting | bytes 2457600 | tf_op jit(solution)/shard_map/reshape | solution.py:141
  105.2 1.8 fusion.5
  108.2 1.4 copy-done.1
  109.6 1.5 convolution_convert_fusion.1
  111.1 2.3 %reshape.327 = bf16[12,80,3,2,80]{4,3,2,1,0:T(2,128)(2,1)S(1)} reshape(bf16[960,480]{1,0:T(8,128)(2,1)S(1)} %convolution_convert_fusion.1) | data formatting | bytes 1843200 | tf_op jit(solution)/shard_map/reshape | solution.py:30
  118.2 1.8 convolution_bitcast_fusion.1
  121.3 4.9 %fusion.19 = f32[12,2,64,80]{3,2,0,1:T(8,128)S(1)} fusion(f32[12,2,64,80]{3,2,0,1:T(8,128)S(1)} %fusion.30, f32[12,2,64,80]{3,2,0,1:T(8,128)S(1)} %copy-done.12, f32[12,2,64]{2,0,1:T(8,128)S(1)} %broadcast_maximum_fusion), kind=kOutput, calls=%fused_computation.29 | output fusion | flops 738895 | bytes 1480704 | tf_op jit(solution)/shard_map/sub | solution.py:75
  130.9 2.0 fusion.60
  134.2 2.3 %collective-permute-start.4 = (f32[2,3,64,160]{3,2,1,0:T(8,128)}, f32[2,3,64,160]{3,2,1,0:T(8,128)}, u32[]{:S(2)}, u32[]{:S(2)}) collective-permute-start(f32[2,3,64,160]{3,2,1,0:T(8,128)} %squeeze.19), channel_id=1, source_target_pairs={{0,16},{16,0},{1,17},{17,1},{2,18},{18,2},{3,19},{19,3},{4,20},{20... | collective-permute-start | bytes 737288 | tf_op jit(solution)/shard_map/ppermute | solution.py:166
  138.8 8.0 %all-to-all-start.2 = ((bf16[8,16,10,160]{3,1,2,0:T(8,128)(2,1)}), bf16[8,16,10,160]{3,1,2,0:T(8,128)(2,1)S(1)}, u32[]{:S(2)}, u32[]{:S(2)}) async-start(bf16[8,16,10,160]{3,1,2,0:T(8,128)(2,1)} %copy.144), calls=%async_computation.2 | async-start | bytes 1310720 | tf_op jit(solution)/shard_map/all_to_all | solution.py:95
  148.6 9.1 %all-to-all-done.2 = bf16[8,16,10,160]{3,1,2,0:T(8,128)(2,1)S(1)} async-done(((bf16[8,16,10,160]{3,1,2,0:T(8,128)(2,1)}), bf16[8,16,10,160]{3,1,2,0:T(8,128)(2,1)S(1)}, u32[]{:S(2)}, u32[]{:S(2)}) %all-to-all-start.2) | async-done | bytes 409632 | tf_op jit(solution)/shard_map/all_to_all | solution.py:95
  158.8 7.2 %all-to-all-start.3 = ((f32[16,1,1600]{2,1,0:T(1,128)}), f32[16,1,1600]{2,1,0:T(1,128)S(1)}, u32[]{:S(2)}, u32[]{:S(2)}) async-start(f32[16,1,1600]{2,1,0:T(1,128)} %reshape.340), calls=%async_computation.3 | async-start | bytes 212992 | tf_op jit(solution)/shard_map/all_to_all | solution.py:95
  166.1 1.9 collective-permute-start.5
  168.0 9.9 %all-to-all-done.3 = f32[16,1,1600]{2,1,0:T(1,128)S(1)} async-done(((f32[16,1,1600]{2,1,0:T(1,128)}), f32[16,1,1600]{2,1,0:T(1,128)S(1)}, u32[]{:S(2)}, u32[]{:S(2)}) %all-to-all-start.3) | async-done | bytes 102432 | tf_op jit(solution)/shard_map/all_to_all | solution.py:95
  180.6 8.4 %all-to-all-start.4 = ((f32[32,1,1600]{2,1,0:T(1,128)}), f32[32,1,1600]{2,1,0:T(1,128)S(1)}, u32[]{:S(2)}, u32[]{:S(2)}) async-start(f32[32,1,1600]{2,1,0:T(1,128)} %reshape.342), calls=%async_computation.4 | async-start | bytes 425984 | tf_op jit(solution)/shard_map/all_to_all | solution.py:95
  189.7 1.7 reshape.330
  191.4 6.1 %all-to-all-done.4 = f32[32,1,1600]{2,1,0:T(1,128)S(1)} async-done(((f32[32,1,1600]{2,1,0:T(1,128)}), f32[32,1,1600]{2,1,0:T(1,128)S(1)}, u32[]{:S(2)}, u32[]{:S(2)}) %all-to-all-start.4) | async-done | bytes 204832 | tf_op jit(solution)/shard_map/all_to_all | solution.py:95
  (87 shorter events, 32.0 us)
Async XLA Ops:
  0.6 4.2 %copy-start = (bf16[80,1920]{1,0:T(8,128)(2,1)S(1)}, bf16[80,1920]{1,0:T(8,128)(2,1)}, u32[]{:S(2)}) copy-start(bf16[80,1920]{1,0:T(8,128)(2,1)} %param.11) | copy-start | bytes 921604
  0.6 26.2 %copy-start.8 = (bf16[1,1,3,64,640]{4,3,2,1,0:T(8,128)(2,1)S(1)}, bf16[1,1,3,64,640]{4,3,2,1,0:T(8,128)(2,1)}, u32[]{:S(2)}) copy-start(bf16[1,1,3,64,640]{4,3,2,1,0:T(8,128)(2,1)} %param.13) | copy-start | bytes 737284
  0.7 20.8 %collective-permute-start = (bf16[240,1280]{1,0:T(8,128)(2,1)}, bf16[240,1280]{1,0:T(8,128)(2,1)S(1)}, u32[]{:S(2)}, u32[]{:S(2)}) collective-permute-start(bf16[240,1280]{1,0:T(8,128)(2,1)} %bitcast.80), channel_id=1, source_target_pairs={{0,128},{128,0},{1,129},{129,1},{2,130},{130,2},{3,131},{131,3},{4... | collective-permute-start | bytes 1843208 | tf_op jit(solution)/shard_map/ppermute | solution.py:121
  5.8 27.1 %all-to-all-start = ((bf16[16,40,120]{2,1,0:T(8,128)(2,1)}), bf16[16,40,120]{2,1,0:T(8,128)(2,1)S(1)}, u32[]{:S(2)}, u32[]{:S(2)}) async-start(bf16[16,40,120]{2,1,0:T(8,128)(2,1)} %broadcast_in_dim.44), calls=%async_computation | async-start | bytes 327680 | tf_op jit(solution)/shard_map/all_to_all | solution.py:95
  23.7 81.1 %collective-permute-start.1 = (bf16[2,240,1280]{2,1,0:T(8,128)(2,1)}, bf16[2,240,1280]{2,1,0:T(8,128)(2,1)S(1)}, u32[]{:S(2)}, u32[]{:S(2)}) collective-permute-start(bf16[2,240,1280]{2,1,0:T(8,128)(2,1)} %pad_maximum_fusion.1), channel_id=1, source_target_pairs={{0,16},{16,0},{1,17},{17,1},{2,18},{18,2},{3,19},{19,3},{4,20},{20... | collective-permute-start | bytes 3686408 | tf_op jit(solution)/shard_map/ppermute | solution.py:134
  34.1 36.8 %all-to-all-start.1 = ((bf16[8,16,40,120]{3,2,1,0:T(8,128)(2,1)}), bf16[8,16,40,120]{3,2,1,0:T(8,128)(2,1)S(1)}, u32[]{:S(2)}, u32[]{:S(2)}) async-start(bf16[8,16,40,120]{3,2,1,0:T(8,128)(2,1)} %broadcast_in_dim.74), calls=%async_computation.1 | async-start | bytes 2621440 | tf_op jit(solution)/shard_map/all_to_all | solution.py:95
  42.3 12.1 %collective-permute-start.2 = (bf16[208,320]{1,0:T(8,128)(2,1)}, bf16[208,320]{1,0:T(8,128)(2,1)}, u32[]{:S(2)}, u32[]{:S(2)}) collective-permute-start(bf16[208,320]{1,0:T(8,128)(2,1)} %get-tuple-element.12), channel_id=1, source_target_pairs={{0,128},{128,0},{1,129},{129,1},{2,130},{130,2},{3,131},{131,3},{4... | collective-permute-start | bytes 399368 | tf_op jit(solution)/shard_map/ppermute | solution.py:122
  56.6 8.7 %collective-permute-start.3 = (bf16[2,208,160]{2,1,0:T(8,128)(2,1)}, bf16[2,208,160]{2,1,0:T(8,128)(2,1)}, u32[]{:S(2)}, u32[]{:S(2)}) collective-permute-start(bf16[2,208,160]{2,1,0:T(8,128)(2,1)} %get-tuple-element.10), channel_id=1, source_target_pairs={{0,16},{16,0},{1,17},{17,1},{2,18},{18,2},{3,19},{19,3},{4,20},{20... | collective-permute-start | bytes 399368 | tf_op jit(solution)/shard_map/ppermute | solution.py:135
  92.4 12.4 %copy-start.3 = (bf16[1,1,3,80,1280]{4,3,2,1,0:T(8,128)(2,1)S(1)}, bf16[1,1,3,80,1280]{4,3,2,1,0:T(8,128)(2,1)}, u32[]{:S(2)}) copy-start(bf16[1,1,3,80,1280]{4,3,2,1,0:T(8,128)(2,1)} %param.7) | copy-start | bytes 1843204
  104.8 2.2 %copy-start.10 = (f32[1280]{0:T(1024)S(1)}, f32[1280]{0:T(1024)}, u32[]{:S(2)}) copy-start(f32[1280]{0:T(1024)} %param.10) | copy-start | bytes 15364
  104.8 2.2 %copy-start.11 = (f32[1280]{0:T(1024)S(1)}, f32[1280]{0:T(1024)}, u32[]{:S(2)}) copy-start(f32[1280]{0:T(1024)} %param.9) | copy-start | bytes 15364
  107.0 2.6 %copy-start.7 = (bf16[1280,480]{0,1:T(8,128)(2,1)S(1)}, bf16[1280,480]{0,1:T(8,128)(2,1)}, u32[]{:S(2)}) copy-start(bf16[1280,480]{0,1:T(8,128)(2,1)} %reshape.326) | copy-start | bytes 3686404
  108.2 1.4 copy-start.1
  111.1 3.3 %copy-start.9 = (pred[12,80,80]{1,2,0:T(8,128)(4,1)S(1)}, pred[12,80,80]{1,2,0:T(8,128)(4,1)}, u32[]{:S(2)}) copy-start(pred[12,80,80]{1,2,0:T(8,128)(4,1)} %broadcast_and_fusion) | copy-start | bytes 230404
  115.6 1.0 copy-start.4
  118.2 1.8 copy-start.12
  128.2 8.2 %copy-start.2 = (bf16[4,240,1280]{2,1,0:T(8,128)(2,1)S(1)}, bf16[4,240,1280]{2,1,0:T(8,128)(2,1)}, u32[]{:S(2)}) copy-start(bf16[4,240,1280]{2,1,0:T(8,128)(2,1)} %copy-done.1) | copy-start | bytes 7372804
  130.9 5.6 %copy-start.6 = (bf16[960,160]{0,1:T(8,128)(2,1)S(1)}, bf16[960,160]{0,1:T(8,128)(2,1)}, u32[]{:S(2)}) copy-start(bf16[960,160]{0,1:T(8,128)(2,1)} %reshape.331) | copy-start | bytes 921604
  134.2 13.2 %collective-permute-start.4 = (f32[2,3,64,160]{3,2,1,0:T(8,128)}, f32[2,3,64,160]{3,2,1,0:T(8,128)}, u32[]{:S(2)}, u32[]{:S(2)}) collective-permute-start(f32[2,3,64,160]{3,2,1,0:T(8,128)} %squeeze.19), channel_id=1, source_target_pairs={{0,16},{16,0},{1,17},{17,1},{2,18},{18,2},{3,19},{19,3},{4,20},{20... | collective-permute-start | bytes 737288 | tf_op jit(solution)/shard_map/ppermute | solution.py:166
  137.3 9.4 %copy-start.5 = (f32[6,64,2,80]{3,1,2,0:T(8,128)S(1)}, f32[6,64,2,80]{3,1,2,0:T(8,128)}, u32[]{:S(2)}) copy-start(f32[6,64,2,80]{3,1,2,0:T(8,128)} %get-tuple-element.7) | copy-start | bytes 737284
  138.8 18.9 %all-to-all-start.2 = ((bf16[8,16,10,160]{3,1,2,0:T(8,128)(2,1)}), bf16[8,16,10,160]{3,1,2,0:T(8,128)(2,1)S(1)}, u32[]{:S(2)}, u32[]{:S(2)}) async-start(bf16[8,16,10,160]{3,1,2,0:T(8,128)(2,1)} %copy.144), calls=%async_computation.2 | async-start | bytes 1310720 | tf_op jit(solution)/shard_map/all_to_all | solution.py:95
  158.8 19.1 %all-to-all-start.3 = ((f32[16,1,1600]{2,1,0:T(1,128)}), f32[16,1,1600]{2,1,0:T(1,128)S(1)}, u32[]{:S(2)}, u32[]{:S(2)}) async-start(f32[16,1,1600]{2,1,0:T(1,128)} %reshape.340), calls=%async_computation.3 | async-start | bytes 212992 | tf_op jit(solution)/shard_map/all_to_all | solution.py:95
  166.1 23.0 %collective-permute-start.5 = (f32[2,3,64,160]{3,2,1,0:T(8,128)S(1)}, f32[2,3,64,160]{3,2,1,0:T(8,128)S(1)}, u32[]{:S(2)}, u32[]{:S(2)}) collective-permute-start(f32[2,3,64,160]{3,2,1,0:T(8,128)S(1)} %get-tuple-element.6), channel_id=1, source_target_pairs={{0,128},{128,0},{1,129},{129,1},{2,130},{130,2},{3,131},{131,3},{4... | collective-permute-start | bytes 737288 | tf_op jit(solution)/shard_map/ppermute | solution.py:168
  180.6 16.9 %all-to-all-start.4 = ((f32[32,1,1600]{2,1,0:T(1,128)}), f32[32,1,1600]{2,1,0:T(1,128)S(1)}, u32[]{:S(2)}, u32[]{:S(2)}) async-start(f32[32,1,1600]{2,1,0:T(1,128)} %reshape.342), calls=%async_computation.4 | async-start | bytes 425984 | tf_op jit(solution)/shard_map/all_to_all | solution.py:95

commit v2 on v1

v2 whole, which is shorter than its diff:
```python
import functools
import math

import jax
import jax.numpy as jnp
from jax import lax
from jax.experimental import pallas as pl
from jax.experimental.pallas import tpu as pltpu
from jax.sharding import Mesh
from jax.sharding import PartitionSpec as P

HEADS = 2
EPSILON = 1e-06
MASKED = -1e30
DP = ("xp", "xi", "y", "c")
PLANE = ("xp", "y")
SWAP = [(0, 1), (1, 0)]
LANES = 128
CHUNK = 16
LIMIT = 56 * 1024 * 1024


def norm_kernel(first_ref, second_ref, gain_ref, bias_ref, out_ref):
    gain, bias = gain_ref[...], bias_ref[...]
    for index, source in enumerate((first_ref, second_ref)):
        for start in range(0, source.shape[0], CHUNK):
            values = source[start : start + CHUNK, :].astype(jnp.float32)
            centre = values - jnp.mean(values, axis=-1, keepdims=True)
            spread = jnp.mean(centre * centre, axis=-1, keepdims=True)
            normed = centre * lax.rsqrt(spread + EPSILON) * gain + bias
            out_ref[index, start : start + CHUNK, :] = normed.astype(jnp.bfloat16)


def across(left, right):
    return lax.dot_general(left, right, (((1,), (1,)), ((), ())), preferred_element_type=jnp.float32)


def along(left, right):
    return lax.dot_general(left, right, (((0,), (0,)), ((), ())), preferred_element_type=jnp.float32)


def plain(left, right):
    return jnp.dot(left, right, preferred_element_type=jnp.float32)


def column_order(piece, quarter):
    out = lax.broadcasted_iota(jnp.int32, (4 * LANES, 6 * LANES), 1)
    row = lax.broadcasted_iota(jnp.int32, (4 * LANES, 6 * LANES), 0)
    kind = (out >= 2 * LANES).astype(jnp.int32) + (out >= 4 * LANES).astype(jnp.int32)
    lane = out - 2 * LANES * kind
    block = sum((lane >= piece * n).astype(jnp.int32) for n in (1, 2, 3))
    source = LANES * block + piece * kind + lane - piece * block
    return jnp.where((row == source) & (lane < quarter), 1.0, 0.0).astype(jnp.bfloat16)


def main_kernel(
    slots, latent_count, ring, sharers,
    here_ref, there_ref, whole_ref, ride_ref, ride_c_ref, query_ref,
    lat_ref, lat_c_ref, packed_ref,
    weight_ref, grad_ref, total_ref, tail_ref,
):
    rows, width_in = here_ref.shape[1:]
    capacity = rows // slots
    quarter = query_ref.shape[1]
    head_size = quarter // HEADS
    piece = quarter // 4
    scale = 1.0 / math.sqrt(head_size)
    for block in range(4):
        halves = [whole_ref[4 * half + block].astype(jnp.float32) for half in range(2)]
        stacked = jnp.stack(halves, axis=1).reshape(width_in, LANES)
        weight_ref[:, LANES * block : LANES * (block + 1)] = stacked.astype(jnp.bfloat16)
    order = column_order(piece, quarter)
    first_head = lax.broadcasted_iota(jnp.int32, (1, quarter), 1) < head_size
    nothing = jnp.zeros((), jnp.bfloat16)

    def head_of(array, head):
        return jnp.where(first_head, array, nothing) if head == 0 else jnp.where(first_head, nothing, array)

    def both_heads(array):
        return jnp.concatenate([head_of(array, 0), head_of(array, 1)], axis=0)

    query_wide = both_heads(query_ref[...])
    grad_ref[...] = jnp.zeros_like(grad_ref)
    image_of = [
        sum((lax.broadcasted_iota(jnp.int32, shape, axis) >= capacity * n).astype(jnp.int32) for n in range(1, slots))
        for shape, axis in (((rows, 1), 0), ((1, rows), 1))
    ]
    place = [
        (lax.broadcasted_iota(jnp.int32, shape, axis) - capacity * image).astype(jnp.float32)
        for (shape, axis), image in zip((((rows, 1), 0), ((1, rows), 1)), image_of)
    ]
    offset = lax.broadcasted_iota(jnp.int32, (capacity, 1), 0).astype(jnp.float32)
    for block in range(4):
        normed_ref, carried_ref, out_ref = (
            (here_ref, ride_ref, lat_ref) if block < 2 else (there_ref, ride_c_ref, lat_c_ref)
        )
        side = block % 2
        sizes = carried_ref[side, slots * latent_count :, :].astype(jnp.float32)
        size = [sizes[n : n + 1, 0:1] for n in range(slots)]
        live = []
        for image, position in zip(image_of, place):
            limit = size[slots - 1] + jnp.zeros_like(position)
            for n in reversed(range(slots - 1)):
                limit = jnp.where(image == n, size[n], limit)
            live.append(position < limit)
        row_label = jnp.where(live[0], image_of[0], -1)
        column_label = jnp.where(live[1], image_of[1], -2)
        allowed = row_label == column_label
        projected = plain(normed_ref[side], weight_ref[...]).astype(jnp.bfloat16)
        sorted_columns = plain(projected, order).astype(jnp.bfloat16)
        queries, keys, values = (
            sorted_columns[:, 2 * LANES * n : 2 * LANES * n + quarter] for n in range(3)
        )
        weights = []
        for head in range(HEADS):
            scores = jnp.where(allowed, across(head_of(queries, head), keys) * scale, MASKED)
            highest = jnp.max(scores, axis=-1, keepdims=True)
            raised = jnp.where(allowed, jnp.exp(scores - highest), 0.0)
            total = jnp.maximum(jnp.sum(raised, axis=-1, keepdims=True), 1.0)
            weights.append((raised / total).astype(jnp.bfloat16))
        mixed = sum(plain(weights[head], head_of(values, head)) for head in range(HEADS))
        mixed = mixed.astype(jnp.bfloat16)
        latent_scores = across(mixed, query_wide) * scale
        mixed_grads = []
        for n in range(slots):
            span = slice(capacity * n, capacity * (n + 1))
            inside = offset < size[n]
            masked = jnp.where(inside, latent_scores[span], MASKED)
            raised = jnp.where(inside, jnp.exp(masked - jnp.max(masked, axis=0, keepdims=True)), 0.0)
            shares = raised / jnp.maximum(jnp.sum(raised, axis=0, keepdims=True), 1.0)
            shares_low = shares.astype(jnp.bfloat16)
            mixed_here = mixed[span]
            latents = along(shares_low, mixed_here)
            out_ref[side, latent_count * n : latent_count * (n + 1), :] = jnp.where(
                first_head, latents[:latent_count], latents[latent_count:]
            )
            cotangent = both_heads(carried_ref[side, latent_count * n : latent_count * (n + 1), :])
            share_grads = across(mixed_here, cotangent)
            middle = jnp.sum(shares * share_grads, axis=0, keepdims=True)
            score_grads = shares * (share_grads - middle) * scale
            high = score_grads.astype(jnp.bfloat16)
            low = (score_grads - high.astype(jnp.float32)).astype(jnp.bfloat16)
            mixed_grad = plain(shares_low, cotangent) + (plain(high, query_wide) + plain(low, query_wide))
            mixed_grads.append(mixed_grad.astype(jnp.bfloat16))
        mixed_grad = jnp.concatenate(mixed_grads, axis=0)
        value_grad = sum(along(weights[head], head_of(mixed_grad, head)) for head in range(HEADS))
        grad_ref[rows * block : rows * (block + 1), :quarter] = value_grad.astype(jnp.bfloat16)
    total = sum(
        along(ref[side], grad_ref[rows * (2 * n + side) : rows * (2 * n + side + 1), :])
        for n, ref in enumerate((here_ref, there_ref))
        for side in range(2)
    )
    total_ref[...] = total[:, :LANES]
    tail_ref[...] = total[:, LANES:]
    depth = width_in // ring
    part = depth // sharers
    per_tile = 2 * LANES // (2 * (quarter - LANES))
    for sharer in range(sharers):
        rest = []
        for row in range(part):
            picked = pl.ds(sharer * part + row, ring, stride=depth)
            packed_ref[sharer, :, LANES * row : LANES * (row + 1)] = total_ref[picked, :].astype(jnp.bfloat16)
            tail = tail_ref[picked, :]
            shift = (row % per_tile) * (quarter - LANES)
            tail = tail if shift == 0 else pltpu.roll(tail, shift, 1)
            if shift == 0:
                rest.append(tail)
            else:
                rest[-1] = rest[-1] + tail
        for n, tile in enumerate(rest):
            lanes = slice(LANES * (part + n), LANES * (part + n + 1))
            packed_ref[sharer, :, lanes] = tile.astype(jnp.bfloat16)


def call(kernel, outs, scratch, flops, *operands):
    memory = pl.BlockSpec(memory_space=pltpu.VMEM)
    size = sum(math.prod(a.shape) * a.dtype.itemsize for a in (*operands, *outs))
    return pl.pallas_call(
        kernel,
        out_shape=outs,
        in_specs=[memory] * len(operands),
        out_specs=[memory] * len(outs),
        scratch_shapes=scratch,
        compiler_params=pltpu.CompilerParams(vmem_limit_bytes=LIMIT),
        cost_estimate=pl.CostEstimate(flops=flops, bytes_accessed=size, transcendentals=0),
    )(*operands)


def layer_norm(first, second, gain, bias):
    out = jax.ShapeDtypeStruct((2,) + first.shape, jnp.bfloat16)
    return call(norm_kernel, [out], [], 20 * 2 * first.size, first, second, gain[None], bias[None])[0]


def attend(here, there, whole, ride, ride_c, query, slots, latent_count, ring):
    rows, width_in = here.shape[1:]
    quarter = query.shape[1]
    sharers = whole.shape[0]
    part = width_in // ring // sharers
    packed = LANES * (part + -(-part * (quarter - LANES) // LANES))
    latents = jax.ShapeDtypeStruct((2, slots * latent_count, quarter), jnp.float32)
    return call(
        functools.partial(main_kernel, slots, latent_count, ring, sharers),
        [latents, latents, jax.ShapeDtypeStruct((sharers, ring, packed), jnp.bfloat16)],
        [
            pltpu.VMEM((width_in, 4 * LANES), jnp.bfloat16),
            pltpu.VMEM((4 * rows, 2 * LANES), jnp.bfloat16),
            pltpu.VMEM((width_in, LANES), jnp.float32),
            pltpu.VMEM((width_in, LANES), jnp.float32),
        ],
        2 * 4 * rows * width_in * 5 * quarter,
        here, there, whole, ride, ride_c, query,
    )


def copies(piece, count):
    return jnp.broadcast_to(piece[None], (count,) + piece.shape)


def exchange(array, axes):
    return lax.all_to_all(array, axes, 0, 0, tiled=True)


def own_half(array, index, axis):
    low, high = jnp.split(array, 2, axis=axis)
    return jnp.where(index == 0, low, high), jnp.where(index == 0, high, low)


def in_order(own, other, index):
    return jnp.where(
        index == 0, jnp.concatenate([own, other], axis=-1), jnp.concatenate([other, own], axis=-1)
    )


def unpack(packed, part, quarter):
    lead = packed.shape[:-1]
    head = packed[..., : LANES * part].reshape(lead + (part, LANES))
    rest = packed[..., LANES * part : LANES * part + part * (quarter - LANES)]
    return jnp.concatenate([head, rest.reshape(lead + (part, quarter - LANES))], axis=-1)


def on_device(patches, counts, norm_gain, norm_bias, input_weight, latent_query, cotangent):
    slots, capacity, width_in = patches.shape[2:]
    latent_count, width = cotangent.shape[3:]
    depth = input_weight.shape[0]
    ring = lax.axis_size("z")
    sharers = lax.axis_size(PLANE)
    xp, xi, y, c = (lax.axis_index(a) for a in DP)
    pair = 2 * xi + c
    quarter = width // 4

    images = patches.reshape(slots * capacity, width_in)
    grads = cotangent.reshape(slots * latent_count, width)
    sizes = jnp.zeros((16, width), jnp.bfloat16) + jnp.pad(
        counts.reshape(slots).astype(jnp.bfloat16), (0, 16 - slots)
    )[:, None]
    ride = jnp.concatenate([grads, sizes], axis=0)

    keep, give = own_half(ride, xi, 1)
    images_x = lax.ppermute(images, "xi", SWAP)
    ride_x = lax.ppermute(give, "xi", SWAP)

    piece = quarter // 4
    rows = lax.dynamic_slice_in_dim(input_weight, xp * (depth // 2), depth // 2, 0)
    target = jnp.arange(LANES, dtype=jnp.int32)
    source = width * (target // piece) + quarter * pair + piece * y + target % piece
    source = jnp.where(target < 3 * piece, source, -1)
    pick = (jnp.arange(3 * width, dtype=jnp.int32)[:, None] == source[None, :]).astype(jnp.bfloat16)
    own = jnp.dot(rows, pick, preferred_element_type=jnp.float32).astype(jnp.bfloat16)
    gathered = exchange(copies(own, ring), "z")

    normed = layer_norm(images, images_x, norm_gain, norm_bias)
    mine, theirs = own_half(jnp.stack([keep, ride_x]), c, 2)
    normed_c = lax.ppermute(normed, "c", SWAP)
    ride_c = lax.ppermute(theirs, "c", SWAP)

    whole = exchange(copies(gathered, sharers), PLANE)
    query = lax.dynamic_slice_in_dim(latent_query, pair * quarter, quarter, 1)
    latents, latents_c, packed = attend(
        normed, normed_c, whole, mine, ride_c, query, slots, latent_count, ring
    )

    part = depth // sharers
    summed = jnp.sum(exchange(packed, PLANE).astype(jnp.float32), axis=0)
    summed = jnp.sum(exchange(summed, "z"), axis=0)
    done = unpack(exchange(copies(summed, 4 * sharers), DP), part, quarter)
    grad_value = (
        done.reshape(2, 2, 4, 2, part, quarter).transpose(0, 2, 4, 1, 3, 5).reshape(depth, width)
    )

    latents_c = lax.ppermute(latents_c, "c", SWAP)
    by_c = in_order(latents, latents_c, c)
    by_x = in_order(by_c[0], lax.ppermute(by_c[1], "xi", SWAP), xi)
    return by_x.reshape(cotangent.shape), grad_value


def solution(mesh):
    fine = Mesh(mesh.devices.reshape(2, 2, 4, 2, 16), DP + ("z",))
    placed = (
        P(DP, "z", None, None, None),
        P(DP, "z", None),
        P(),
        P(),
        P("z", None),
        P(),
        P(DP, "z", None, None, None),
    )
    return jax.shard_map(
        on_device,
        mesh=fine,
        in_specs=placed,
        out_specs=(P(DP, "z", None, None, None), P("z", None)),
        check_vma=False,
    )
```

time: 202 us -> 138 us (0.68)
  local copies, waits for them, and re-layouts: 59.4 us -> 11.3 us
  other arithmetic: 23.4 us -> 3.89 us
  Pallas kernels: 0 us -> 15.6 us
  matrix products: 9.91 us -> 0.32 us
  waiting for transfers between devices: 41 us -> 38.1 us
    reshape x7 -> x0, local copies, waits for them, and re-layouts: 23.3 us -> none  [the longest x1 12.4 us: on_device(): weight = whole.reshape(2, 4, ring, depth // 2, 3, piece).transpose(2, 0,...]
    transpose x3 -> x0, local copies, waits for them, and re-layouts: 17.9 us -> none  [the longest x1 16.1 us: on_device(): weight = whole.reshape(2, 4, ring, depth // 2, 3, piece).transpose(2, 0,...]
    pallas_call x0 -> x2, Pallas kernels: none -> 15.6 us  [call(): pl.pallas_call(kernel, out_shape=outs, in_specs=[memory] * len(operands),...]
    dot_general x9 -> x0, matrix products: 8.23 us -> none  [the longest x1 1.78 us: backward_window(): jnp.einsum('ghlr,glhd->grhd', shares_low, grad_blocks, preferred_element_...]
    sub x2 -> x0, other arithmetic: 5.26 us -> none  [the longest x1 4.92 us: backward_window(): score_grads = shares * (share_grads - centre) * scale]
    all_to_all x5, waiting for transfers between devices: 30.3 us -> 26.4 us  [exchange(): return lax.all_to_all(array, axes, 0, 0, tiled=True)]
    slice x5 -> x3, local copies, waits for them, and re-layouts: 3.84 us -> 0.06 us  [the longest x1 0.04 us: on_device(): by_x = in_order(by_c[0], lax.ppermute(by_c[1], 'xi', SWAP), xi)]
    broadcast_in_dim x0 -> x2, local copies, waits for them, and re-layouts: none -> 2.58 us  [the longest x1 1.3 us: layer_norm(): gain[None]]
  transfers between devices with their start and end apart: 11 -> 11, of which waited for: 6 -> 5; matrix products, arithmetic and copies ran while one was open for 30% -> 8% of each run, Pallas kernels for 0% -> 2%
where the time goes in v2:
time: 138 us; the launch traced here: 137 us
  starting transfers between devices  67 us (49%)
  waiting for transfers between devices  38.1 us (28%)
  Pallas kernels  15.6 us (11%)
  local copies, waits for them, and re-layouts  11.3 us (8%)
  other arithmetic  3.89 us (3%)
    all_to_all x5, starting transfers between devices, exchange(): return lax.all_to_all(array, axes, 0, 0, tiled=True)  46.5 us
    all_to_all x5, waiting for transfers between devices, exchange(): return lax.all_to_all(array, axes, 0, 0, tiled=True)  26.4 us
    pallas_call x2, Pallas kernels, call(): pl.pallas_call(kernel, out_shape=outs, in_specs=[memory] * len(operands),...  15.6 us
    ppermute x1, waiting for transfers between devices, on_device(): ride_x = lax.ppermute(give, 'xi', SWAP)  11.7 us
    ppermute x1, starting transfers between devices, on_device(): ride_c = lax.ppermute(theirs, 'c', SWAP)  7.21 us
    ppermute x1, starting transfers between devices, on_device(): images_x = lax.ppermute(images, 'xi', SWAP)  4.08 us
    ppermute x1, starting transfers between devices, on_device(): normed_c = lax.ppermute(normed, 'c', SWAP)  3.13 us
  transfers between devices with their start and end apart: 11, of which 5 were waited for; matrix products, arithmetic and copies ran while one was open for 8% of the time, Pallas kernels for 2%

profile of v2, /device:TPU:1, one launch (start us, length us, event | category | flops | bytes accessed | tf_op | source)
XLA Modules:
  0.0 137.2 jit_solution(15037548278168901974)
XLA Ops:
  0.6 4.1 %collective-permute-start = (bf16[240,1280]{1,0:T(8,128)(2,1)}, bf16[240,1280]{1,0:T(8,128)(2,1)S(1)}, u32[]{:S(2)}, u32[]{:S(2)}) collective-permute-start(bf16[240,1280]{1,0:T(8,128)(2,1)} %bitcast.19), channel_id=1, source_target_pairs={{0,128},{128,0},{1,129},{129,1},{2,130},{130,2},{3,131},{131,3},{4... | collective-permute-start | bytes 1843208 | tf_op jit(solution)/shard_map/ppermute | solution.py:259
  5.1 0.7 broadcast_in_dim.14
  5.8 14.9 %all-to-all-start = ((bf16[16,40,128]{2,1,0:T(8,128)(2,1)}), bf16[16,40,128]{2,1,0:T(8,128)(2,1)S(1)}, u32[]{:S(2)}, u32[]{:S(2)}) async-start(bf16[16,40,128]{2,1,0:T(8,128)(2,1)} %broadcast_in_dim.14), calls=%async_computation | async-start | bytes 327680 | tf_op jit(solution)/shard_map/all_to_all | solution.py:220
  20.7 1.3 broadcast_in_dim.12.gain_ref
  22.0 1.3 broadcast_in_dim.13.bias_ref
  23.3 0.8 copy-done.2
  24.1 3.2 %shard_map.86.here_ref = bf16[2,240,1280]{2,1,0:T(8,128)(2,1)} custom-call(bf16[240,1280]{1,0:T(8,128)(2,1)} %bitcast.20, bf16[240,1280]{1,0:T(8,128)(2,1)} %copy-done.2, f32[1,1280]{1,0:T(1,128)} %broadcast_in_dim.12.gain_ref, f32[1,1280]{1,0:T(1,128)} %broadcast_in_dim.13.bias_ref), custom_call_target="tpu_custom_call" | custom-call | flops 12288000 | bytes 2467840 | tf_op jit(solution)/shard_map/pallas_call | solution.py:178
  27.3 3.1 %collective-permute-start.1 = (bf16[2,240,1280]{2,1,0:T(8,128)(2,1)}, bf16[2,240,1280]{2,1,0:T(8,128)(2,1)S(1)}, u32[]{:S(2)}, u32[]{:S(2)}) collective-permute-start(bf16[2,240,1280]{2,1,0:T(8,128)(2,1)} %shard_map.86.here_ref), channel_id=1, source_target_pairs={{0,16},{16,0},{1,17},{17,1},{2,18},{18,2},{3,19},{19,3},{4,20},{20... | collective-permute-start | bytes 3686408 | tf_op jit(solution)/shard_map/ppermute | solution.py:273
  30.5 2.4 %all-to-all-done = bf16[16,40,128]{2,1,0:T(8,128)(2,1)S(1)} async-done(((bf16[16,40,128]{2,1,0:T(8,128)(2,1)}), bf16[16,40,128]{2,1,0:T(8,128)(2,1)S(1)}, u32[]{:S(2)}, u32[]{:S(2)}) %all-to-all-start) | async-done | bytes 163872 | tf_op jit(solution)/shard_map/all_to_all | solution.py:220
  32.9 1.3 broadcast_in_dim.15
  34.1 6.5 %all-to-all-start.1 = ((bf16[8,16,40,128]{3,2,1,0:T(8,128)(2,1)}), bf16[8,16,40,128]{3,2,1,0:T(8,128)(2,1)S(1)}, u32[]{:S(2)}, u32[]{:S(2)}) async-start(bf16[8,16,40,128]{3,2,1,0:T(8,128)(2,1)} %broadcast_in_dim.15), calls=%async_computation.1 | async-start | bytes 2621440 | tf_op jit(solution)/shard_map/all_to_all | solution.py:220
  41.0 1.9 %collective-permute-start.2 = (bf16[208,320]{1,0:T(8,128)(2,1)S(1)}, bf16[208,320]{1,0:T(8,128)(2,1)S(1)}, u32[]{:S(2)}, u32[]{:S(2)}) collective-permute-start(bf16[208,320]{1,0:T(8,128)(2,1)S(1)} %get-tuple-element.13), channel_id=1, source_target_pairs={{0,128},{128,0},{1,129},{129,1},{2,130},{130,2},{3,131},{131,3},{4... | collective-permute-start | bytes 399368 | tf_op jit(solution)/shard_map/ppermute | solution.py:260
  42.9 11.7 %collective-permute-done.2 = bf16[208,320]{1,0:T(8,128)(2,1)S(1)} collective-permute-done((bf16[208,320]{1,0:T(8,128)(2,1)S(1)}, bf16[208,320]{1,0:T(8,128)(2,1)S(1)}, u32[]{:S(2)}, u32[]{:S(2)}) %collective-permute-start.2) | collective-permute-done | bytes 133152 | tf_op jit(solution)/shard_map/ppermute | solution.py:260
  54.6 0.9 broadcast_select_fusion
  55.5 7.2 %collective-permute-start.3 = (bf16[2,208,160]{2,1,0:T(8,128)(2,1)S(1)}, bf16[2,208,160]{2,1,0:T(8,128)(2,1)}, u32[]{:S(2)}, u32[]{:S(2)}) collective-permute-start(bf16[2,208,160]{2,1,0:T(8,128)(2,1)S(1)} %get-tuple-element.10), channel_id=1, source_target_pairs={{0,16},{16,0},{1,17},{17,1},{2,18},{18,2},{3,19},{19,3},{4,20},{20... | collective-permute-start | bytes 399368 | tf_op jit(solution)/shard_map/ppermute | solution.py:274
  62.7 1.5 %constant_dynamic-slice_fusion.query_ref = bf16[64,160]{1,0:T(8,128)(2,1)} fusion(bf16[64,640]{1,0:T(8,128)(2,1)} %param.12, s32[]{:T(128)S(6)} %select_n.93), kind=kLoop, calls=%fused_computation.31 | loop fusion | bytes 40964 | tf_op jit(solution)/shard_map/dynamic_slice | solution.py:277
  64.3 1.1 copy-done.1
  65.3 0.3 copy-done.4
  65.7 12.4 %shard_map.87 = (f32[2,192,160]{2,1,0:T(8,128)}, f32[2,192,160]{2,1,0:T(8,128)}, bf16[8,16,1664]{2,1,0:T(8,128)(2,1)}) custom-call(bf16[2,240,1280]{2,1,0:T(8,128)(2,1)} %shard_map.86.here_ref, bf16[2,240,1280]{2,1,0:T(8,128)(2,1)} %copy-done.4, bf16[8,16,40,128]{3,2,1,0:T(8,128)(2,1)} %copy-done.1, bf16[2,208,160]{2,1,0:T(8,128)(2,1)} %get-tuple-element.11.ride_ref, ...), custom_call_target="tpu_custom_call" | custom-call | flops 1966080000 | bytes 4972544 | tf_op jit(solution)/shard_map/pallas_call | solution.py:178
  78.1 2.0 %collective-permute-start.4 = (f32[2,192,160]{2,1,0:T(8,128)}, f32[2,192,160]{2,1,0:T(8,128)S(1)}, u32[]{:S(2)}, u32[]{:S(2)}) collective-permute-start(f32[2,192,160]{2,1,0:T(8,128)} %get-tuple-element.6), channel_id=1, source_target_pairs={{0,16},{16,0},{1,17},{17,1},{2,18},{18,2},{3,19},{19,3},{4,20},{20... | collective-permute-start | bytes 737288 | tf_op jit(solution)/shard_map/ppermute | solution.py:290
  80.1 8.0 %all-to-all-start.2 = ((bf16[8,16,1664]{2,1,0:T(8,128)(2,1)}), bf16[8,16,1664]{2,1,0:T(8,128)(2,1)S(1)}, u32[]{:S(2)}, u32[]{:S(2)}) async-start(bf16[8,16,1664]{2,1,0:T(8,128)(2,1)} %get-tuple-element.7), calls=%async_computation.2 | async-start | bytes 851968 | tf_op jit(solution)/shard_map/all_to_all | solution.py:220
  88.0 1.5 %maximum_select_fusion = f32[2,192,320]{2,1,0:T(8,128)S(1)} fusion(f32[2,192,160]{2,1,0:T(8,128)S(1)} %collective-permute-done.4, f32[2,192,160]{2,1,0:T(8,128)} %get-tuple-element.5, pred[]{:T(512)S(6)} %eq.13), kind=kLoop, calls=%fused_computation.3 | loop fusion | flops 368640 | bytes 983041 | tf_op jit(solution)/shard_map/jit(_where)/select_n | solution.py:229
  89.5 6.9 %all-to-all-done.2 = bf16[8,16,1664]{2,1,0:T(8,128)(2,1)S(1)} async-done(((bf16[8,16,1664]{2,1,0:T(8,128)(2,1)}), bf16[8,16,1664]{2,1,0:T(8,128)(2,1)S(1)}, u32[]{:S(2)}, u32[]{:S(2)}) %all-to-all-start.2) | async-done | bytes 426016 | tf_op jit(solution)/shard_map/all_to_all | solution.py:220
  96.5 0.7 all_to_all.24
  97.2 8.7 %all-to-all-start.3 = ((f32[16,1,1664]{2,1,0:T(1,128)}), f32[16,1,1664]{2,1,0:T(1,128)S(1)}, u32[]{:S(2)}, u32[]{:S(2)}) async-start(f32[16,1,1664]{2,1,0:T(1,128)} %all_to_all.24), calls=%async_computation.3 | async-start | bytes 212992 | tf_op jit(solution)/shard_map/all_to_all | solution.py:220
  106.0 2.2 %collective-permute-start.5 = (f32[192,320]{1,0:T(8,128)S(1)}, f32[192,320]{1,0:T(8,128)S(1)}, u32[]{:S(2)}, u32[]{:S(2)}) collective-permute-start(f32[192,320]{1,0:T(8,128)S(1)} %get-tuple-element.9), channel_id=1, source_target_pairs={{0,128},{128,0},{1,129},{129,1},{2,130},{130,2},{3,131},{131,3},{4... | collective-permute-start | bytes 737288 | tf_op jit(solution)/shard_map/ppermute | solution.py:292
  108.2 9.6 %all-to-all-done.3 = f32[16,1,1664]{2,1,0:T(1,128)S(1)} async-done(((f32[16,1,1664]{2,1,0:T(1,128)}), f32[16,1,1664]{2,1,0:T(1,128)S(1)}, u32[]{:S(2)}, u32[]{:S(2)}) %all-to-all-start.3) | async-done | bytes 106528 | tf_op jit(solution)/shard_map/all_to_all | solution.py:220
  117.9 0.8 broadcast_in_dim.16
  118.6 8.4 %all-to-all-start.4 = ((f32[32,1,1664]{2,1,0:T(1,128)}), f32[32,1,1664]{2,1,0:T(1,128)S(1)}, u32[]{:S(2)}, u32[]{:S(2)}) async-start(f32[32,1,1664]{2,1,0:T(1,128)} %broadcast_in_dim.16), calls=%async_computation.4 | async-start | bytes 425984 | tf_op jit(solution)/shard_map/all_to_all | solution.py:220
  127.1 1.0 maximum_select_fusion.1
  128.1 7.5 %all-to-all-done.4 = f32[32,1,1664]{2,1,0:T(1,128)S(1)} async-done(((f32[32,1,1664]{2,1,0:T(1,128)}), f32[32,1,1664]{2,1,0:T(1,128)S(1)}, u32[]{:S(2)}, u32[]{:S(2)}) %all-to-all-start.4) | async-done | bytes 213024 | tf_op jit(solution)/shard_map/all_to_all | solution.py:220
  136.1 1.1 reshape.117
  (31 shorter events, 1.3 us)
Async XLA Ops:
  0.6 4.1 %copy-start = (bf16[80,1920]{1,0:T(8,128)(2,1)S(1)}, bf16[80,1920]{1,0:T(8,128)(2,1)}, u32[]{:S(2)}) copy-start(bf16[80,1920]{1,0:T(8,128)(2,1)} %param.11) | copy-start | bytes 921604
  0.6 22.7 %collective-permute-start = (bf16[240,1280]{1,0:T(8,128)(2,1)}, bf16[240,1280]{1,0:T(8,128)(2,1)S(1)}, u32[]{:S(2)}, u32[]{:S(2)}) collective-permute-start(bf16[240,1280]{1,0:T(8,128)(2,1)} %bitcast.19), channel_id=1, source_target_pairs={{0,128},{128,0},{1,129},{129,1},{2,130},{130,2},{3,131},{131,3},{4... | collective-permute-start | bytes 1843208 | tf_op jit(solution)/shard_map/ppermute | solution.py:259
  5.8 27.1 %all-to-all-start = ((bf16[16,40,128]{2,1,0:T(8,128)(2,1)}), bf16[16,40,128]{2,1,0:T(8,128)(2,1)S(1)}, u32[]{:S(2)}, u32[]{:S(2)}) async-start(bf16[16,40,128]{2,1,0:T(8,128)(2,1)} %broadcast_in_dim.14), calls=%async_computation | async-start | bytes 327680 | tf_op jit(solution)/shard_map/all_to_all | solution.py:220
  23.3 0.8 copy-start.2
  27.3 36.9 %collective-permute-start.1 = (bf16[2,240,1280]{2,1,0:T(8,128)(2,1)}, bf16[2,240,1280]{2,1,0:T(8,128)(2,1)S(1)}, u32[]{:S(2)}, u32[]{:S(2)}) collective-permute-start(bf16[2,240,1280]{2,1,0:T(8,128)(2,1)} %shard_map.86.here_ref), channel_id=1, source_target_pairs={{0,16},{16,0},{1,17},{17,1},{2,18},{18,2},{3,19},{19,3},{4,20},{20... | collective-permute-start | bytes 3686408 | tf_op jit(solution)/shard_map/ppermute | solution.py:273
  34.1 6.5 %copy-start.5 = (s32[1,1,3]{2,1,0:T(1,128)S(1)}, s32[1,1,3]{2,1,0:T(1,128)}, u32[]{:S(2)}) copy-start(s32[1,1,3]{2,1,0:T(1,128)} %param.8) | copy-start | bytes 40
  34.1 6.6 %copy-start.3 = (bf16[1,1,3,64,640]{4,3,2,1,0:T(8,128)(2,1)S(1)}, bf16[1,1,3,64,640]{4,3,2,1,0:T(8,128)(2,1)}, u32[]{:S(2)}) copy-start(bf16[1,1,3,64,640]{4,3,2,1,0:T(8,128)(2,1)} %param.13) | copy-start | bytes 737284
  34.1 30.1 %all-to-all-start.1 = ((bf16[8,16,40,128]{3,2,1,0:T(8,128)(2,1)}), bf16[8,16,40,128]{3,2,1,0:T(8,128)(2,1)S(1)}, u32[]{:S(2)}, u32[]{:S(2)}) async-start(bf16[8,16,40,128]{3,2,1,0:T(8,128)(2,1)} %broadcast_in_dim.15), calls=%async_computation.1 | async-start | bytes 2621440 | tf_op jit(solution)/shard_map/all_to_all | solution.py:220
  41.0 13.6 %collective-permute-start.2 = (bf16[208,320]{1,0:T(8,128)(2,1)S(1)}, bf16[208,320]{1,0:T(8,128)(2,1)S(1)}, u32[]{:S(2)}, u32[]{:S(2)}) collective-permute-start(bf16[208,320]{1,0:T(8,128)(2,1)S(1)} %get-tuple-element.13), channel_id=1, source_target_pairs={{0,128},{128,0},{1,129},{129,1},{2,130},{130,2},{3,131},{131,3},{4... | collective-permute-start | bytes 399368 | tf_op jit(solution)/shard_map/ppermute | solution.py:260
  55.5 8.7 %collective-permute-start.3 = (bf16[2,208,160]{2,1,0:T(8,128)(2,1)S(1)}, bf16[2,208,160]{2,1,0:T(8,128)(2,1)}, u32[]{:S(2)}, u32[]{:S(2)}) collective-permute-start(bf16[2,208,160]{2,1,0:T(8,128)(2,1)S(1)} %get-tuple-element.10), channel_id=1, source_target_pairs={{0,16},{16,0},{1,17},{17,1},{2,18},{18,2},{3,19},{19,3},{4,20},{20... | collective-permute-start | bytes 399368 | tf_op jit(solution)/shard_map/ppermute | solution.py:274
  64.2 1.1 copy-start.1
  64.3 1.4 %copy-start.4 = (bf16[2,240,1280]{2,1,0:T(8,128)(2,1)}, bf16[2,240,1280]{2,1,0:T(8,128)(2,1)S(1)}, u32[]{:S(2)}) copy-start(bf16[2,240,1280]{2,1,0:T(8,128)(2,1)S(1)} %collective-permute-done.1.there_ref) | copy-start | bytes 3686404
  78.1 9.9 %collective-permute-start.4 = (f32[2,192,160]{2,1,0:T(8,128)}, f32[2,192,160]{2,1,0:T(8,128)S(1)}, u32[]{:S(2)}, u32[]{:S(2)}) collective-permute-start(f32[2,192,160]{2,1,0:T(8,128)} %get-tuple-element.6), channel_id=1, source_target_pairs={{0,16},{16,0},{1,17},{17,1},{2,18},{18,2},{3,19},{19,3},{4,20},{20... | collective-permute-start | bytes 737288 | tf_op jit(solution)/shard_map/ppermute | solution.py:290
  80.1 16.4 %all-to-all-start.2 = ((bf16[8,16,1664]{2,1,0:T(8,128)(2,1)}), bf16[8,16,1664]{2,1,0:T(8,128)(2,1)S(1)}, u32[]{:S(2)}, u32[]{:S(2)}) async-start(bf16[8,16,1664]{2,1,0:T(8,128)(2,1)} %get-tuple-element.7), calls=%async_computation.2 | async-start | bytes 851968 | tf_op jit(solution)/shard_map/all_to_all | solution.py:220
  97.2 20.5 %all-to-all-start.3 = ((f32[16,1,1664]{2,1,0:T(1,128)}), f32[16,1,1664]{2,1,0:T(1,128)S(1)}, u32[]{:S(2)}, u32[]{:S(2)}) async-start(f32[16,1,1664]{2,1,0:T(1,128)} %all_to_all.24), calls=%async_computation.3 | async-start | bytes 212992 | tf_op jit(solution)/shard_map/all_to_all | solution.py:220
  106.0 21.1 %collective-permute-start.5 = (f32[192,320]{1,0:T(8,128)S(1)}, f32[192,320]{1,0:T(8,128)S(1)}, u32[]{:S(2)}, u32[]{:S(2)}) collective-permute-start(f32[192,320]{1,0:T(8,128)S(1)} %get-tuple-element.9), channel_id=1, source_target_pairs={{0,128},{128,0},{1,129},{129,1},{2,130},{130,2},{3,131},{131,3},{4... | collective-permute-start | bytes 737288 | tf_op jit(solution)/shard_map/ppermute | solution.py:292
  118.6 16.9 %all-to-all-start.4 = ((f32[32,1,1664]{2,1,0:T(1,128)}), f32[32,1,1664]{2,1,0:T(1,128)S(1)}, u32[]{:S(2)}, u32[]{:S(2)}) async-start(f32[32,1,1664]{2,1,0:T(1,128)} %broadcast_in_dim.16), calls=%async_computation.4 | async-start | bytes 425984 | tf_op jit(solution)/shard_map/all_to_all | solution.py:220

commit v3 on v2

v3 whole, which is shorter than its diff:
```python
import functools
import math

import jax
import jax.numpy as jnp
from jax import lax
from jax.experimental import pallas as pl
from jax.experimental.pallas import tpu as pltpu
from jax.sharding import Mesh
from jax.sharding import PartitionSpec as P

HEADS = 2
EPSILON = 1e-06
MASKED = -1e30
DP = ("xp", "xi", "y", "c")
PLANE = ("xp", "y")
SWAP = [(0, 1), (1, 0)]
LANES = 128
CHUNK = 16
WAVE = 4
LIMIT = 56 * 1024 * 1024


def pack_kernel(place_ref, counts_ref, images_ref, grads_ref, send_ref, keep_ref):
    rows, half = images_ref.shape[0], grads_ref.shape[1] // 2
    slots = counts_ref.shape[0]
    latent_count = grads_ref.shape[0] // slots
    row = iota((latent_count, half), 0)
    counts = jnp.zeros((latent_count, half), jnp.float32)
    for n in range(slots):
        counts = jnp.where(row == n, counts_ref[n].astype(jnp.float32), counts)
    blocks = [grads_ref[latent_count * n : latent_count * (n + 1), :] for n in range(slots)]
    low = jnp.concatenate([block[:, :half] for block in blocks] + [counts.astype(jnp.bfloat16)], axis=1)
    high = jnp.concatenate([block[:, half:] for block in blocks] + [counts.astype(jnp.bfloat16)], axis=1)
    first = place_ref[0] == 0
    send_ref[:rows, :] = images_ref[...]
    send_ref[rows:, :] = jnp.where(first, high, low)
    keep_ref[...] = jnp.where(first, low, high)


def norm_kernel(images_ref, keep_ref, came_ref, gain_ref, bias_ref, out_ref):
    gain, bias = gain_ref[...].reshape(1, -1), bias_ref[...].reshape(1, -1)
    rows = images_ref.shape[0]
    for index, source in enumerate((images_ref, came_ref)):
        for start in range(0, rows, CHUNK):
            values = source[start : start + CHUNK, :].astype(jnp.float32)
            centre = values - jnp.mean(values, axis=-1, keepdims=True)
            spread = jnp.mean(centre * centre, axis=-1, keepdims=True)
            normed = centre * lax.rsqrt(spread + EPSILON) * gain + bias
            out_ref[index, start : start + CHUNK, :] = normed.astype(jnp.bfloat16)
    out_ref[0, rows:, :] = keep_ref[...]
    out_ref[1, rows:, :] = came_ref[rows:, :]


def across(left, right):
    return lax.dot_general(left, right, (((1,), (1,)), ((), ())), preferred_element_type=jnp.float32)


def along(left, right):
    return lax.dot_general(left, right, (((0,), (0,)), ((), ())), preferred_element_type=jnp.float32)


def plain(left, right):
    return jnp.dot(left, right, preferred_element_type=jnp.float32)


def one_hot(chosen):
    return jnp.where(chosen, 1.0, 0.0).astype(jnp.bfloat16)


def iota(shape, axis):
    return lax.broadcasted_iota(jnp.int32, shape, axis)


def column_order(piece, quarter):
    row, out = iota((4 * LANES, 6 * LANES), 0), iota((4 * LANES, 6 * LANES), 1)
    kind = (out >= 2 * LANES).astype(jnp.int32) + (out >= 4 * LANES).astype(jnp.int32)
    lane = out - 2 * LANES * kind
    block = sum((lane >= piece * n).astype(jnp.int32) for n in (1, 2, 3))
    source = LANES * block + piece * kind + lane - piece * block
    return one_hot((row == source) & (lane < quarter))


def main_kernel(
    slots, latent_count, ring, sharers,
    index_ref, near_ref, far_ref, whole_ref, query_ref,
    lat_ref, lat_c_ref, packed_ref,
    weight_ref, grad_ref, total_ref, tail_ref,
):
    width_in = near_ref.shape[2]
    rows = near_ref.shape[1] - latent_count
    capacity = rows // slots
    quarter = lat_ref.shape[2]
    head_size = quarter // HEADS
    scale = 1.0 / math.sqrt(head_size)
    for block in range(4):
        halves = [whole_ref[4 * half + block].astype(jnp.float32) for half in range(2)]
        stacked = jnp.stack(halves, axis=1).reshape(width_in, LANES)
        weight_ref[:, LANES * block : LANES * (block + 1)] = stacked.astype(jnp.bfloat16)
    order = column_order(quarter // 4, quarter)
    first_head = iota((1, quarter), 1) < head_size
    nothing = jnp.zeros((), jnp.bfloat16)

    def head_of(array, head):
        return jnp.where(first_head, array, nothing) if head == 0 else jnp.where(first_head, nothing, array)

    def both_heads(array):
        return jnp.concatenate([head_of(array, 0), head_of(array, 1)], axis=0)

    width = query_ref.shape[1]
    pick = one_hot(
        (iota((width, 2 * LANES), 0) == quarter * index_ref[0] + iota((width, 2 * LANES), 1))
        & (iota((width, 2 * LANES), 1) < quarter)
    )
    query = both_heads(plain(query_ref[...], pick).astype(jnp.bfloat16)[:, :quarter])
    grad_ref[...] = jnp.zeros_like(grad_ref)
    image_of = [
        sum((iota(shape, axis) >= capacity * n).astype(jnp.int32) for n in range(1, slots))
        for shape, axis in (((rows, 1), 0), ((1, rows), 1))
    ]
    place = [
        (iota(shape, axis) - capacity * image).astype(jnp.float32)
        for (shape, axis), image in zip((((rows, 1), 0), ((1, rows), 1)), image_of)
    ]
    members = [ref.at[n] for ref in (near_ref, far_ref) for n in range(ref.shape[0])]
    first_pair = index_ref[0] % 2 == 0
    outs = [ref.at[n] for ref in (lat_ref, lat_c_ref) for n in range(ref.shape[0])]
    apart = slots, capacity, HEADS * latent_count

    def limits(block):
        sizes = members[block][rows : rows + 16, 2 * quarter * slots :].astype(jnp.float32)
        size = [sizes[n : n + 1, 0:1] for n in range(slots)]
        live = []
        for image, position in zip(image_of, place):
            limit = size[slots - 1] + jnp.zeros_like(position)
            for n in reversed(range(slots - 1)):
                limit = jnp.where(image == n, size[n], limit)
            live.append(position < limit)
        return jnp.where(live[0], image_of[0], -1), jnp.where(live[1], image_of[1], -2)

    def attention(scores, allowed):
        scores = jnp.where(allowed, scores * scale, MASKED)
        highest = jnp.max(scores, axis=-1, keepdims=True)
        raised = jnp.where(allowed, jnp.exp(scores - highest), 0.0)
        total = jnp.maximum(jnp.sum(raised, axis=-1, keepdims=True), 1.0)
        return (raised * (1.0 / total)).astype(jnp.bfloat16)

    def over_patches(scores, labels):
        inside = (labels[0] >= 0).reshape(slots, capacity, 1)
        masked = jnp.where(inside, scores.reshape(apart) * scale, MASKED)
        raised = jnp.where(inside, jnp.exp(masked - jnp.max(masked, axis=1, keepdims=True)), 0.0)
        return raised * (1.0 / jnp.maximum(jnp.sum(raised, axis=1, keepdims=True), 1.0))

    def normed(block):
        return members[block][:rows, :]

    def cotangent_of(block, n):
        ride = members[block][rows:, 2 * quarter * n : 2 * quarter * (n + 1)]
        return both_heads(jnp.where(first_pair, ride[:, :quarter], ride[:, quarter:]))

    def span(n):
        return slice(latent_count * n, latent_count * (n + 1))

    for first in range(0, len(members), WAVE):
        blocks = range(first, min(first + WAVE, len(members)))
        labels = [limits(b) for b in blocks]
        projected = [plain(normed(b), weight_ref[...]).astype(jnp.bfloat16) for b in blocks]
        parts = [plain(p, order).astype(jnp.bfloat16) for p in projected]
        parts = [[p[:, 2 * LANES * n : 2 * LANES * n + quarter] for n in range(3)] for p in parts]
        scores = [[across(head_of(q, h), k) for h in range(HEADS)] for q, k, _ in parts]
        weights = [[attention(s, m[0] == m[1]) for s in both] for both, m in zip(scores, labels)]
        mixed = [
            sum(plain(w[h], head_of(v, h)) for h in range(HEADS)).astype(jnp.bfloat16)
            for w, (_, _, v) in zip(weights, parts)
        ]
        shares = [over_patches(across(m, query), l) for m, l in zip(mixed, labels)]
        low = [s.astype(jnp.bfloat16) for s in shares]
        split = [m.reshape(slots, capacity, quarter) for m in mixed]
        cotangent = [[cotangent_of(b, n) for n in range(slots)] for b in blocks]
        share_grads = [
            jnp.stack([across(s[n], g[n]) for n in range(slots)]) for s, g in zip(split, cotangent)
        ]
        for b, l, s in zip(blocks, low, split):
            for n in range(slots):
                latents = along(l[n], s[n])
                outs[b][span(n), :] = jnp.where(first_head, latents[:latent_count], latents[latent_count:])
        score_grads = [
            s * (g - jnp.sum(s * g, axis=1, keepdims=True)) * scale for s, g in zip(shares, share_grads)
        ]
        score_grads = [g.reshape(rows, HEADS * latent_count) for g in score_grads]
        high = [g.astype(jnp.bfloat16) for g in score_grads]
        rest = [(g - h.astype(jnp.float32)).astype(jnp.bfloat16) for g, h in zip(score_grads, high)]
        from_values = [
            jnp.concatenate([plain(l[n], g[n]) for n in range(slots)], axis=0) for l, g in zip(low, cotangent)
        ]
        mixed_grad = [
            (v + (plain(h, query) + plain(r, query))).astype(jnp.bfloat16)
            for v, h, r in zip(from_values, high, rest)
        ]
        for b, w, g in zip(blocks, weights, mixed_grad):
            value_grad = sum(along(w[h], head_of(g, h)) for h in range(HEADS))
            grad_ref[rows * b : rows * (b + 1), :quarter] = value_grad.astype(jnp.bfloat16)
    total = sum(
        along(grad_ref[rows * b : rows * (b + 1), :], normed(b)) for b in range(len(members))
    )
    total_ref[...] = total[:LANES].T
    tail_ref[...] = total[LANES:].T
    depth = width_in // ring
    part = depth // sharers
    per_tile = LANES // (quarter - LANES)
    for sharer in range(sharers):
        rest = []
        for row in range(part):
            picked = pl.ds(sharer * part + row, ring, stride=depth)
            packed_ref[sharer, :, LANES * row : LANES * (row + 1)] = total_ref[picked, :].astype(jnp.bfloat16)
            tail = tail_ref[picked, :]
            shift = (row % per_tile) * (quarter - LANES)
            if shift == 0:
                rest.append(tail)
            else:
                rest[-1] = rest[-1] + pltpu.roll(tail, shift, 1)
        for n, tile in enumerate(rest):
            lanes = slice(LANES * (part + n), LANES * (part + n + 1))
            packed_ref[sharer, :, lanes] = tile.astype(jnp.bfloat16)


def order_kernel(index_ref, own_ref, x_ref, out_ref, parts_ref):
    quarter = own_ref.shape[2]
    parts_ref[:2] = own_ref[...]
    parts_ref[2:] = x_ref[...]
    for pair in range(4):
        out_ref[:, quarter * pair : quarter * (pair + 1)] = parts_ref[pair ^ index_ref[0]]


def call(kernel, outs, scratch, flops, *operands):
    memory = pl.BlockSpec(memory_space=pltpu.VMEM)
    scalars = pl.BlockSpec(memory_space=pltpu.SMEM)
    size = sum(math.prod(a.shape) * a.dtype.itemsize for a in (*operands, *outs))
    return pl.pallas_call(
        kernel,
        out_shape=outs,
        in_specs=[scalars if a.dtype == jnp.int32 else memory for a in operands],
        out_specs=[memory] * len(outs),
        scratch_shapes=scratch,
        compiler_params=pltpu.CompilerParams(vmem_limit_bytes=LIMIT),
        cost_estimate=pl.CostEstimate(flops=flops, bytes_accessed=size, transcendentals=0),
    )(*operands)


def pack(place, counts, images, grads):
    below = grads.shape[0] // counts.shape[0]
    send = jax.ShapeDtypeStruct((images.shape[0] + below, images.shape[1]), jnp.bfloat16)
    keep = jax.ShapeDtypeStruct((below, images.shape[1]), jnp.bfloat16)
    return call(pack_kernel, [send, keep], [], images.size, place, counts, images, grads)


def layer_norm(images, keep, came, gain, bias):
    out = jax.ShapeDtypeStruct((2,) + came.shape, jnp.bfloat16)
    return call(norm_kernel, [out], [], 40 * images.size, images, keep, came, gain, bias)[0]


def attend(index, near, far, whole, query, slots, latent_count, ring):
    width_in = near.shape[2]
    rows = near.shape[1] - latent_count
    quarter = query.shape[1] // 4
    sharers = whole.shape[0]
    part = width_in // ring // sharers
    packed = LANES * (part + -(-part * (quarter - LANES) // LANES))
    latents = jax.ShapeDtypeStruct((2, slots * latent_count, quarter), jnp.float32)
    return call(
        functools.partial(main_kernel, slots, latent_count, ring, sharers),
        [latents, latents, jax.ShapeDtypeStruct((sharers, ring, packed), jnp.bfloat16)],
        [
            pltpu.VMEM((width_in, 4 * LANES), jnp.bfloat16),
            pltpu.VMEM((4 * rows, 2 * LANES), jnp.bfloat16),
            pltpu.VMEM((width_in, LANES), jnp.float32),
            pltpu.VMEM((width_in, LANES), jnp.float32),
        ],
        2 * 4 * rows * width_in * 5 * quarter,
        index, near, far, whole, query,
    )


def copies(piece, count):
    return jnp.broadcast_to(piece[None], (count,) + piece.shape)


def exchange(array, axes):
    return lax.all_to_all(array, axes, 0, 0, tiled=True)


def unpack(packed, part, quarter):
    lead = packed.shape[:-1]
    head = packed[..., : LANES * part].reshape(lead + (part, LANES))
    rest = packed[..., LANES * part : LANES * part + part * (quarter - LANES)]
    return jnp.concatenate([head, rest.reshape(lead + (part, quarter - LANES))], axis=-1)


def on_device(patches, counts, norm_gain, norm_bias, input_weight, latent_query, cotangent):
    slots, capacity, width_in = patches.shape[2:]
    latent_count, width = cotangent.shape[3:]
    depth = input_weight.shape[0]
    ring = lax.axis_size("z")
    sharers = lax.axis_size(PLANE)
    xp, xi, y, c = (lax.axis_index(a) for a in DP)
    pair = 2 * xi + c
    quarter = width // 4

    images = patches.reshape(slots * capacity, width_in)
    grads = cotangent.reshape(slots * latent_count, width)
    send, keep = pack(xi.astype(jnp.int32).reshape(1), counts.reshape(slots), images, grads)
    came = lax.ppermute(send, "xi", SWAP)

    piece = quarter // 4
    rows = lax.dynamic_slice_in_dim(input_weight, xp * (depth // 2), depth // 2, 0)
    target = jnp.arange(LANES, dtype=jnp.int32)
    source = width * (target // piece) + quarter * pair + piece * y + target % piece
    source = jnp.where(target < 3 * piece, source, -1)
    pick = (jnp.arange(3 * width, dtype=jnp.int32)[:, None] == source[None, :]).astype(jnp.bfloat16)
    own = jnp.dot(rows, pick, preferred_element_type=jnp.float32).astype(jnp.bfloat16)
    gathered = exchange(copies(own, ring), "z")

    normed = layer_norm(images, keep, came, norm_gain, norm_bias)
    gathered, normed = lax.optimization_barrier((gathered, normed))
    normed_c = lax.ppermute(normed, "c", SWAP)

    whole = exchange(copies(gathered, sharers), PLANE)
    index = pair.astype(jnp.int32).reshape(1)
    latents, latents_c, packed = attend(
        index, normed, normed_c, whole, latent_query, slots, latent_count, ring
    )

    part = depth // sharers
    summed = jnp.sum(exchange(packed, PLANE).astype(jnp.float32), axis=0)
    summed, latents_c = lax.optimization_barrier((summed, latents_c))
    both = jnp.stack([latents, lax.ppermute(latents_c, "c", SWAP)], axis=1)
    summed = jnp.sum(exchange(summed, "z"), axis=0)
    latents_x = lax.ppermute(both[1], "xi", SWAP)
    done = unpack(exchange(copies(summed, 4 * sharers), DP), part, quarter)
    grad_value = (
        done.reshape(2, 2, 4, 2, part, quarter).transpose(0, 2, 4, 1, 3, 5).reshape(depth, width)
    )

    shape = jax.ShapeDtypeStruct((slots * latent_count, width), jnp.float32)
    parts = pltpu.VMEM((4,) + latents.shape[1:], jnp.float32)
    latents = call(order_kernel, [shape], [parts], both.size, index, both[0], latents_x)[0]
    return latents.reshape(cotangent.shape), grad_value


def solution(mesh):
    fine = Mesh(mesh.devices.reshape(2, 2, 4, 2, 16), DP + ("z",))
    placed = (
        P(DP, "z", None, None, None),
        P(DP, "z", None),
        P(),
        P(),
        P("z", None),
        P(),
        P(DP, "z", None, None, None),
    )
    return jax.shard_map(
        on_device,
        mesh=fine,
        in_specs=placed,
        out_specs=(P(DP, "z", None, None, None), P("z", None)),
        check_vma=False,
    )
```

time: 138 us -> 131 us (0.949)
  blocking collectives: 0 us -> 38 us
  starting transfers between devices: 67 us -> 43.4 us
  waiting for transfers between devices: 38.1 us -> 22.5 us
  local copies, waits for them, and re-layouts: 11.3 us -> 6.6 us
  other arithmetic: 3.89 us -> 0.99 us
  Pallas kernels: 15.6 us -> 17.3 us
    all_to_all x0 -> x2, blocking collectives: none -> 38 us  [exchange(): return lax.all_to_all(array, axes, 0, 0, tiled=True)]
    all_to_all x5 -> x3, starting transfers between devices: 46.5 us -> 26.3 us  [exchange(): return lax.all_to_all(array, axes, 0, 0, tiled=True)]
    ppermute x5 -> x3, waiting for transfers between devices: 11.7 us -> 0.01 us  [the longest x1 0.01 us: on_device(): both = jnp.stack([latents, lax.ppermute(latents_c, 'c', SWAP)], axis=1)]
    ppermute x5 -> x3, starting transfers between devices: 17.4 us -> 10.9 us  [the longest x1 4.75 us: on_device(): both = jnp.stack([latents, lax.ppermute(latents_c, 'c', SWAP)], axis=1)]
    all_to_all x5 -> x3, waiting for transfers between devices: 26.4 us -> 22.5 us  [exchange(): return lax.all_to_all(array, axes, 0, 0, tiled=True)]
    select_n x3 -> x0, other arithmetic: 3.39 us -> none  [the longest x2 2.48 us: in_order(): jnp.where(index == 0, jnp.concatenate([own, other], axis=-1), jnp.concate...]
    ppermute x1, starting transfers between devices: 3.13 us -> 6.28 us  [on_device(): normed_c = lax.ppermute(normed, 'c', SWAP)]
    broadcast_in_dim x2 -> x0, local copies, waits for them, and re-layouts: 2.58 us -> none  [the longest x1 1.3 us: layer_norm(): gain[None]]
  transfers between devices with their start and end apart: 11 -> 7, of which waited for: 5 -> 3; matrix products, arithmetic and copies ran while one was open for 8% -> 2% of each run, Pallas kernels for 2% -> 4%
where the time goes in v3:
time: 131 us; the launch traced here: 130 us
  starting transfers between devices  43.4 us (33%)
  blocking collectives  38 us (29%)
  waiting for transfers between devices  22.5 us (17%)
  Pallas kernels  17.3 us (13%)
  local copies, waits for them, and re-layouts  6.6 us (5%)
    all_to_all x2, blocking collectives, exchange(): return lax.all_to_all(array, axes, 0, 0, tiled=True)  38 us
    all_to_all x3, starting transfers between devices, exchange(): return lax.all_to_all(array, axes, 0, 0, tiled=True)  26.3 us
    all_to_all x3, waiting for transfers between devices, exchange(): return lax.all_to_all(array, axes, 0, 0, tiled=True)  22.5 us
    pallas_call x4, Pallas kernels, call(): pl.pallas_call(kernel, out_shape=outs, in_specs=[scalars if a.dtype == jn...  17.3 us
    ppermute x1, starting transfers between devices, on_device(): normed_c = lax.ppermute(normed, 'c', SWAP)  6.28 us
    ppermute x1, starting transfers between devices, on_device(): both = jnp.stack([latents, lax.ppermute(latents_c, 'c', SWAP)], axis=1)  4.75 us
    ppermute x1, starting transfers between devices, on_device(): came = lax.ppermute(send, 'xi', SWAP)  3.94 us
    unnamed x11, local copies, waits for them, and re-layouts  2.78 us
  transfers between devices with their start and end apart: 7, of which 3 were waited for; matrix products, arithmetic and copies ran while one was open for 2% of the time, Pallas kernels for 4%

profile of v3, /device:TPU:1, one launch (start us, length us, event | category | flops | bytes accessed | tf_op | source)
XLA Modules:
  0.0 129.9 jit_solution(14633914263819593476)
XLA Ops:
  0.6 0.0 copy-start
  0.7 2.2 %shard_map.86 = (bf16[304,1280]{1,0:T(8,128)(2,1)}, bf16[64,1280]{1,0:T(8,128)(2,1)}) custom-call(s32[1]{0:T(128)} %bitcast.2.place_ref, s32[3]{0:T(128)} %bitcast.25, bf16[240,1280]{1,0:T(8,128)(2,1)} %bitcast.17, bf16[192,640]{1,0:T(8,128)(2,1)} %bitcast.24), custom_call_target="tpu_custom_call" | custom-call | flops 307200 | bytes 1802256 | tf_op jit(solution)/shard_map/pallas_call | solution.py:239
  2.9 3.9 %collective-permute-start = (bf16[304,1280]{1,0:T(8,128)(2,1)}, bf16[304,1280]{1,0:T(8,128)(2,1)S(1)}, u32[]{:S(2)}, u32[]{:S(2)}) collective-permute-start(bf16[304,1280]{1,0:T(8,128)(2,1)} %get-tuple-element.12), channel_id=1, source_target_pairs={{0,128},{128,0},{1,129},{129,1},{2,130},{130,2},{3,131},{131,3},{4... | collective-permute-start | bytes 2334728 | tf_op jit(solution)/shard_map/ppermute | solution.py:312
  6.9 0.3 convolution_convert_fusion
  7.2 0.7 broadcast_in_dim.8
  7.9 14.9 %all-to-all-start = ((bf16[16,40,128]{2,1,0:T(8,128)(2,1)}), bf16[16,40,128]{2,1,0:T(8,128)(2,1)S(1)}, u32[]{:S(2)}, u32[]{:S(2)}) async-start(bf16[16,40,128]{2,1,0:T(8,128)(2,1)} %broadcast_in_dim.8), calls=%async_computation | async-start | bytes 327680 | tf_op jit(solution)/shard_map/all_to_all | solution.py:289
  22.8 0.9 copy-done.1
  23.7 3.5 %shard_map.87.near_ref = bf16[2,304,1280]{2,1,0:T(8,128)(2,1)} custom-call(bf16[240,1280]{1,0:T(8,128)(2,1)} %bitcast.18, bf16[64,1280]{1,0:T(8,128)(2,1)} %get-tuple-element.11.keep_ref, bf16[304,1280]{1,0:T(8,128)(2,1)} %copy-done.1, f32[1280]{0:T(1024)} %gain_ref.1, f32[1280]{0:T(1024)} %bias_ref.1), custom_call_target="tpu_custom_call" | custom-call | flops 12288000 | bytes 3123200 | tf_op jit(solution)/shard_map/pallas_call | solution.py:239
  27.1 7.8 %all-to-all-done = bf16[16,40,128]{2,1,0:T(8,128)(2,1)S(1)} async-done(((bf16[16,40,128]{2,1,0:T(8,128)(2,1)}), bf16[16,40,128]{2,1,0:T(8,128)(2,1)S(1)}, u32[]{:S(2)}, u32[]{:S(2)}) %all-to-all-start) | async-done | bytes 163872 | tf_op jit(solution)/shard_map/all_to_all | solution.py:289
  35.0 6.3 %collective-permute-start.1 = (bf16[2,304,1280]{2,1,0:T(8,128)(2,1)}, bf16[2,304,1280]{2,1,0:T(8,128)(2,1)S(1)}, u32[]{:S(2)}, u32[]{:S(2)}) collective-permute-start(bf16[2,304,1280]{2,1,0:T(8,128)(2,1)} %shard_map.87.near_ref), channel_id=1, source_target_pairs={{0,16},{16,0},{1,17},{17,1},{2,18},{18,2},{3,19},{19,3},{4,20},{20... | collective-permute-start | bytes 4669448 | tf_op jit(solution)/shard_map/ppermute | solution.py:325
  41.3 0.2 broadcast_in_dim.9
  41.4 25.1 %all_to_all.33.whole_ref = bf16[8,16,40,128]{3,2,1,0:T(8,128)(2,1)} all-to-all(bf16[8,16,40,128]{3,2,1,0:T(8,128)(2,1)S(1)} %broadcast_in_dim.9), channel_id=1, replica_groups=mesh['xp'=2,'xi'=2,'y'=4,'c'=2,'z'=16] {'xp','y'}, dimensions={0} | all-to-all | bytes 2621440 | tf_op jit(solution)/shard_map/all_to_all | solution.py:289
  66.6 1.2 copy-done.4
  67.7 9.4 %shard_map.88 = (f32[2,192,160]{2,1,0:T(8,128)}, f32[2,192,160]{2,1,0:T(8,128)}, bf16[8,16,1664]{2,1,0:T(8,128)(2,1)}) custom-call(s32[1]{0:T(128)} %bitcast.index_ref, bf16[2,304,1280]{2,1,0:T(8,128)(2,1)} %shard_map.87.near_ref, bf16[2,304,1280]{2,1,0:T(8,128)(2,1)} %copy-done.4, bf16[8,16,40,128]{3,2,1,0:T(8,128)(2,1)} %all_to_all.33.whole_ref, ...), custom_call_target="tpu_custom_call" | custom-call | flops 1966080000 | bytes 5423108 | tf_op jit(solution)/shard_map/pallas_call | solution.py:239
  77.1 12.9 %all_to_all.34 = bf16[8,16,1664]{2,1,0:T(8,128)(2,1)S(1)} all-to-all(bf16[8,16,1664]{2,1,0:T(8,128)(2,1)} %get-tuple-element.16), channel_id=1, replica_groups=mesh['xp'=2,'xi'=2,'y'=4,'c'=2,'z'=16] {'xp','y'}, dimensions={0} | all-to-all | bytes 851968 | tf_op jit(solution)/shard_map/all_to_all | solution.py:289
  90.0 0.1 convert_reduce_fusion
  90.1 4.8 %collective-permute-start.2 = (f32[2,192,160]{2,1,0:T(8,128)}, f32[2,192,160]{2,1,0:T(8,128)S(1)}, u32[]{:S(2)}, u32[]{:S(2)}) collective-permute-start(f32[2,192,160]{2,1,0:T(8,128)} %get-tuple-element.18), channel_id=1, source_target_pairs={{0,16},{16,0},{1,17},{17,1},{2,18},{18,2},{3,19},{19,3},{4,20},{20... | collective-permute-start | bytes 737288 | tf_op jit(solution)/shard_map/ppermute | solution.py:336
  94.8 0.7 all_to_all.24
  95.5 5.8 %all-to-all-start.3 = ((f32[16,1,1664]{2,1,0:T(1,128)}), f32[16,1,1664]{2,1,0:T(1,128)S(1)}, u32[]{:S(2)}, u32[]{:S(2)}) async-start(f32[16,1,1664]{2,1,0:T(1,128)} %all_to_all.24), calls=%async_computation.3 | async-start | bytes 212992 | tf_op jit(solution)/shard_map/all_to_all | solution.py:289
  101.3 0.0 collective-permute-done.2
  101.3 0.8 fusion.3
  102.1 2.2 %collective-permute-start.3 = (f32[2,192,160]{2,1,0:T(8,128)S(1)}, f32[2,192,160]{2,1,0:T(8,128)S(1)}, u32[]{:S(2)}, u32[]{:S(2)}) collective-permute-start(f32[2,192,160]{2,1,0:T(8,128)S(1)} %get-tuple-element.20), channel_id=1, source_target_pairs={{0,128},{128,0},{1,129},{129,1},{2,130},{130,2},{3,131},{131,3},{4... | collective-permute-start | bytes 737288 | tf_op jit(solution)/shard_map/ppermute | solution.py:338
  104.3 9.0 %all-to-all-done.3 = f32[16,1,1664]{2,1,0:T(1,128)S(1)} async-done(((f32[16,1,1664]{2,1,0:T(1,128)}), f32[16,1,1664]{2,1,0:T(1,128)S(1)}, u32[]{:S(2)}, u32[]{:S(2)}) %all-to-all-start.3) | async-done | bytes 106528 | tf_op jit(solution)/shard_map/all_to_all | solution.py:289
  113.3 0.1 reduce_sum.19
  113.4 0.8 broadcast_in_dim.10
  114.1 5.6 %all-to-all-start.4 = ((f32[32,1,1664]{2,1,0:T(1,128)}), f32[32,1,1664]{2,1,0:T(1,128)S(1)}, u32[]{:S(2)}, u32[]{:S(2)}) async-start(f32[32,1,1664]{2,1,0:T(1,128)} %broadcast_in_dim.10), calls=%async_computation.4 | async-start | bytes 425984 | tf_op jit(solution)/shard_map/all_to_all | solution.py:289
  119.8 0.7 copy-done.3
  120.5 2.2 %shard_map.89 = f32[192,640]{1,0:T(8,128)} custom-call(s32[1]{0:T(128)} %bitcast.index_ref, f32[2,192,160]{2,1,0:T(8,128)} %get-tuple-element.21.own_ref, f32[2,192,160]{2,1,0:T(8,128)} %copy-done.3), custom_call_target="tpu_custom_call" | custom-call | flops 122880 | bytes 983044 | tf_op jit(solution)/shard_map/pallas_call | solution.py:239
  122.7 5.7 %all-to-all-done.4 = f32[32,1,1664]{2,1,0:T(1,128)S(1)} async-done(((f32[32,1,1664]{2,1,0:T(1,128)}), f32[32,1,1664]{2,1,0:T(1,128)S(1)}, u32[]{:S(2)}, u32[]{:S(2)}) %all-to-all-start.4) | async-done | bytes 213024 | tf_op jit(solution)/shard_map/all_to_all | solution.py:289
  128.4 0.1 concatenate.9
  128.6 0.3 copy.10
  128.9 1.1 reshape.72
  (15 shorter events, 0.1 us)
Async XLA Ops:
  0.6 6.2 %copy-start = (bf16[80,1920]{1,0:T(8,128)(2,1)S(1)}, bf16[80,1920]{1,0:T(8,128)(2,1)}, u32[]{:S(2)}) copy-start(bf16[80,1920]{1,0:T(8,128)(2,1)} %param.11) | copy-start | bytes 921604
  2.9 19.9 %collective-permute-start = (bf16[304,1280]{1,0:T(8,128)(2,1)}, bf16[304,1280]{1,0:T(8,128)(2,1)S(1)}, u32[]{:S(2)}, u32[]{:S(2)}) collective-permute-start(bf16[304,1280]{1,0:T(8,128)(2,1)} %get-tuple-element.12), channel_id=1, source_target_pairs={{0,128},{128,0},{1,129},{129,1},{2,130},{130,2},{3,131},{131,3},{4... | collective-permute-start | bytes 2334728 | tf_op jit(solution)/shard_map/ppermute | solution.py:312
  7.9 27.1 %all-to-all-start = ((bf16[16,40,128]{2,1,0:T(8,128)(2,1)}), bf16[16,40,128]{2,1,0:T(8,128)(2,1)S(1)}, u32[]{:S(2)}, u32[]{:S(2)}) async-start(bf16[16,40,128]{2,1,0:T(8,128)(2,1)} %broadcast_in_dim.8), calls=%async_computation | async-start | bytes 327680 | tf_op jit(solution)/shard_map/all_to_all | solution.py:289
  22.8 0.9 copy-start.1
  35.0 31.6 %collective-permute-start.1 = (bf16[2,304,1280]{2,1,0:T(8,128)(2,1)}, bf16[2,304,1280]{2,1,0:T(8,128)(2,1)S(1)}, u32[]{:S(2)}, u32[]{:S(2)}) collective-permute-start(bf16[2,304,1280]{2,1,0:T(8,128)(2,1)} %shard_map.87.near_ref), channel_id=1, source_target_pairs={{0,16},{16,0},{1,17},{17,1},{2,18},{18,2},{3,19},{19,3},{4,20},{20... | collective-permute-start | bytes 4669448 | tf_op jit(solution)/shard_map/ppermute | solution.py:325
  66.6 1.2 copy-start.4
  77.1 24.2 %copy-start.2 = (f32[2,192,160]{2,1,0:T(8,128)S(1)}, f32[2,192,160]{2,1,0:T(8,128)}, u32[]{:S(2)}) copy-start(f32[2,192,160]{2,1,0:T(8,128)} %get-tuple-element.15) | copy-start | bytes 737284
  90.1 11.2 %collective-permute-start.2 = (f32[2,192,160]{2,1,0:T(8,128)}, f32[2,192,160]{2,1,0:T(8,128)S(1)}, u32[]{:S(2)}, u32[]{:S(2)}) collective-permute-start(f32[2,192,160]{2,1,0:T(8,128)} %get-tuple-element.18), channel_id=1, source_target_pairs={{0,16},{16,0},{1,17},{17,1},{2,18},{18,2},{3,19},{19,3},{4,20},{20... | collective-permute-start | bytes 737288 | tf_op jit(solution)/shard_map/ppermute | solution.py:336
  95.5 17.7 %all-to-all-start.3 = ((f32[16,1,1664]{2,1,0:T(1,128)}), f32[16,1,1664]{2,1,0:T(1,128)S(1)}, u32[]{:S(2)}, u32[]{:S(2)}) async-start(f32[16,1,1664]{2,1,0:T(1,128)} %all_to_all.24), calls=%async_computation.3 | async-start | bytes 212992 | tf_op jit(solution)/shard_map/all_to_all | solution.py:289
  102.1 17.6 %collective-permute-start.3 = (f32[2,192,160]{2,1,0:T(8,128)S(1)}, f32[2,192,160]{2,1,0:T(8,128)S(1)}, u32[]{:S(2)}, u32[]{:S(2)}) collective-permute-start(f32[2,192,160]{2,1,0:T(8,128)S(1)} %get-tuple-element.20), channel_id=1, source_target_pairs={{0,128},{128,0},{1,129},{129,1},{2,130},{130,2},{3,131},{131,3},{4... | collective-permute-start | bytes 737288 | tf_op jit(solution)/shard_map/ppermute | solution.py:338
  114.1 14.2 %all-to-all-start.4 = ((f32[32,1,1664]{2,1,0:T(1,128)}), f32[32,1,1664]{2,1,0:T(1,128)S(1)}, u32[]{:S(2)}, u32[]{:S(2)}) async-start(f32[32,1,1664]{2,1,0:T(1,128)} %broadcast_in_dim.10), calls=%async_computation.4 | async-start | bytes 425984 | tf_op jit(solution)/shard_map/all_to_all | solution.py:289
  119.8 0.7 copy-start.3

commit v4 on v3

--- a/solution.py
+++ b/solution.py
@@ -18,7 +18,7 @@
 LANES = 128
 CHUNK = 16
 WAVE = 4
-LIMIT = 56 * 1024 * 1024
+MIB = 1024 * 1024
 
 
 def pack_kernel(place_ref, counts_ref, images_ref, grads_ref, send_ref, keep_ref):
@@ -232,7 +232,7 @@
         out_ref[:, quarter * pair : quarter * (pair + 1)] = parts_ref[pair ^ index_ref[0]]
 
 
-def call(kernel, outs, scratch, flops, *operands):
+def call(kernel, outs, scratch, flops, *operands, limit=24):
     memory = pl.BlockSpec(memory_space=pltpu.VMEM)
     scalars = pl.BlockSpec(memory_space=pltpu.SMEM)
     size = sum(math.prod(a.shape) * a.dtype.itemsize for a in (*operands, *outs))
@@ -242,7 +242,7 @@
         in_specs=[scalars if a.dtype == jnp.int32 else memory for a in operands],
         out_specs=[memory] * len(outs),
         scratch_shapes=scratch,
-        compiler_params=pltpu.CompilerParams(vmem_limit_bytes=LIMIT),
+        compiler_params=pltpu.CompilerParams(vmem_limit_bytes=limit * MIB),
         cost_estimate=pl.CostEstimate(flops=flops, bytes_accessed=size, transcendentals=0),
     )(*operands)
 
@@ -251,7 +251,7 @@
     below = grads.shape[0] // counts.shape[0]
     send = jax.ShapeDtypeStruct((images.shape[0] + below, images.shape[1]), jnp.bfloat16)
     keep = jax.ShapeDtypeStruct((below, images.shape[1]), jnp.bfloat16)
-    return call(pack_kernel, [send, keep], [], images.size, place, counts, images, grads)
+    return call(pack_kernel, [send, keep], [], images.size, place, counts, images, grads, limit=56)
 
 
 def layer_norm(images, keep, came, gain, bias):
@@ -321,8 +321,8 @@
     gathered = exchange(copies(own, ring), "z")
 
     normed = layer_norm(images, keep, came, norm_gain, norm_bias)
-    gathered, normed = lax.optimization_barrier((gathered, normed))
     normed_c = lax.ppermute(normed, "c", SWAP)
+    gathered, _ = lax.optimization_barrier((gathered, normed))
 
     whole = exchange(copies(gathered, sharers), PLANE)
     index = pair.astype(jnp.int32).reshape(1)
@@ -331,12 +331,12 @@
     )
 
     part = depth // sharers
-    summed = jnp.sum(exchange(packed, PLANE).astype(jnp.float32), axis=0)
-    summed, latents_c = lax.optimization_barrier((summed, latents_c))
+    came = exchange(packed, PLANE).astype(jnp.float32)
+    summed = jnp.sum(came.reshape(sharers, ring, 1, -1), axis=0)
     both = jnp.stack([latents, lax.ppermute(latents_c, "c", SWAP)], axis=1)
     summed = jnp.sum(exchange(summed, "z"), axis=0)
     latents_x = lax.ppermute(both[1], "xi", SWAP)
-    done = unpack(exchange(copies(summed, 4 * sharers), DP), part, quarter)
+    done = unpack(exchange(copies(summed, 4 * sharers), DP)[:, 0], part, quarter)
     grad_value = (
         done.reshape(2, 2, 4, 2, part, quarter).transpose(0, 2, 4, 1, 3, 5).reshape(depth, width)
     )

time: 131 us -> 123 us (0.939)
  blocking collectives: 38 us -> 20.7 us
  starting transfers between devices: 43.4 us -> 59.4 us
  Pallas kernels: 17.3 us -> 12.7 us
  local copies, waits for them, and re-layouts: 6.6 us -> 4.78 us
    all_to_all x2 -> x1, blocking collectives: 38 us -> 20.7 us  [exchange(): return lax.all_to_all(array, axes, 0, 0, tiled=True)]
    all_to_all x3 -> x4, starting transfers between devices: 26.3 us -> 41.1 us  [exchange(): return lax.all_to_all(array, axes, 0, 0, tiled=True)]
    pallas_call x4, Pallas kernels: 17.3 us -> 12.7 us  [call(): pl.pallas_call(kernel, out_shape=outs, in_specs=[scalars if a.dtype == jn...]
    ppermute x1, starting transfers between devices: 4.75 us -> 7.76 us  [on_device(): both = jnp.stack([latents, lax.ppermute(latents_c, 'c', SWAP)], axis=1)]
    ppermute x1, starting transfers between devices: 6.28 us -> 4.41 us  [on_device(): normed_c = lax.ppermute(normed, 'c', SWAP)]
    unnamed x11 -> x13, local copies, waits for them, and re-layouts: 2.78 us -> 0.95 us
    all_to_all x3 -> x4, waiting for transfers between devices: 22.5 us -> 23.3 us  [exchange(): return lax.all_to_all(array, axes, 0, 0, tiled=True)]
  transfers between devices with their start and end apart: 7 -> 8, of which waited for: 3 -> 4; matrix products, arithmetic and copies ran while one was open for 2% -> 2% of each run, Pallas kernels for 4% -> 2%
where the time goes in v4:
time: 123 us
  starting transfers between devices  59.4 us (48%)
  waiting for transfers between devices  23.3 us (19%)
  blocking collectives  20.7 us (17%)
  Pallas kernels  12.7 us (10%)
  local copies, waits for them, and re-layouts  4.78 us (4%)
    all_to_all x4, starting transfers between devices, exchange(): return lax.all_to_all(array, axes, 0, 0, tiled=True)  41.1 us
    all_to_all x4, waiting for transfers between devices, exchange(): return lax.all_to_all(array, axes, 0, 0, tiled=True)  23.3 us
    all_to_all x1, blocking collectives, exchange(): return lax.all_to_all(array, axes, 0, 0, tiled=True)  20.7 us
    pallas_call x4, Pallas kernels, call(): pl.pallas_call(kernel, out_shape=outs, in_specs=[scalars if a.dtype == jn...  12.7 us
    ppermute x1, starting transfers between devices, on_device(): both = jnp.stack([latents, lax.ppermute(latents_c, 'c', SWAP)], axis=1)  7.76 us
    ppermute x1, starting transfers between devices, on_device(): normed_c = lax.ppermute(normed, 'c', SWAP)  4.41 us
    ppermute x1, starting transfers between devices, on_device(): came = lax.ppermute(send, 'xi', SWAP)  3.94 us
  transfers between devices with their start and end apart: 8, of which 4 were waited for; matrix products, arithmetic and copies ran while one was open for 2% of the time, Pallas kernels for 2%

profile of v4, /device:TPU:1, one launch (start us, length us, event | category | flops | bytes accessed | tf_op | source)
XLA Modules:
  0.0 122.5 jit_solution(8066255427012952004)
XLA Ops:
  0.6 0.0 copy-start
  0.7 2.2 %shard_map.86 = (bf16[304,1280]{1,0:T(8,128)(2,1)}, bf16[64,1280]{1,0:T(8,128)(2,1)}) custom-call(s32[1]{0:T(128)} %bitcast.2.place_ref, s32[3]{0:T(128)} %bitcast.25, bf16[240,1280]{1,0:T(8,128)(2,1)} %bitcast.17, bf16[192,640]{1,0:T(8,128)(2,1)} %bitcast.24), custom_call_target="tpu_custom_call" | custom-call | flops 307200 | bytes 1802256 | tf_op jit(solution)/shard_map/pallas_call | solution.py:239
  2.9 3.9 %collective-permute-start = (bf16[304,1280]{1,0:T(8,128)(2,1)}, bf16[304,1280]{1,0:T(8,128)(2,1)S(1)}, u32[]{:S(2)}, u32[]{:S(2)}) collective-permute-start(bf16[304,1280]{1,0:T(8,128)(2,1)} %get-tuple-element.9), channel_id=1, source_target_pairs={{0,128},{128,0},{1,129},{129,1},{2,130},{130,2},{3,131},{131,3},{4... | collective-permute-start | bytes 2334728 | tf_op jit(solution)/shard_map/ppermute | solution.py:312
  6.9 0.3 convolution_convert_fusion
  7.2 0.7 broadcast_in_dim.8
  7.9 14.9 %all-to-all-start = ((bf16[16,40,128]{2,1,0:T(8,128)(2,1)}), bf16[16,40,128]{2,1,0:T(8,128)(2,1)S(1)}, u32[]{:S(2)}, u32[]{:S(2)}) async-start(bf16[16,40,128]{2,1,0:T(8,128)(2,1)} %broadcast_in_dim.8), calls=%async_computation | async-start | bytes 327680 | tf_op jit(solution)/shard_map/all_to_all | solution.py:289
  22.9 0.0 copy-start.2
  22.9 0.9 copy-done.2
  23.8 0.9 shard_map.87.near_ref
  24.7 4.4 %collective-permute-start.1 = (bf16[2,304,1280]{2,1,0:T(8,128)(2,1)S(1)}, bf16[2,304,1280]{2,1,0:T(8,128)(2,1)}, u32[]{:S(2)}, u32[]{:S(2)}) collective-permute-start(bf16[2,304,1280]{2,1,0:T(8,128)(2,1)S(1)} %shard_map.87.near_ref), channel_id=1, source_target_pairs={{0,16},{16,0},{1,17},{17,1},{2,18},{18,2},{3,19},{19,3},{4,20},{20... | collective-permute-start | bytes 4669448 | tf_op jit(solution)/shard_map/ppermute | solution.py:324
  29.1 5.9 %all-to-all-done = bf16[16,40,128]{2,1,0:T(8,128)(2,1)S(1)} async-done(((bf16[16,40,128]{2,1,0:T(8,128)(2,1)}), bf16[16,40,128]{2,1,0:T(8,128)(2,1)S(1)}, u32[]{:S(2)}, u32[]{:S(2)}) %all-to-all-start) | async-done | bytes 163872 | tf_op jit(solution)/shard_map/all_to_all | solution.py:289
  35.0 0.2 broadcast_in_dim.9
  35.2 0.0 copy-start.5
  35.2 20.7 %all_to_all.25.whole_ref = bf16[8,16,40,128]{3,2,1,0:T(8,128)(2,1)S(1)} all-to-all(bf16[8,16,40,128]{3,2,1,0:T(8,128)(2,1)S(1)} %broadcast_in_dim.9), channel_id=1, replica_groups=mesh['xp'=2,'xi'=2,'y'=4,'c'=2,'z'=16] {'xp','y'}, dimensions={0} | all-to-all | bytes 2621440 | tf_op jit(solution)/shard_map/all_to_all | solution.py:289
  55.9 8.5 %shard_map.88 = (f32[2,192,160]{2,1,0:T(8,128)S(1)}, f32[2,192,160]{2,1,0:T(8,128)S(1)}, bf16[8,16,1664]{2,1,0:T(8,128)(2,1)}) custom-call(s32[1]{0:T(128)} %bitcast.index_ref, bf16[2,304,1280]{2,1,0:T(8,128)(2,1)S(1)} %shard_map.87.near_ref, bf16[2,304,1280]{2,1,0:T(8,128)(2,1)} %collective-permute-done.1.far_ref, ...), custom_call_target="tpu_custom_call" | custom-call | flops 1966080000 | bytes 5423108 | tf_op jit(solution)/shard_map/pallas_call | solution.py:239
  64.5 4.1 %all-to-all-start.2 = ((bf16[8,16,1664]{2,1,0:T(8,128)(2,1)}), bf16[8,16,1664]{2,1,0:T(8,128)(2,1)S(1)}, u32[]{:S(2)}, u32[]{:S(2)}) async-start(bf16[8,16,1664]{2,1,0:T(8,128)(2,1)} %get-tuple-element.13), calls=%async_computation.2 | async-start | bytes 851968 | tf_op jit(solution)/shard_map/all_to_all | solution.py:289
  68.6 7.8 %collective-permute-start.2 = (f32[2,192,160]{2,1,0:T(8,128)S(1)}, f32[2,192,160]{2,1,0:T(8,128)S(1)}, u32[]{:S(2)}, u32[]{:S(2)}) collective-permute-start(f32[2,192,160]{2,1,0:T(8,128)S(1)} %get-tuple-element.12), channel_id=1, source_target_pairs={{0,16},{16,0},{1,17},{17,1},{2,18},{18,2},{3,19},{19,3},{4,20},{20... | collective-permute-start | bytes 737288 | tf_op jit(solution)/shard_map/ppermute | solution.py:336
  76.3 0.5 all-to-all-done.2
  76.8 0.1 convert_reduce_fusion
  76.9 0.7 reduce_sum.21
  77.6 14.0 %all-to-all-start.3 = ((f32[16,1,1664]{2,1,0:T(1,128)}), f32[16,1,1664]{2,1,0:T(1,128)S(1)}, u32[]{:S(2)}, u32[]{:S(2)}) async-start(f32[16,1,1664]{2,1,0:T(1,128)} %reduce_sum.21), calls=%async_computation.3 | async-start | bytes 212992 | tf_op jit(solution)/shard_map/all_to_all | solution.py:289
  91.6 0.1 fusion.3
  91.7 2.2 %collective-permute-start.3 = (f32[2,192,160]{2,1,0:T(8,128)S(1)}, f32[2,192,160]{2,1,0:T(8,128)S(1)}, u32[]{:S(2)}, u32[]{:S(2)}) collective-permute-start(f32[2,192,160]{2,1,0:T(8,128)S(1)} %get-tuple-element.14), channel_id=1, source_target_pairs={{0,128},{128,0},{1,129},{129,1},{2,130},{130,2},{3,131},{131,3},{4... | collective-permute-start | bytes 737288 | tf_op jit(solution)/shard_map/ppermute | solution.py:338
  93.9 9.5 %all-to-all-done.3 = f32[16,1,1664]{2,1,0:T(1,128)S(1)} async-done(((f32[16,1,1664]{2,1,0:T(1,128)}), f32[16,1,1664]{2,1,0:T(1,128)S(1)}, u32[]{:S(2)}, u32[]{:S(2)}) %all-to-all-start.3) | async-done | bytes 106528 | tf_op jit(solution)/shard_map/all_to_all | solution.py:289
  103.5 0.1 reduce_sum.22
  103.5 0.8 broadcast_in_dim.10
  104.3 8.1 %all-to-all-start.4 = ((f32[32,1,1664]{2,1,0:T(1,128)}), f32[32,1,1664]{2,1,0:T(1,128)S(1)}, u32[]{:S(2)}, u32[]{:S(2)}) async-start(f32[32,1,1664]{2,1,0:T(1,128)} %broadcast_in_dim.10), calls=%async_computation.4 | async-start | bytes 425984 | tf_op jit(solution)/shard_map/all_to_all | solution.py:289
  112.5 1.1 shard_map.89
  113.5 7.4 %all-to-all-done.4 = f32[32,1,1664]{2,1,0:T(1,128)S(1)} async-done(((f32[32,1,1664]{2,1,0:T(1,128)}), f32[32,1,1664]{2,1,0:T(1,128)S(1)}, u32[]{:S(2)}, u32[]{:S(2)}) %all-to-all-start.4) | async-done | bytes 213024 | tf_op jit(solution)/shard_map/all_to_all | solution.py:289
  121.0 0.1 concatenate.9
  121.2 0.3 copy.10
  121.4 1.1 reshape.71
  (18 shorter events, 0.2 us)
Async XLA Ops:
  0.6 6.3 %copy-start = (bf16[80,1920]{1,0:T(8,128)(2,1)S(1)}, bf16[80,1920]{1,0:T(8,128)(2,1)}, u32[]{:S(2)}) copy-start(bf16[80,1920]{1,0:T(8,128)(2,1)} %param.11) | copy-start | bytes 921604
  0.6 22.2 %copy-start.1 = (bf16[1,1,3,80,1280]{4,3,2,1,0:T(8,128)(2,1)S(1)}, bf16[1,1,3,80,1280]{4,3,2,1,0:T(8,128)(2,1)}, u32[]{:S(2)}) copy-start(bf16[1,1,3,80,1280]{4,3,2,1,0:T(8,128)(2,1)} %param.7) | copy-start | bytes 1843204
  0.7 22.2 %copy-start.4 = (f32[1280]{0:T(1024)S(1)}, f32[1280]{0:T(1024)}, u32[]{:S(2)}) copy-start(f32[1280]{0:T(1024)} %bias_ref.1) | copy-start | bytes 15364
  0.7 22.2 %copy-start.3 = (f32[1280]{0:T(1024)S(1)}, f32[1280]{0:T(1024)}, u32[]{:S(2)}) copy-start(f32[1280]{0:T(1024)} %gain_ref.1) | copy-start | bytes 15364
  2.9 19.9 %collective-permute-start = (bf16[304,1280]{1,0:T(8,128)(2,1)}, bf16[304,1280]{1,0:T(8,128)(2,1)S(1)}, u32[]{:S(2)}, u32[]{:S(2)}) collective-permute-start(bf16[304,1280]{1,0:T(8,128)(2,1)} %get-tuple-element.9), channel_id=1, source_target_pairs={{0,128},{128,0},{1,129},{129,1},{2,130},{130,2},{3,131},{131,3},{4... | collective-permute-start | bytes 2334728 | tf_op jit(solution)/shard_map/ppermute | solution.py:312
  7.9 27.1 %all-to-all-start = ((bf16[16,40,128]{2,1,0:T(8,128)(2,1)}), bf16[16,40,128]{2,1,0:T(8,128)(2,1)S(1)}, u32[]{:S(2)}, u32[]{:S(2)}) async-start(bf16[16,40,128]{2,1,0:T(8,128)(2,1)} %broadcast_in_dim.8), calls=%async_computation | async-start | bytes 327680 | tf_op jit(solution)/shard_map/all_to_all | solution.py:289
  22.9 0.9 copy-start.2
  24.7 31.2 %collective-permute-start.1 = (bf16[2,304,1280]{2,1,0:T(8,128)(2,1)S(1)}, bf16[2,304,1280]{2,1,0:T(8,128)(2,1)}, u32[]{:S(2)}, u32[]{:S(2)}) collective-permute-start(bf16[2,304,1280]{2,1,0:T(8,128)(2,1)S(1)} %shard_map.87.near_ref), channel_id=1, source_target_pairs={{0,16},{16,0},{1,17},{17,1},{2,18},{18,2},{3,19},{19,3},{4,20},{20... | collective-permute-start | bytes 4669448 | tf_op jit(solution)/shard_map/ppermute | solution.py:324
  35.2 20.7 %copy-start.5 = (bf16[64,640]{1,0:T(8,128)(2,1)S(1)}, bf16[64,640]{1,0:T(8,128)(2,1)}, u32[]{:S(2)}) copy-start(bf16[64,640]{1,0:T(8,128)(2,1)} %query_ref.1) | copy-start | bytes 245764
  64.5 12.3 %all-to-all-start.2 = ((bf16[8,16,1664]{2,1,0:T(8,128)(2,1)}), bf16[8,16,1664]{2,1,0:T(8,128)(2,1)S(1)}, u32[]{:S(2)}, u32[]{:S(2)}) async-start(bf16[8,16,1664]{2,1,0:T(8,128)(2,1)} %get-tuple-element.13), calls=%async_computation.2 | async-start | bytes 851968 | tf_op jit(solution)/shard_map/all_to_all | solution.py:289
  68.6 23.0 %collective-permute-start.2 = (f32[2,192,160]{2,1,0:T(8,128)S(1)}, f32[2,192,160]{2,1,0:T(8,128)S(1)}, u32[]{:S(2)}, u32[]{:S(2)}) collective-permute-start(f32[2,192,160]{2,1,0:T(8,128)S(1)} %get-tuple-element.12), channel_id=1, source_target_pairs={{0,16},{16,0},{1,17},{17,1},{2,18},{18,2},{3,19},{19,3},{4,20},{20... | collective-permute-start | bytes 737288 | tf_op jit(solution)/shard_map/ppermute | solution.py:336
  77.6 25.9 %all-to-all-start.3 = ((f32[16,1,1664]{2,1,0:T(1,128)}), f32[16,1,1664]{2,1,0:T(1,128)S(1)}, u32[]{:S(2)}, u32[]{:S(2)}) async-start(f32[16,1,1664]{2,1,0:T(1,128)} %reduce_sum.21), calls=%async_computation.3 | async-start | bytes 212992 | tf_op jit(solution)/shard_map/all_to_all | solution.py:289
  91.7 20.8 %collective-permute-start.3 = (f32[2,192,160]{2,1,0:T(8,128)S(1)}, f32[2,192,160]{2,1,0:T(8,128)S(1)}, u32[]{:S(2)}, u32[]{:S(2)}) collective-permute-start(f32[2,192,160]{2,1,0:T(8,128)S(1)} %get-tuple-element.14), channel_id=1, source_target_pairs={{0,128},{128,0},{1,129},{129,1},{2,130},{130,2},{3,131},{131,3},{4... | collective-permute-start | bytes 737288 | tf_op jit(solution)/shard_map/ppermute | solution.py:338
  104.3 16.6 %all-to-all-start.4 = ((f32[32,1,1664]{2,1,0:T(1,128)}), f32[32,1,1664]{2,1,0:T(1,128)S(1)}, u32[]{:S(2)}, u32[]{:S(2)}) async-start(f32[32,1,1664]{2,1,0:T(1,128)} %broadcast_in_dim.10), calls=%async_computation.4 | async-start | bytes 425984 | tf_op jit(solution)/shard_map/all_to_all | solution.py:289

commit v5 on v4

--- a/solution.py
+++ b/solution.py
@@ -12,8 +12,9 @@
 HEADS = 2
 EPSILON = 1e-06
 MASKED = -1e30
-DP = ("xp", "xi", "y", "c")
-PLANE = ("xp", "y")
+DP = ("x", "y", "c")
+PLANE = ("x", "y")
+RING = ("zh", "zl")
 SWAP = [(0, 1), (1, 0)]
 LANES = 128
 CHUNK = 16
@@ -38,18 +39,21 @@
     keep_ref[...] = jnp.where(first, low, high)
 
 
-def norm_kernel(images_ref, keep_ref, came_ref, gain_ref, bias_ref, out_ref):
+def norm_kernel(rows_ref, below_ref, gain_ref, bias_ref, out_ref):
     gain, bias = gain_ref[...].reshape(1, -1), bias_ref[...].reshape(1, -1)
-    rows = images_ref.shape[0]
-    for index, source in enumerate((images_ref, came_ref)):
-        for start in range(0, rows, CHUNK):
-            values = source[start : start + CHUNK, :].astype(jnp.float32)
-            centre = values - jnp.mean(values, axis=-1, keepdims=True)
-            spread = jnp.mean(centre * centre, axis=-1, keepdims=True)
-            normed = centre * lax.rsqrt(spread + EPSILON) * gain + bias
-            out_ref[index, start : start + CHUNK, :] = normed.astype(jnp.bfloat16)
-    out_ref[0, rows:, :] = keep_ref[...]
-    out_ref[1, rows:, :] = came_ref[rows:, :]
+    rows = out_ref.shape[0] - below_ref.shape[0]
+    for start in range(0, rows, CHUNK):
+        values = rows_ref[start : start + CHUNK, :].astype(jnp.float32)
+        centre = values - jnp.mean(values, axis=-1, keepdims=True)
+        spread = jnp.mean(centre * centre, axis=-1, keepdims=True)
+        normed = centre * lax.rsqrt(spread + EPSILON) * gain + bias
+        out_ref[start : start + CHUNK, :] = normed.astype(jnp.bfloat16)
+    out_ref[rows:, :] = below_ref[...]
+
+
+def norm_came_kernel(came_ref, gain_ref, bias_ref, out_ref, *, below):
+    rows = out_ref.shape[0] - below
+    norm_kernel(came_ref.at[:rows], came_ref.at[rows:], gain_ref, bias_ref, out_ref)
 
 
 def across(left, right):
@@ -72,32 +76,41 @@
     return lax.broadcasted_iota(jnp.int32, shape, axis)
 
 
-def column_order(piece, quarter):
-    row, out = iota((4 * LANES, 6 * LANES), 0), iota((4 * LANES, 6 * LANES), 1)
-    kind = (out >= 2 * LANES).astype(jnp.int32) + (out >= 4 * LANES).astype(jnp.int32)
-    lane = out - 2 * LANES * kind
-    block = sum((lane >= piece * n).astype(jnp.int32) for n in (1, 2, 3))
-    source = LANES * block + piece * kind + lane - piece * block
-    return one_hot((row == source) & (lane < quarter))
+def columns(projected, piece, start, stop):
+    span = 3 * piece
+    parts = []
+    for tile in range(start // span, (stop - 1) // span + 1):
+        low, high = max(start - span * tile, 0), min(stop - span * tile, span)
+        parts.append(projected[:, LANES * tile + low : LANES * tile + high])
+    return jnp.concatenate(parts, axis=1)
 
 
 def main_kernel(
     slots, latent_count, ring, sharers,
-    index_ref, near_ref, far_ref, whole_ref, query_ref,
+    indepartner_ref, own_ref, partner_ref, own_c_ref, partner_c_ref, whole_ref, query_ref,
     lat_ref, lat_c_ref, packed_ref,
-    weight_ref, grad_ref, total_ref, tail_ref,
+    held_ref, arrived, weight_ref, grad_ref, total_ref, tail_ref,
 ):
-    width_in = near_ref.shape[2]
-    rows = near_ref.shape[1] - latent_count
+    width_in = own_ref.shape[1]
+    rows = own_ref.shape[0] - latent_count
+    fetched = [
+        pltpu.make_async_copy(ref, held_ref.at[n], arrived.at[n])
+        for n, ref in enumerate((own_ref, partner_ref, own_c_ref, partner_c_ref))
+    ]
+    for copy in fetched:
+        copy.start()
     capacity = rows // slots
     quarter = lat_ref.shape[2]
     head_size = quarter // HEADS
     scale = 1.0 / math.sqrt(head_size)
+    strip = width_in // ring // 4
     for block in range(4):
-        halves = [whole_ref[4 * half + block].astype(jnp.float32) for half in range(2)]
-        stacked = jnp.stack(halves, axis=1).reshape(width_in, LANES)
-        weight_ref[:, LANES * block : LANES * (block + 1)] = stacked.astype(jnp.bfloat16)
-    order = column_order(quarter // 4, quarter)
+        for part in range(4):
+            strips = whole_ref[4 * part + block].astype(jnp.float32)
+            for step in range(ring):
+                start = strip * (4 * step + part)
+                total_ref[start : start + strip, :] = strips[step, :strip]
+        weight_ref[:, LANES * block : LANES * (block + 1)] = total_ref[...].astype(jnp.bfloat16)
     first_head = iota((1, quarter), 1) < head_size
     nothing = jnp.zeros((), jnp.bfloat16)
 
@@ -109,11 +122,11 @@
 
     width = query_ref.shape[1]
     pick = one_hot(
-        (iota((width, 2 * LANES), 0) == quarter * index_ref[0] + iota((width, 2 * LANES), 1))
+        (iota((width, 2 * LANES), 0) == quarter * indepartner_ref[0] + iota((width, 2 * LANES), 1))
         & (iota((width, 2 * LANES), 1) < quarter)
     )
     query = both_heads(plain(query_ref[...], pick).astype(jnp.bfloat16)[:, :quarter])
-    grad_ref[...] = jnp.zeros_like(grad_ref)
+    tail_ref[...] = jnp.zeros_like(tail_ref)
     image_of = [
         sum((iota(shape, axis) >= capacity * n).astype(jnp.int32) for n in range(1, slots))
         for shape, axis in (((rows, 1), 0), ((1, rows), 1))
@@ -122,8 +135,8 @@
         (iota(shape, axis) - capacity * image).astype(jnp.float32)
         for (shape, axis), image in zip((((rows, 1), 0), ((1, rows), 1)), image_of)
     ]
-    members = [ref.at[n] for ref in (near_ref, far_ref) for n in range(ref.shape[0])]
-    first_pair = index_ref[0] % 2 == 0
+    members = [held_ref.at[n] for n in range(4)]
+    first_pair = indepartner_ref[0] % 2 == 0
     outs = [ref.at[n] for ref in (lat_ref, lat_c_ref) for n in range(ref.shape[0])]
     apart = slots, capacity, HEADS * latent_count
 
@@ -141,7 +154,7 @@
     def attention(scores, allowed):
         scores = jnp.where(allowed, scores * scale, MASKED)
         highest = jnp.max(scores, axis=-1, keepdims=True)
-        raised = jnp.where(allowed, jnp.exp(scores - highest), 0.0)
+        raised = jnp.exp(scores - highest)
         total = jnp.maximum(jnp.sum(raised, axis=-1, keepdims=True), 1.0)
         return (raised * (1.0 / total)).astype(jnp.bfloat16)
 
@@ -161,12 +174,15 @@
     def span(n):
         return slice(latent_count * n, latent_count * (n + 1))
 
+    for copy in fetched:
+        copy.wait()
     for first in range(0, len(members), WAVE):
         blocks = range(first, min(first + WAVE, len(members)))
         labels = [limits(b) for b in blocks]
         projected = [plain(normed(b), weight_ref[...]).astype(jnp.bfloat16) for b in blocks]
-        parts = [plain(p, order).astype(jnp.bfloat16) for p in projected]
-        parts = [[p[:, 2 * LANES * n : 2 * LANES * n + quarter] for n in range(3)] for p in parts]
+        parts = [
+            [columns(p, quarter // 4, quarter * n, quarter * (n + 1)) for n in range(3)] for p in projected
+        ]
         scores = [[across(head_of(q, h), k) for h in range(HEADS)] for q, k, _ in parts]
         weights = [[attention(s, m[0] == m[1]) for s in both] for both, m in zip(scores, labels)]
         mixed = [
@@ -199,12 +215,12 @@
         ]
         for b, w, g in zip(blocks, weights, mixed_grad):
             value_grad = sum(along(w[h], head_of(g, h)) for h in range(HEADS))
-            grad_ref[rows * b : rows * (b + 1), :quarter] = value_grad.astype(jnp.bfloat16)
+            grad_ref[rows * b : rows * (b + 1), :] = value_grad.astype(jnp.bfloat16)
     total = sum(
         along(grad_ref[rows * b : rows * (b + 1), :], normed(b)) for b in range(len(members))
     )
     total_ref[...] = total[:LANES].T
-    tail_ref[...] = total[LANES:].T
+    tail_ref[:, : quarter - LANES] = total[LANES:].T
     depth = width_in // ring
     part = depth // sharers
     per_tile = LANES // (quarter - LANES)
@@ -224,22 +240,25 @@
             packed_ref[sharer, :, lanes] = tile.astype(jnp.bfloat16)
 
 
-def order_kernel(index_ref, own_ref, x_ref, out_ref, parts_ref):
+def order_kernel(indepartner_ref, own_ref, partner_ref, out_ref, parts_ref):
     quarter = own_ref.shape[2]
     parts_ref[:2] = own_ref[...]
-    parts_ref[2:] = x_ref[...]
+    parts_ref[2:] = partner_ref[...]
     for pair in range(4):
-        out_ref[:, quarter * pair : quarter * (pair + 1)] = parts_ref[pair ^ index_ref[0]]
-
-
-def call(kernel, outs, scratch, flops, *operands, limit=24):
+        out_ref[:, quarter * pair : quarter * (pair + 1)] = parts_ref[pair ^ indepartner_ref[0]]
+
+
+def call(kernel, outs, scratch, flops, *operands, limit=24, unplaced=()):
     memory = pl.BlockSpec(memory_space=pltpu.VMEM)
     scalars = pl.BlockSpec(memory_space=pltpu.SMEM)
     size = sum(math.prod(a.shape) * a.dtype.itemsize for a in (*operands, *outs))
     return pl.pallas_call(
         kernel,
         out_shape=outs,
-        in_specs=[scalars if a.dtype == jnp.int32 else memory for a in operands],
+        in_specs=[
+            pl.BlockSpec(memory_space=pl.ANY) if n in unplaced else scalars if a.dtype == jnp.int32 else memory
+            for n, a in enumerate(operands)
+        ],
         out_specs=[memory] * len(outs),
         scratch_shapes=scratch,
         compiler_params=pltpu.CompilerParams(vmem_limit_bytes=limit * MIB),
@@ -254,14 +273,20 @@
     return call(pack_kernel, [send, keep], [], images.size, place, counts, images, grads, limit=56)
 
 
-def layer_norm(images, keep, came, gain, bias):
-    out = jax.ShapeDtypeStruct((2,) + came.shape, jnp.bfloat16)
-    return call(norm_kernel, [out], [], 40 * images.size, images, keep, came, gain, bias)[0]
-
-
-def attend(index, near, far, whole, query, slots, latent_count, ring):
-    width_in = near.shape[2]
-    rows = near.shape[1] - latent_count
+def layer_norm(rows, below, gain, bias):
+    out = jax.ShapeDtypeStruct((rows.shape[0] + below.shape[0], rows.shape[1]), jnp.bfloat16)
+    return call(norm_kernel, [out], [], 20 * rows.size, rows, below, gain, bias)[0]
+
+
+def layer_norm_came(came, below, gain, bias):
+    out = jax.ShapeDtypeStruct(came.shape, jnp.bfloat16)
+    kernel = functools.partial(norm_came_kernel, below=below)
+    return call(kernel, [out], [], 20 * came.size, came, gain, bias)[0]
+
+
+def attend(index, members, whole, query, slots, latent_count, ring):
+    width_in = members[0].shape[1]
+    rows = members[0].shape[0] - latent_count
     quarter = query.shape[1] // 4
     sharers = whole.shape[0]
     part = width_in // ring // sharers
@@ -271,13 +296,15 @@
         functools.partial(main_kernel, slots, latent_count, ring, sharers),
         [latents, latents, jax.ShapeDtypeStruct((sharers, ring, packed), jnp.bfloat16)],
         [
+            pltpu.VMEM((4,) + members[0].shape, jnp.bfloat16),
+            pltpu.SemaphoreType.DMA((4,)),
             pltpu.VMEM((width_in, 4 * LANES), jnp.bfloat16),
-            pltpu.VMEM((4 * rows, 2 * LANES), jnp.bfloat16),
+            pltpu.VMEM((4 * rows, quarter), jnp.bfloat16),
             pltpu.VMEM((width_in, LANES), jnp.float32),
             pltpu.VMEM((width_in, LANES), jnp.float32),
         ],
         2 * 4 * rows * width_in * 5 * quarter,
-        index, near, far, whole, query,
+        index, *members, whole, query, unplaced=(1, 2, 3, 4), limit=56,
     )
 
 
@@ -300,68 +327,74 @@
     slots, capacity, width_in = patches.shape[2:]
     latent_count, width = cotangent.shape[3:]
     depth = input_weight.shape[0]
-    ring = lax.axis_size("z")
+    ring = lax.axis_size(RING)
     sharers = lax.axis_size(PLANE)
-    xp, xi, y, c = (lax.axis_index(a) for a in DP)
-    pair = 2 * xi + c
+    x, y, c = (lax.axis_index(a) for a in DP)
+    near_z = lax.axis_index("zl")
+    pair = 2 * near_z + c
     quarter = width // 4
 
     images = patches.reshape(slots * capacity, width_in)
     grads = cotangent.reshape(slots * latent_count, width)
-    send, keep = pack(xi.astype(jnp.int32).reshape(1), counts.reshape(slots), images, grads)
-    came = lax.ppermute(send, "xi", SWAP)
+    send, keep = pack(near_z.astype(jnp.int32).reshape(1), counts.reshape(slots), images, grads)
+    came = lax.ppermute(send, "zl", SWAP)
 
     piece = quarter // 4
-    rows = lax.dynamic_slice_in_dim(input_weight, xp * (depth // 2), depth // 2, 0)
-    target = jnp.arange(LANES, dtype=jnp.int32)
-    source = width * (target // piece) + quarter * pair + piece * y + target % piece
-    source = jnp.where(target < 3 * piece, source, -1)
+    strip = depth // 4
+    rows = lax.dynamic_slice_in_dim(input_weight, x * strip, strip, 0)
+    target = jnp.arange(2 * LANES, dtype=jnp.int32)
+    column = 3 * piece * y + target % LANES
+    source = width * (column // quarter) + quarter * (2 * (target // LANES) + c) + column % quarter
+    source = jnp.where(target % LANES < 3 * piece, source, -1)
     pick = (jnp.arange(3 * width, dtype=jnp.int32)[:, None] == source[None, :]).astype(jnp.bfloat16)
     own = jnp.dot(rows, pick, preferred_element_type=jnp.float32).astype(jnp.bfloat16)
-    gathered = exchange(copies(own, ring), "z")
-
-    normed = layer_norm(images, keep, came, norm_gain, norm_bias)
-    normed_c = lax.ppermute(normed, "c", SWAP)
-    gathered, _ = lax.optimization_barrier((gathered, normed))
+    own = jnp.pad(jnp.stack([own[:, :LANES], own[:, LANES:]]), ((0, 0), (0, 4), (0, 0)))
+    pieces = copies(own, ring // 2).reshape(ring, strip + 4, LANES)
+    gathered = exchange(pieces, RING)
+
+    own_rows = layer_norm(images, keep, norm_gain, norm_bias)
+    own_c = lax.ppermute(own_rows, "c", SWAP)
+    came_rows = layer_norm_came(came, keep.shape[0], norm_gain, norm_bias)
+    came_c = lax.ppermute(came_rows, "c", SWAP)
 
     whole = exchange(copies(gathered, sharers), PLANE)
     index = pair.astype(jnp.int32).reshape(1)
     latents, latents_c, packed = attend(
-        index, normed, normed_c, whole, latent_query, slots, latent_count, ring
+        index, (own_rows, came_rows, own_c, came_c), whole, latent_query, slots, latent_count, ring
     )
 
     part = depth // sharers
     came = exchange(packed, PLANE).astype(jnp.float32)
     summed = jnp.sum(came.reshape(sharers, ring, 1, -1), axis=0)
     both = jnp.stack([latents, lax.ppermute(latents_c, "c", SWAP)], axis=1)
-    summed = jnp.sum(exchange(summed, "z"), axis=0)
-    latents_x = lax.ppermute(both[1], "xi", SWAP)
-    done = unpack(exchange(copies(summed, 4 * sharers), DP)[:, 0], part, quarter)
-    grad_value = (
-        done.reshape(2, 2, 4, 2, part, quarter).transpose(0, 2, 4, 1, 3, 5).reshape(depth, width)
-    )
+    summed = exchange(summed, RING)
+    summed = jnp.sum(summed.reshape(ring // 2, 2, -1), axis=0)
+    latents_z = lax.ppermute(both[1], "zl", SWAP)
+    done = unpack(exchange(copies(summed, 2 * sharers), DP), part, quarter)
+    done = done.reshape(4, 4, 2, 2, part, quarter).transpose(0, 1, 4, 3, 2, 5)
+    grad_value = done.reshape(depth, width)
 
     shape = jax.ShapeDtypeStruct((slots * latent_count, width), jnp.float32)
     parts = pltpu.VMEM((4,) + latents.shape[1:], jnp.float32)
-    latents = call(order_kernel, [shape], [parts], both.size, index, both[0], latents_x)[0]
+    latents = call(order_kernel, [shape], [parts], both.size, index, both[0], latents_z)[0]
     return latents.reshape(cotangent.shape), grad_value
 
 
 def solution(mesh):
-    fine = Mesh(mesh.devices.reshape(2, 2, 4, 2, 16), DP + ("z",))
+    fine = Mesh(mesh.devices.reshape(4, 4, 2, 8, 2), DP + RING)
     placed = (
-        P(DP, "z", None, None, None),
-        P(DP, "z", None),
+        P(DP, RING, None, None, None),
+        P(DP, RING, None),
         P(),
         P(),
-        P("z", None),
+        P(RING, None),
         P(),
-        P(DP, "z", None, None, None),
+        P(DP, RING, None, None, None),
     )
     return jax.shard_map(
         on_device,
         mesh=fine,
         in_specs=placed,
-        out_specs=(P(DP, "z", None, None, None), P("z", None)),
+        out_specs=(P(DP, RING, None, None, None), P(RING, None)),
         check_vma=False,
     )

time: 123 us -> 121 us (0.984)
  blocking collectives: 20.7 us -> 0 us
  waiting for transfers between devices: 23.3 us -> 38 us
  starting transfers between devices: 59.4 us -> 61 us
    all_to_all x1 -> x0, blocking collectives: 20.7 us -> none  [exchange(): return lax.all_to_all(array, axes, 0, 0, tiled=True)]
    all_to_all x4 -> x5, waiting for transfers between devices: 23.3 us -> 35.8 us  [exchange(): return lax.all_to_all(array, axes, 0, 0, tiled=True)]
    ppermute x3 -> x4, starting transfers between devices: 10.6 us -> 13.3 us  [the longest x1 4.85 us: on_device(): own_c = lax.ppermute(own_rows, 'c', SWAP)]
    ppermute x1, starting transfers between devices: 7.76 us -> 5.42 us  [on_device(): both = jnp.stack([latents, lax.ppermute(latents_c, 'c', SWAP)], axis=1)]
    ppermute x3 -> x4, waiting for transfers between devices: 0.01 us -> 2.22 us  [the longest x1 2.21 us: on_device(): came_c = lax.ppermute(came_rows, 'c', SWAP)]
    all_to_all x4 -> x5, starting transfers between devices: 41.1 us -> 42.3 us  [exchange(): return lax.all_to_all(array, axes, 0, 0, tiled=True)]
    pallas_call x4 -> x5, Pallas kernels: 12.7 us -> 13.9 us  [call(): pl.pallas_call(kernel, out_shape=outs, in_specs=[pl.BlockSpec(memory_spac...]
  transfers between devices with their start and end apart: 8 -> 10, of which waited for: 4 -> 6; matrix products, arithmetic and copies ran while one was open for 2% -> 3% of each run, Pallas kernels for 2% -> 3%
where the time goes in v5:
time: 121 us
  starting transfers between devices  61 us (50%)
  waiting for transfers between devices  38 us (31%)
  Pallas kernels  13.9 us (11%)
  local copies, waits for them, and re-layouts  5.93 us (5%)
    all_to_all x5, starting transfers between devices, exchange(): return lax.all_to_all(array, axes, 0, 0, tiled=True)  42.3 us
    all_to_all x5, waiting for transfers between devices, exchange(): return lax.all_to_all(array, axes, 0, 0, tiled=True)  35.8 us
    pallas_call x5, Pallas kernels, call(): pl.pallas_call(kernel, out_shape=outs, in_specs=[pl.BlockSpec(memory_spac...  13.9 us
    ppermute x1, starting transfers between devices, on_device(): both = jnp.stack([latents, lax.ppermute(latents_c, 'c', SWAP)], axis=1)  5.42 us
    ppermute x1, starting transfers between devices, on_device(): own_c = lax.ppermute(own_rows, 'c', SWAP)  4.85 us
    ppermute x1, starting transfers between devices, on_device(): latents_z = lax.ppermute(both[1], 'zl', SWAP)  3.27 us
    ppermute x1, starting transfers between devices, on_device(): came = lax.ppermute(send, 'zl', SWAP)  3.26 us
    broadcast_in_dim x3, local copies, waits for them, and re-layouts, copies(): return jnp.broadcast_to(piece[None], (count,) + piece.shape)  2.85 us
  transfers between devices with their start and end apart: 10, of which 6 were waited for; matrix products, arithmetic and copies ran while one was open for 3% of the time, Pallas kernels for 3%

profile of v5, /device:TPU:1, one launch (start us, length us, event | category | flops | bytes accessed | tf_op | source)
XLA Modules:
  0.0 120.7 jit_solution(8971871342294146065)
XLA Ops:
  0.7 0.9 copy-done
  1.6 0.5 fusion.1
  2.1 0.7 broadcast_in_dim.8
  2.8 15.7 %all-to-all-start = ((bf16[16,24,128]{2,1,0:T(8,128)(2,1)}), bf16[16,24,128]{2,1,0:T(8,128)(2,1)S(1)}, u32[]{:S(2)}, u32[]{:S(2)}) async-start(bf16[16,24,128]{2,1,0:T(8,128)(2,1)} %bitcast.7), calls=%async_computation | async-start | bytes 196608 | tf_op jit(solution)/shard_map/all_to_all | solution.py:316
  18.5 2.2 %shard_map.86 = (bf16[304,1280]{1,0:T(8,128)(2,1)}, bf16[64,1280]{1,0:T(8,128)(2,1)}) custom-call(s32[1]{0:T(128)} %bitcast.2.place_ref, s32[3]{0:T(128)} %bitcast.29, bf16[240,1280]{1,0:T(8,128)(2,1)} %bitcast.23, bf16[192,640]{1,0:T(8,128)(2,1)} %bitcast.28), custom_call_target="tpu_custom_call" | custom-call | flops 307200 | bytes 1802256 | tf_op jit(solution)/shard_map/pallas_call | solution.py:255
  20.7 3.3 %collective-permute-start = (bf16[304,1280]{1,0:T(8,128)(2,1)}, bf16[304,1280]{1,0:T(8,128)(2,1)S(1)}, u32[]{:S(2)}, u32[]{:S(2)}) collective-permute-start(bf16[304,1280]{1,0:T(8,128)(2,1)} %get-tuple-element.8), channel_id=1, source_target_pairs={{0,1},{1,0},{2,3},{3,2},{4,5},{5,4},{6,7},{7,6},{8,9},{9,8},{10,11... | collective-permute-start | bytes 2334728 | tf_op jit(solution)/shard_map/ppermute | solution.py:340
  23.9 6.4 %all-to-all-done = bf16[16,24,128]{2,1,0:T(8,128)(2,1)S(1)} async-done(((bf16[16,24,128]{2,1,0:T(8,128)(2,1)}), bf16[16,24,128]{2,1,0:T(8,128)(2,1)S(1)}, u32[]{:S(2)}, u32[]{:S(2)}) %all-to-all-start) | async-done | bytes 98336 | tf_op jit(solution)/shard_map/all_to_all | solution.py:316
  30.4 1.4 %broadcast_in_dim.9 = bf16[16,16,24,128]{3,2,1,0:T(8,128)(2,1)} broadcast(bf16[16,24,128]{2,1,0:T(8,128)(2,1)S(1)} %all-to-all-done), dimensions={1,2,3} | broadcast | bytes 1671168 | tf_op jit(solution)/shard_map/broadcast_in_dim | solution.py:312
  31.8 6.9 %all-to-all-start.1 = ((bf16[16,16,24,128]{3,2,1,0:T(8,128)(2,1)}), bf16[16,16,24,128]{3,2,1,0:T(8,128)(2,1)}, u32[]{:S(2)}, u32[]{:S(2)}) async-start(bf16[16,16,24,128]{3,2,1,0:T(8,128)(2,1)} %broadcast_in_dim.9), calls=%async_computation.1 | async-start | bytes 3145728 | tf_op jit(solution)/shard_map/all_to_all | solution.py:316
  38.8 0.4 shard_map.87.own_ref
  39.3 4.8 %collective-permute-start.1 = (bf16[304,1280]{1,0:T(8,128)(2,1)S(1)}, bf16[304,1280]{1,0:T(8,128)(2,1)S(1)}, u32[]{:S(2)}, u32[]{:S(2)}) collective-permute-start(bf16[304,1280]{1,0:T(8,128)(2,1)S(1)} %shard_map.87.own_ref), channel_id=1, source_target_pairs={{0,16},{16,0},{1,17},{17,1},{2,18},{18,2},{3,19},{19,3},{4,20},{20... | collective-permute-start | bytes 2334728 | tf_op jit(solution)/shard_map/ppermute | solution.py:356
  44.1 0.4 shard_map.88.partner_ref
  44.6 1.9 %collective-permute-start.2 = (bf16[304,1280]{1,0:T(8,128)(2,1)S(1)}, bf16[304,1280]{1,0:T(8,128)(2,1)S(1)}, u32[]{:S(2)}, u32[]{:S(2)}) collective-permute-start(bf16[304,1280]{1,0:T(8,128)(2,1)S(1)} %shard_map.88.partner_ref), channel_id=1, source_target_pairs={{0,16},{16,0},{1,17},{17,1},{2,18},{18,2},{3,19},{19,3},{4,20},{20... | collective-permute-start | bytes 2334728 | tf_op jit(solution)/shard_map/ppermute | solution.py:358
  46.6 2.2 %collective-permute-done.2.partner_c_ref = bf16[304,1280]{1,0:T(8,128)(2,1)S(1)} collective-permute-done((bf16[304,1280]{1,0:T(8,128)(2,1)S(1)}, bf16[304,1280]{1,0:T(8,128)(2,1)S(1)}, u32[]{:S(2)}, u32[]{:S(2)}) %collective-permute-start.2) | collective-permute-done | bytes 778272 | tf_op jit(solution)/shard_map/ppermute | solution.py:358
  48.8 9.9 %all-to-all-done.1.whole_ref = bf16[16,16,24,128]{3,2,1,0:T(8,128)(2,1)} async-done(((bf16[16,16,24,128]{3,2,1,0:T(8,128)(2,1)}), bf16[16,16,24,128]{3,2,1,0:T(8,128)(2,1)}, u32[]{:S(2)}, u32[]{:S(2)}) %all-to-all-start.1) | async-done | bytes 1572896 | tf_op jit(solution)/shard_map/all_to_all | solution.py:316
  58.7 9.8 %shard_map.89 = (f32[2,192,160]{2,1,0:T(8,128)}, f32[2,192,160]{2,1,0:T(8,128)}, bf16[16,16,896]{2,1,0:T(8,128)(2,1)}) custom-call(s32[1]{0:T(128)} %bitcast.indepartner_ref, bf16[304,1280]{1,0:T(8,128)(2,1)} %copy-done.2, bf16[304,1280]{1,0:T(8,128)(2,1)} %copy-done.3, bf16[304,1280]{1,0:T(8,128)(2,1)} %copy-done.8, bf16[304,1280]{1,0:T(8,128)(2,1)} %copy-done.9, ...), custom_call_target="tpu_custom_call" | custom-call | flops 1966080000 | bytes 5718020 | tf_op jit(solution)/shard_map/pallas_call | solution.py:255
  68.5 4.8 %all-to-all-start.2 = ((bf16[16,16,896]{2,1,0:T(8,128)(2,1)}), bf16[16,16,896]{2,1,0:T(8,128)(2,1)S(1)}, u32[]{:S(2)}, u32[]{:S(2)}) async-start(bf16[16,16,896]{2,1,0:T(8,128)(2,1)} %get-tuple-element.11), calls=%async_computation.2 | async-start | bytes 917504 | tf_op jit(solution)/shard_map/all_to_all | solution.py:316
  73.3 5.4 %collective-permute-start.3 = (f32[2,192,160]{2,1,0:T(8,128)}, f32[2,192,160]{2,1,0:T(8,128)S(1)}, u32[]{:S(2)}, u32[]{:S(2)}) collective-permute-start(f32[2,192,160]{2,1,0:T(8,128)} %get-tuple-element.10), channel_id=1, source_target_pairs={{0,16},{16,0},{1,17},{17,1},{2,18},{18,2},{3,19},{19,3},{4,20},{20... | collective-permute-start | bytes 737288 | tf_op jit(solution)/shard_map/ppermute | solution.py:369
  78.7 3.3 %all-to-all-done.2 = bf16[16,16,896]{2,1,0:T(8,128)(2,1)S(1)} async-done(((bf16[16,16,896]{2,1,0:T(8,128)(2,1)}), bf16[16,16,896]{2,1,0:T(8,128)(2,1)S(1)}, u32[]{:S(2)}, u32[]{:S(2)}) %all-to-all-start.2) | async-done | bytes 458784 | tf_op jit(solution)/shard_map/all_to_all | solution.py:316
  82.0 0.1 convert_reduce_fusion
  82.1 0.7 reduce_sum.21
  82.8 5.1 %all-to-all-start.3 = ((f32[16,1,896]{2,1,0:T(1,128)}), f32[16,1,896]{2,1,0:T(1,128)S(1)}, u32[]{:S(2)}, u32[]{:S(2)}) async-start(f32[16,1,896]{2,1,0:T(1,128)} %reduce_sum.21), calls=%async_computation.3 | async-start | bytes 114688 | tf_op jit(solution)/shard_map/all_to_all | solution.py:316
  87.9 3.3 %collective-permute-start.4 = (f32[2,192,160]{2,1,0:T(8,128)S(1)}, f32[2,192,160]{2,1,0:T(8,128)S(1)}, u32[]{:S(2)}, u32[]{:S(2)}) collective-permute-start(f32[2,192,160]{2,1,0:T(8,128)S(1)} %get-tuple-element.12), channel_id=1, source_target_pairs={{0,1},{1,0},{2,3},{3,2},{4,5},{5,4},{6,7},{7,6},{8,9},{9,8},{10,11... | collective-permute-start | bytes 737288 | tf_op jit(solution)/shard_map/ppermute | solution.py:372
  91.2 8.5 %all-to-all-done.3 = f32[16,1,896]{2,1,0:T(1,128)S(1)} async-done(((f32[16,1,896]{2,1,0:T(1,128)}), f32[16,1,896]{2,1,0:T(1,128)S(1)}, u32[]{:S(2)}, u32[]{:S(2)}) %all-to-all-start.3) | async-done | bytes 57376 | tf_op jit(solution)/shard_map/all_to_all | solution.py:316
  99.7 0.1 reduce.2
  99.9 0.7 broadcast_in_dim.10
  100.6 9.8 %all-to-all-start.4 = ((f32[32,2,896]{2,1,0:T(2,128)}), f32[32,2,896]{2,1,0:T(2,128)S(1)}, u32[]{:S(2)}, u32[]{:S(2)}) async-start(f32[32,2,896]{2,1,0:T(2,128)} %broadcast_in_dim.10), calls=%async_computation.4 | async-start | bytes 458752 | tf_op jit(solution)/shard_map/all_to_all | solution.py:316
  110.4 1.1 shard_map.90
  111.5 7.7 %all-to-all-done.4 = f32[32,2,896]{2,1,0:T(2,128)S(1)} async-done(((f32[32,2,896]{2,1,0:T(2,128)}), f32[32,2,896]{2,1,0:T(2,128)S(1)}, u32[]{:S(2)}, u32[]{:S(2)}) %all-to-all-start.4) | async-done | bytes 229408 | tf_op jit(solution)/shard_map/all_to_all | solution.py:316
  119.3 0.1 concatenate.9
  119.4 0.2 copy.12
  119.6 1.1 reshape.92
  (35 shorter events, 0.4 us)
Async XLA Ops:
  0.6 1.0 copy-start
  2.8 27.6 %all-to-all-start = ((bf16[16,24,128]{2,1,0:T(8,128)(2,1)}), bf16[16,24,128]{2,1,0:T(8,128)(2,1)S(1)}, u32[]{:S(2)}, u32[]{:S(2)}) async-start(bf16[16,24,128]{2,1,0:T(8,128)(2,1)} %bitcast.7), calls=%async_computation | async-start | bytes 196608 | tf_op jit(solution)/shard_map/all_to_all | solution.py:316
  20.7 23.5 %collective-permute-start = (bf16[304,1280]{1,0:T(8,128)(2,1)}, bf16[304,1280]{1,0:T(8,128)(2,1)S(1)}, u32[]{:S(2)}, u32[]{:S(2)}) collective-permute-start(bf16[304,1280]{1,0:T(8,128)(2,1)} %get-tuple-element.8), channel_id=1, source_target_pairs={{0,1},{1,0},{2,3},{3,2},{4,5},{5,4},{6,7},{7,6},{8,9},{9,8},{10,11... | collective-permute-start | bytes 2334728 | tf_op jit(solution)/shard_map/ppermute | solution.py:340
  31.8 7.0 %copy-start.1 = (bf16[1,1,3,80,1280]{4,3,2,1,0:T(8,128)(2,1)S(1)}, bf16[1,1,3,80,1280]{4,3,2,1,0:T(8,128)(2,1)}, u32[]{:S(2)}) copy-start(bf16[1,1,3,80,1280]{4,3,2,1,0:T(8,128)(2,1)} %param.7) | copy-start | bytes 1843204
  31.8 7.0 %copy-start.4 = (bf16[64,1280]{1,0:T(8,128)(2,1)S(1)}, bf16[64,1280]{1,0:T(8,128)(2,1)}, u32[]{:S(2)}) copy-start(bf16[64,1280]{1,0:T(8,128)(2,1)} %get-tuple-element.7.below_ref) | copy-start | bytes 491524
  31.8 7.0 %copy-start.5 = (f32[1280]{0:T(1024)S(1)}, f32[1280]{0:T(1024)}, u32[]{:S(2)}) copy-start(f32[1280]{0:T(1024)} %gain_ref.3) | copy-start | bytes 15364
  31.8 7.0 %copy-start.6 = (f32[1280]{0:T(1024)S(1)}, f32[1280]{0:T(1024)}, u32[]{:S(2)}) copy-start(f32[1280]{0:T(1024)} %bias_ref.3) | copy-start | bytes 15364
  31.8 26.9 %all-to-all-start.1 = ((bf16[16,16,24,128]{3,2,1,0:T(8,128)(2,1)}), bf16[16,16,24,128]{3,2,1,0:T(8,128)(2,1)}, u32[]{:S(2)}, u32[]{:S(2)}) async-start(bf16[16,16,24,128]{3,2,1,0:T(8,128)(2,1)} %broadcast_in_dim.9), calls=%async_computation.1 | async-start | bytes 3145728 | tf_op jit(solution)/shard_map/all_to_all | solution.py:316
  39.3 19.5 %copy-start.2 = (bf16[304,1280]{1,0:T(8,128)(2,1)}, bf16[304,1280]{1,0:T(8,128)(2,1)S(1)}, u32[]{:S(2)}) copy-start(bf16[304,1280]{1,0:T(8,128)(2,1)S(1)} %shard_map.87.own_ref) | copy-start | bytes 2334724
  39.3 7.3 %collective-permute-start.1 = (bf16[304,1280]{1,0:T(8,128)(2,1)S(1)}, bf16[304,1280]{1,0:T(8,128)(2,1)S(1)}, u32[]{:S(2)}, u32[]{:S(2)}) collective-permute-start(bf16[304,1280]{1,0:T(8,128)(2,1)S(1)} %shard_map.87.own_ref), channel_id=1, source_target_pairs={{0,16},{16,0},{1,17},{17,1},{2,18},{18,2},{3,19},{19,3},{4,20},{20... | collective-permute-start | bytes 2334728 | tf_op jit(solution)/shard_map/ppermute | solution.py:356
  44.6 14.1 %copy-start.3 = (bf16[304,1280]{1,0:T(8,128)(2,1)}, bf16[304,1280]{1,0:T(8,128)(2,1)S(1)}, u32[]{:S(2)}) copy-start(bf16[304,1280]{1,0:T(8,128)(2,1)S(1)} %shard_map.88.partner_ref) | copy-start | bytes 2334724
  44.6 4.2 %collective-permute-start.2 = (bf16[304,1280]{1,0:T(8,128)(2,1)S(1)}, bf16[304,1280]{1,0:T(8,128)(2,1)S(1)}, u32[]{:S(2)}, u32[]{:S(2)}) collective-permute-start(bf16[304,1280]{1,0:T(8,128)(2,1)S(1)} %shard_map.88.partner_ref), channel_id=1, source_target_pairs={{0,16},{16,0},{1,17},{17,1},{2,18},{18,2},{3,19},{19,3},{4,20},{20... | collective-permute-start | bytes 2334728 | tf_op jit(solution)/shard_map/ppermute | solution.py:358
  46.6 12.2 %copy-start.8 = (bf16[304,1280]{1,0:T(8,128)(2,1)}, bf16[304,1280]{1,0:T(8,128)(2,1)S(1)}, u32[]{:S(2)}) copy-start(bf16[304,1280]{1,0:T(8,128)(2,1)S(1)} %collective-permute-done.1.own_c_ref) | copy-start | bytes 2334724
  48.8 10.0 %copy-start.9 = (bf16[304,1280]{1,0:T(8,128)(2,1)}, bf16[304,1280]{1,0:T(8,128)(2,1)S(1)}, u32[]{:S(2)}) copy-start(bf16[304,1280]{1,0:T(8,128)(2,1)S(1)} %collective-permute-done.2.partner_c_ref) | copy-start | bytes 2334724
  68.5 19.3 %copy-start.7 = (f32[2,192,160]{2,1,0:T(8,128)S(1)}, f32[2,192,160]{2,1,0:T(8,128)}, u32[]{:S(2)}) copy-start(f32[2,192,160]{2,1,0:T(8,128)} %get-tuple-element.9) | copy-start | bytes 737284
  68.5 13.5 %all-to-all-start.2 = ((bf16[16,16,896]{2,1,0:T(8,128)(2,1)}), bf16[16,16,896]{2,1,0:T(8,128)(2,1)S(1)}, u32[]{:S(2)}, u32[]{:S(2)}) async-start(bf16[16,16,896]{2,1,0:T(8,128)(2,1)} %get-tuple-element.11), calls=%async_computation.2 | async-start | bytes 917504 | tf_op jit(solution)/shard_map/all_to_all | solution.py:316
  73.3 14.5 %collective-permute-start.3 = (f32[2,192,160]{2,1,0:T(8,128)}, f32[2,192,160]{2,1,0:T(8,128)S(1)}, u32[]{:S(2)}, u32[]{:S(2)}) collective-permute-start(f32[2,192,160]{2,1,0:T(8,128)} %get-tuple-element.10), channel_id=1, source_target_pairs={{0,16},{16,0},{1,17},{17,1},{2,18},{18,2},{3,19},{19,3},{4,20},{20... | collective-permute-start | bytes 737288 | tf_op jit(solution)/shard_map/ppermute | solution.py:369
  82.8 16.9 %all-to-all-start.3 = ((f32[16,1,896]{2,1,0:T(1,128)}), f32[16,1,896]{2,1,0:T(1,128)S(1)}, u32[]{:S(2)}, u32[]{:S(2)}) async-start(f32[16,1,896]{2,1,0:T(1,128)} %reduce_sum.21), calls=%async_computation.3 | async-start | bytes 114688 | tf_op jit(solution)/shard_map/all_to_all | solution.py:316
  87.9 22.5 %collective-permute-start.4 = (f32[2,192,160]{2,1,0:T(8,128)S(1)}, f32[2,192,160]{2,1,0:T(8,128)S(1)}, u32[]{:S(2)}, u32[]{:S(2)}) collective-permute-start(f32[2,192,160]{2,1,0:T(8,128)S(1)} %get-tuple-element.12), channel_id=1, source_target_pairs={{0,1},{1,0},{2,3},{3,2},{4,5},{5,4},{6,7},{7,6},{8,9},{9,8},{10,11... | collective-permute-start | bytes 737288 | tf_op jit(solution)/shard_map/ppermute | solution.py:372
  100.6 18.5 %all-to-all-start.4 = ((f32[32,2,896]{2,1,0:T(2,128)}), f32[32,2,896]{2,1,0:T(2,128)S(1)}, u32[]{:S(2)}, u32[]{:S(2)}) async-start(f32[32,2,896]{2,1,0:T(2,128)} %broadcast_in_dim.10), calls=%async_computation.4 | async-start | bytes 458752 | tf_op jit(solution)/shard_map/all_to_all | solution.py:316

commit v6 on v5

--- a/solution.py
+++ b/solution.py
@@ -54,6 +54,29 @@
 def norm_came_kernel(came_ref, gain_ref, bias_ref, out_ref, *, below):
     rows = out_ref.shape[0] - below
     norm_kernel(came_ref.at[:rows], came_ref.at[rows:], gain_ref, bias_ref, out_ref)
+
+
+def spread_kernel(in_ref, out_ref, flat_ref):
+    ring = in_ref.shape[0]
+    strip = flat_ref.shape[0] // ring
+    for step in range(ring):
+        flat_ref[strip * step : strip * (step + 1), :] = in_ref[step].astype(jnp.float32)[:strip]
+    flat = flat_ref[...].astype(jnp.bfloat16)
+    for receiver in range(out_ref.shape[0]):
+        out_ref[receiver] = flat
+
+
+def plane_sum_kernel(in_ref, out_ref):
+    total = sum(in_ref[n].astype(jnp.float32) for n in range(in_ref.shape[0]))
+    for step in range(out_ref.shape[0]):
+        out_ref[step] = total[step : step + 1, :]
+
+
+def ring_sum_kernel(in_ref, out_ref):
+    kinds = [sum(in_ref[n] for n in range(kind, in_ref.shape[0], 2)) for kind in range(2)]
+    pair = jnp.concatenate(kinds, axis=0)
+    for receiver in range(out_ref.shape[0]):
+        out_ref[receiver] = pair
 
 
 def across(left, right):
@@ -109,7 +132,7 @@
             strips = whole_ref[4 * part + block].astype(jnp.float32)
             for step in range(ring):
                 start = strip * (4 * step + part)
-                total_ref[start : start + strip, :] = strips[step, :strip]
+                total_ref[start : start + strip, :] = strips[strip * step : strip * (step + 1)]
         weight_ref[:, LANES * block : LANES * (block + 1)] = total_ref[...].astype(jnp.bfloat16)
     first_head = iota((1, quarter), 1) < head_size
     nothing = jnp.zeros((), jnp.bfloat16)
@@ -357,20 +380,24 @@
     came_rows = layer_norm_came(came, keep.shape[0], norm_gain, norm_bias)
     came_c = lax.ppermute(came_rows, "c", SWAP)
 
-    whole = exchange(copies(gathered, sharers), PLANE)
+    shape = jax.ShapeDtypeStruct((sharers, ring * strip, LANES), jnp.bfloat16)
+    flat = pltpu.VMEM(shape.shape[1:], jnp.float32)
+    whole = exchange(call(spread_kernel, [shape], [flat], gathered.size, gathered)[0], PLANE)
     index = pair.astype(jnp.int32).reshape(1)
     latents, latents_c, packed = attend(
         index, (own_rows, came_rows, own_c, came_c), whole, latent_query, slots, latent_count, ring
     )
 
     part = depth // sharers
-    came = exchange(packed, PLANE).astype(jnp.float32)
-    summed = jnp.sum(came.reshape(sharers, ring, 1, -1), axis=0)
+    came = exchange(packed, PLANE)
+    shape = jax.ShapeDtypeStruct((ring, 1, packed.shape[2]), jnp.float32)
+    summed = call(plane_sum_kernel, [shape], [], came.size, came)[0]
     both = jnp.stack([latents, lax.ppermute(latents_c, "c", SWAP)], axis=1)
     summed = exchange(summed, RING)
-    summed = jnp.sum(summed.reshape(ring // 2, 2, -1), axis=0)
+    shape = jax.ShapeDtypeStruct((2 * sharers, 2, packed.shape[2]), jnp.float32)
+    summed = call(ring_sum_kernel, [shape], [], summed.size, summed)[0]
     latents_z = lax.ppermute(both[1], "zl", SWAP)
-    done = unpack(exchange(copies(summed, 2 * sharers), DP), part, quarter)
+    done = unpack(exchange(summed, DP), part, quarter)
     done = done.reshape(4, 4, 2, 2, part, quarter).transpose(0, 1, 4, 3, 2, 5)
     grad_value = done.reshape(depth, width)
 

time: 121 us -> 118 us (0.975)
  local copies, waits for them, and re-layouts: 5.93 us -> 3.04 us
  Pallas kernels: 13.9 us -> 16.4 us
  waiting for transfers between devices: 38 us -> 35.9 us
    pallas_call x5 -> x8, Pallas kernels: 13.9 us -> 16.4 us  [call(): pl.pallas_call(kernel, out_shape=outs, in_specs=[pl.BlockSpec(memory_spac...]
    broadcast_in_dim x3 -> x1, local copies, waits for them, and re-layouts: 2.85 us -> 0.66 us  [copies(): return jnp.broadcast_to(piece[None], (count,) + piece.shape)]
    all_to_all x5, waiting for transfers between devices: 35.8 us -> 33.8 us  [exchange(): return lax.all_to_all(array, axes, 0, 0, tiled=True)]
  transfers between devices with their start and end apart: 10 -> 10, of which waited for: 6 -> 6; matrix products, arithmetic and copies ran while one was open for 3% -> 0% of each run, Pallas kernels for 3% -> 6%
where the time goes in v6:
time: 118 us; the launch traced here: 117 us
  starting transfers between devices  60.1 us (51%)
  waiting for transfers between devices  35.9 us (30%)
  Pallas kernels  16.4 us (14%)
  local copies, waits for them, and re-layouts  3.04 us (3%)
    all_to_all x5, starting transfers between devices, exchange(): return lax.all_to_all(array, axes, 0, 0, tiled=True)  42.4 us
    all_to_all x5, waiting for transfers between devices, exchange(): return lax.all_to_all(array, axes, 0, 0, tiled=True)  33.8 us
    pallas_call x8, Pallas kernels, call(): pl.pallas_call(kernel, out_shape=outs, in_specs=[pl.BlockSpec(memory_spac...  16.4 us
    ppermute x1, starting transfers between devices, on_device(): own_c = lax.ppermute(own_rows, 'c', SWAP)  4.85 us
    ppermute x1, starting transfers between devices, on_device(): both = jnp.stack([latents, lax.ppermute(latents_c, 'c', SWAP)], axis=1)  4.32 us
    ppermute x1, starting transfers between devices, on_device(): latents_z = lax.ppermute(both[1], 'zl', SWAP)  3.27 us
    ppermute x1, starting transfers between devices, on_device(): came = lax.ppermute(send, 'zl', SWAP)  3.26 us
  transfers between devices with their start and end apart: 10, of which 6 were waited for; matrix products, arithmetic and copies ran while one was open for 0% of the time, Pallas kernels for 6%

profile of v6, /device:TPU:1, one launch (start us, length us, event | category | flops | bytes accessed | tf_op | source)
XLA Modules:
  0.0 117.0 jit_solution(6288641809076645354)
XLA Ops:
  0.7 0.9 copy-done
  1.6 0.5 fusion.1
  2.1 0.7 broadcast_in_dim.4
  2.8 15.7 %all-to-all-start = ((bf16[16,24,128]{2,1,0:T(8,128)(2,1)}), bf16[16,24,128]{2,1,0:T(8,128)(2,1)S(1)}, u32[]{:S(2)}, u32[]{:S(2)}) async-start(bf16[16,24,128]{2,1,0:T(8,128)(2,1)} %bitcast.7), calls=%async_computation | async-start | bytes 196608 | tf_op jit(solution)/shard_map/all_to_all | solution.py:339
  18.5 2.2 %shard_map.86 = (bf16[304,1280]{1,0:T(8,128)(2,1)}, bf16[64,1280]{1,0:T(8,128)(2,1)}) custom-call(s32[1]{0:T(128)} %bitcast.2.place_ref, s32[3]{0:T(128)} %bitcast.29, bf16[240,1280]{1,0:T(8,128)(2,1)} %bitcast.23, bf16[192,640]{1,0:T(8,128)(2,1)} %bitcast.28), custom_call_target="tpu_custom_call" | custom-call | flops 307200 | bytes 1802256 | tf_op jit(solution)/shard_map/pallas_call | solution.py:278
  20.7 3.3 %collective-permute-start = (bf16[304,1280]{1,0:T(8,128)(2,1)}, bf16[304,1280]{1,0:T(8,128)(2,1)S(1)}, u32[]{:S(2)}, u32[]{:S(2)}) collective-permute-start(bf16[304,1280]{1,0:T(8,128)(2,1)} %get-tuple-element.8), channel_id=1, source_target_pairs={{0,1},{1,0},{2,3},{3,2},{4,5},{5,4},{6,7},{7,6},{8,9},{9,8},{10,11... | collective-permute-start | bytes 2334728 | tf_op jit(solution)/shard_map/ppermute | solution.py:363
  23.9 6.4 %all-to-all-done.in_ref = bf16[16,24,128]{2,1,0:T(8,128)(2,1)S(1)} async-done(((bf16[16,24,128]{2,1,0:T(8,128)(2,1)}), bf16[16,24,128]{2,1,0:T(8,128)(2,1)S(1)}, u32[]{:S(2)}, u32[]{:S(2)}) %all-to-all-start) | async-done | bytes 98336 | tf_op jit(solution)/shard_map/all_to_all | solution.py:339
  30.4 1.2 shard_map.89
  31.5 6.9 %all-to-all-start.1 = ((bf16[16,320,128]{2,1,0:T(8,128)(2,1)}), bf16[16,320,128]{2,1,0:T(8,128)(2,1)}, u32[]{:S(2)}, u32[]{:S(2)}) async-start(bf16[16,320,128]{2,1,0:T(8,128)(2,1)} %shard_map.89), calls=%async_computation.1 | async-start | bytes 2621440 | tf_op jit(solution)/shard_map/all_to_all | solution.py:339
  38.5 0.4 shard_map.87.own_ref
  39.0 4.8 %collective-permute-start.1 = (bf16[304,1280]{1,0:T(8,128)(2,1)S(1)}, bf16[304,1280]{1,0:T(8,128)(2,1)S(1)}, u32[]{:S(2)}, u32[]{:S(2)}) collective-permute-start(bf16[304,1280]{1,0:T(8,128)(2,1)S(1)} %shard_map.87.own_ref), channel_id=1, source_target_pairs={{0,16},{16,0},{1,17},{17,1},{2,18},{18,2},{3,19},{19,3},{4,20},{20... | collective-permute-start | bytes 2334728 | tf_op jit(solution)/shard_map/ppermute | solution.py:379
  43.9 0.4 shard_map.88.partner_ref
  44.3 2.0 %collective-permute-start.2 = (bf16[304,1280]{1,0:T(8,128)(2,1)S(1)}, bf16[304,1280]{1,0:T(8,128)(2,1)S(1)}, u32[]{:S(2)}, u32[]{:S(2)}) collective-permute-start(bf16[304,1280]{1,0:T(8,128)(2,1)S(1)} %shard_map.88.partner_ref), channel_id=1, source_target_pairs={{0,16},{16,0},{1,17},{17,1},{2,18},{18,2},{3,19},{19,3},{4,20},{20... | collective-permute-start | bytes 2334728 | tf_op jit(solution)/shard_map/ppermute | solution.py:381
  46.4 2.1 %collective-permute-done.2.partner_c_ref = bf16[304,1280]{1,0:T(8,128)(2,1)S(1)} collective-permute-done((bf16[304,1280]{1,0:T(8,128)(2,1)S(1)}, bf16[304,1280]{1,0:T(8,128)(2,1)S(1)}, u32[]{:S(2)}, u32[]{:S(2)}) %collective-permute-start.2) | collective-permute-done | bytes 778272 | tf_op jit(solution)/shard_map/ppermute | solution.py:381
  48.5 6.8 %all-to-all-done.1.whole_ref = bf16[16,320,128]{2,1,0:T(8,128)(2,1)} async-done(((bf16[16,320,128]{2,1,0:T(8,128)(2,1)}), bf16[16,320,128]{2,1,0:T(8,128)(2,1)}, u32[]{:S(2)}, u32[]{:S(2)}) %all-to-all-start.1) | async-done | bytes 1310752 | tf_op jit(solution)/shard_map/all_to_all | solution.py:339
  55.3 9.7 %shard_map.90 = (f32[2,192,160]{2,1,0:T(8,128)}, f32[2,192,160]{2,1,0:T(8,128)}, bf16[16,16,896]{2,1,0:T(8,128)(2,1)}) custom-call(s32[1]{0:T(128)} %bitcast.indepartner_ref, bf16[304,1280]{1,0:T(8,128)(2,1)} %copy-done.2, bf16[304,1280]{1,0:T(8,128)(2,1)} %copy-done.3, bf16[304,1280]{1,0:T(8,128)(2,1)} %copy-done.8, bf16[304,1280]{1,0:T(8,128)(2,1)} %copy-done.9, ...), custom_call_target="tpu_custom_call" | custom-call | flops 1966080000 | bytes 5455876 | tf_op jit(solution)/shard_map/pallas_call | solution.py:278
  65.0 5.7 %all-to-all-start.2 = ((bf16[16,16,896]{2,1,0:T(8,128)(2,1)}), bf16[16,16,896]{2,1,0:T(8,128)(2,1)S(1)}, u32[]{:S(2)}, u32[]{:S(2)}) async-start(bf16[16,16,896]{2,1,0:T(8,128)(2,1)} %get-tuple-element.11), calls=%async_computation.2 | async-start | bytes 917504 | tf_op jit(solution)/shard_map/all_to_all | solution.py:339
  70.8 4.3 %collective-permute-start.3 = (f32[2,192,160]{2,1,0:T(8,128)}, f32[2,192,160]{2,1,0:T(8,128)S(1)}, u32[]{:S(2)}, u32[]{:S(2)}) collective-permute-start(f32[2,192,160]{2,1,0:T(8,128)} %get-tuple-element.10), channel_id=1, source_target_pairs={{0,16},{16,0},{1,17},{17,1},{2,18},{18,2},{3,19},{19,3},{4,20},{20... | collective-permute-start | bytes 737288 | tf_op jit(solution)/shard_map/ppermute | solution.py:395
  75.1 4.5 %all-to-all-done.2.in_ref = bf16[16,16,896]{2,1,0:T(8,128)(2,1)S(1)} async-done(((bf16[16,16,896]{2,1,0:T(8,128)(2,1)}), bf16[16,16,896]{2,1,0:T(8,128)(2,1)S(1)}, u32[]{:S(2)}, u32[]{:S(2)}) %all-to-all-start.2) | async-done | bytes 458784 | tf_op jit(solution)/shard_map/all_to_all | solution.py:339
  79.6 0.7 shard_map.92
  80.3 5.0 %all-to-all-start.3 = ((f32[16,1,896]{2,1,0:T(1,128)}), f32[16,1,896]{2,1,0:T(1,128)S(1)}, u32[]{:S(2)}, u32[]{:S(2)}) async-start(f32[16,1,896]{2,1,0:T(1,128)} %shard_map.92), calls=%async_computation.3 | async-start | bytes 114688 | tf_op jit(solution)/shard_map/all_to_all | solution.py:339
  85.3 0.1 fusion.5
  85.3 3.3 %collective-permute-start.4 = (f32[2,192,160]{2,1,0:T(8,128)S(1)}, f32[2,192,160]{2,1,0:T(8,128)S(1)}, u32[]{:S(2)}, u32[]{:S(2)}) collective-permute-start(f32[2,192,160]{2,1,0:T(8,128)S(1)} %get-tuple-element.12), channel_id=1, source_target_pairs={{0,1},{1,0},{2,3},{3,2},{4,5},{5,4},{6,7},{7,6},{8,9},{9,8},{10,11... | collective-permute-start | bytes 737288 | tf_op jit(solution)/shard_map/ppermute | solution.py:399
  88.6 8.4 %all-to-all-done.3.in_ref = f32[16,1,896]{2,1,0:T(1,128)S(1)} async-done(((f32[16,1,896]{2,1,0:T(1,128)}), f32[16,1,896]{2,1,0:T(1,128)S(1)}, u32[]{:S(2)}, u32[]{:S(2)}) %all-to-all-start.3) | async-done | bytes 57376 | tf_op jit(solution)/shard_map/all_to_all | solution.py:339
  97.0 0.7 shard_map.93
  97.7 9.0 %all-to-all-start.4 = ((f32[32,2,896]{2,1,0:T(2,128)}), f32[32,2,896]{2,1,0:T(2,128)S(1)}, u32[]{:S(2)}, u32[]{:S(2)}) async-start(f32[32,2,896]{2,1,0:T(2,128)} %shard_map.93), calls=%async_computation.4 | async-start | bytes 458752 | tf_op jit(solution)/shard_map/all_to_all | solution.py:339
  106.7 1.1 shard_map.91
  107.8 7.7 %all-to-all-done.4 = f32[32,2,896]{2,1,0:T(2,128)S(1)} async-done(((f32[32,2,896]{2,1,0:T(2,128)}), f32[32,2,896]{2,1,0:T(2,128)S(1)}, u32[]{:S(2)}, u32[]{:S(2)}) %all-to-all-start.4) | async-done | bytes 229408 | tf_op jit(solution)/shard_map/all_to_all | solution.py:339
  115.6 0.1 concatenate.9
  115.7 0.1 maximum_bitcast_fusion
  115.7 0.2 copy.14
  115.9 1.1 reshape.84
  (31 shorter events, 0.2 us)
Async XLA Ops:
  0.6 1.0 copy-start
  2.8 27.6 %all-to-all-start = ((bf16[16,24,128]{2,1,0:T(8,128)(2,1)}), bf16[16,24,128]{2,1,0:T(8,128)(2,1)S(1)}, u32[]{:S(2)}, u32[]{:S(2)}) async-start(bf16[16,24,128]{2,1,0:T(8,128)(2,1)} %bitcast.7), calls=%async_computation | async-start | bytes 196608 | tf_op jit(solution)/shard_map/all_to_all | solution.py:339
  20.7 23.2 %collective-permute-start = (bf16[304,1280]{1,0:T(8,128)(2,1)}, bf16[304,1280]{1,0:T(8,128)(2,1)S(1)}, u32[]{:S(2)}, u32[]{:S(2)}) collective-permute-start(bf16[304,1280]{1,0:T(8,128)(2,1)} %get-tuple-element.8), channel_id=1, source_target_pairs={{0,1},{1,0},{2,3},{3,2},{4,5},{5,4},{6,7},{7,6},{8,9},{9,8},{10,11... | collective-permute-start | bytes 2334728 | tf_op jit(solution)/shard_map/ppermute | solution.py:363
  31.5 7.0 %copy-start.1 = (bf16[1,1,3,80,1280]{4,3,2,1,0:T(8,128)(2,1)S(1)}, bf16[1,1,3,80,1280]{4,3,2,1,0:T(8,128)(2,1)}, u32[]{:S(2)}) copy-start(bf16[1,1,3,80,1280]{4,3,2,1,0:T(8,128)(2,1)} %param.7) | copy-start | bytes 1843204
  31.5 7.0 %copy-start.4 = (bf16[64,1280]{1,0:T(8,128)(2,1)S(1)}, bf16[64,1280]{1,0:T(8,128)(2,1)}, u32[]{:S(2)}) copy-start(bf16[64,1280]{1,0:T(8,128)(2,1)} %get-tuple-element.7.below_ref) | copy-start | bytes 491524
  31.5 7.0 %copy-start.5 = (f32[1280]{0:T(1024)S(1)}, f32[1280]{0:T(1024)}, u32[]{:S(2)}) copy-start(f32[1280]{0:T(1024)} %gain_ref.3) | copy-start | bytes 15364
  31.5 7.0 %copy-start.6 = (f32[1280]{0:T(1024)S(1)}, f32[1280]{0:T(1024)}, u32[]{:S(2)}) copy-start(f32[1280]{0:T(1024)} %bias_ref.3) | copy-start | bytes 15364
  31.5 23.8 %all-to-all-start.1 = ((bf16[16,320,128]{2,1,0:T(8,128)(2,1)}), bf16[16,320,128]{2,1,0:T(8,128)(2,1)}, u32[]{:S(2)}, u32[]{:S(2)}) async-start(bf16[16,320,128]{2,1,0:T(8,128)(2,1)} %shard_map.89), calls=%async_computation.1 | async-start | bytes 2621440 | tf_op jit(solution)/shard_map/all_to_all | solution.py:339
  39.0 16.3 %copy-start.2 = (bf16[304,1280]{1,0:T(8,128)(2,1)}, bf16[304,1280]{1,0:T(8,128)(2,1)S(1)}, u32[]{:S(2)}) copy-start(bf16[304,1280]{1,0:T(8,128)(2,1)S(1)} %shard_map.87.own_ref) | copy-start | bytes 2334724
  39.0 7.3 %collective-permute-start.1 = (bf16[304,1280]{1,0:T(8,128)(2,1)S(1)}, bf16[304,1280]{1,0:T(8,128)(2,1)S(1)}, u32[]{:S(2)}, u32[]{:S(2)}) collective-permute-start(bf16[304,1280]{1,0:T(8,128)(2,1)S(1)} %shard_map.87.own_ref), channel_id=1, source_target_pairs={{0,16},{16,0},{1,17},{17,1},{2,18},{18,2},{3,19},{19,3},{4,20},{20... | collective-permute-start | bytes 2334728 | tf_op jit(solution)/shard_map/ppermute | solution.py:379
  44.3 11.0 %copy-start.3 = (bf16[304,1280]{1,0:T(8,128)(2,1)}, bf16[304,1280]{1,0:T(8,128)(2,1)S(1)}, u32[]{:S(2)}) copy-start(bf16[304,1280]{1,0:T(8,128)(2,1)S(1)} %shard_map.88.partner_ref) | copy-start | bytes 2334724
  44.3 4.2 %collective-permute-start.2 = (bf16[304,1280]{1,0:T(8,128)(2,1)S(1)}, bf16[304,1280]{1,0:T(8,128)(2,1)S(1)}, u32[]{:S(2)}, u32[]{:S(2)}) collective-permute-start(bf16[304,1280]{1,0:T(8,128)(2,1)S(1)} %shard_map.88.partner_ref), channel_id=1, source_target_pairs={{0,16},{16,0},{1,17},{17,1},{2,18},{18,2},{3,19},{19,3},{4,20},{20... | collective-permute-start | bytes 2334728 | tf_op jit(solution)/shard_map/ppermute | solution.py:381
  46.3 9.0 %copy-start.8 = (bf16[304,1280]{1,0:T(8,128)(2,1)}, bf16[304,1280]{1,0:T(8,128)(2,1)S(1)}, u32[]{:S(2)}) copy-start(bf16[304,1280]{1,0:T(8,128)(2,1)S(1)} %collective-permute-done.1.own_c_ref) | copy-start | bytes 2334724
  48.5 6.9 %copy-start.9 = (bf16[304,1280]{1,0:T(8,128)(2,1)}, bf16[304,1280]{1,0:T(8,128)(2,1)S(1)}, u32[]{:S(2)}) copy-start(bf16[304,1280]{1,0:T(8,128)(2,1)S(1)} %collective-permute-done.2.partner_c_ref) | copy-start | bytes 2334724
  65.0 20.2 %copy-start.7 = (f32[2,192,160]{2,1,0:T(8,128)S(1)}, f32[2,192,160]{2,1,0:T(8,128)}, u32[]{:S(2)}) copy-start(f32[2,192,160]{2,1,0:T(8,128)} %get-tuple-element.9) | copy-start | bytes 737284
  65.0 14.5 %all-to-all-start.2 = ((bf16[16,16,896]{2,1,0:T(8,128)(2,1)}), bf16[16,16,896]{2,1,0:T(8,128)(2,1)S(1)}, u32[]{:S(2)}, u32[]{:S(2)}) async-start(bf16[16,16,896]{2,1,0:T(8,128)(2,1)} %get-tuple-element.11), calls=%async_computation.2 | async-start | bytes 917504 | tf_op jit(solution)/shard_map/all_to_all | solution.py:339
  70.8 14.5 %collective-permute-start.3 = (f32[2,192,160]{2,1,0:T(8,128)}, f32[2,192,160]{2,1,0:T(8,128)S(1)}, u32[]{:S(2)}, u32[]{:S(2)}) collective-permute-start(f32[2,192,160]{2,1,0:T(8,128)} %get-tuple-element.10), channel_id=1, source_target_pairs={{0,16},{16,0},{1,17},{17,1},{2,18},{18,2},{3,19},{19,3},{4,20},{20... | collective-permute-start | bytes 737288 | tf_op jit(solution)/shard_map/ppermute | solution.py:395
  80.3 16.7 %all-to-all-start.3 = ((f32[16,1,896]{2,1,0:T(1,128)}), f32[16,1,896]{2,1,0:T(1,128)S(1)}, u32[]{:S(2)}, u32[]{:S(2)}) async-start(f32[16,1,896]{2,1,0:T(1,128)} %shard_map.92), calls=%async_computation.3 | async-start | bytes 114688 | tf_op jit(solution)/shard_map/all_to_all | solution.py:339
  85.3 21.4 %collective-permute-start.4 = (f32[2,192,160]{2,1,0:T(8,128)S(1)}, f32[2,192,160]{2,1,0:T(8,128)S(1)}, u32[]{:S(2)}, u32[]{:S(2)}) collective-permute-start(f32[2,192,160]{2,1,0:T(8,128)S(1)} %get-tuple-element.12), channel_id=1, source_target_pairs={{0,1},{1,0},{2,3},{3,2},{4,5},{5,4},{6,7},{7,6},{8,9},{9,8},{10,11... | collective-permute-start | bytes 737288 | tf_op jit(solution)/shard_map/ppermute | solution.py:399
  97.7 17.7 %all-to-all-start.4 = ((f32[32,2,896]{2,1,0:T(2,128)}), f32[32,2,896]{2,1,0:T(2,128)S(1)}, u32[]{:S(2)}, u32[]{:S(2)}) async-start(f32[32,2,896]{2,1,0:T(2,128)} %shard_map.93), calls=%async_computation.4 | async-start | bytes 458752 | tf_op jit(solution)/shard_map/all_to_all | solution.py:339
